TPU v7x, 512 devices: a whole 4x8x8 slice. The times are simulated.
512 devices in a mesh: dp: 8 (over x, core), mp: 64 (over z, y).
Axes of the slice: x: 4, y: 8, z: 8, core: 2. Of those that a mesh axis runs over, the one named last changes fastest.
Arguments:
- grad_parts: bfloat16 [8, 64, 4, 512, 512], P('dp', 'mp'), may hold values from -0.09375 to 0.09375
- factors: float32 [64, 8, 512, 512], P('mp', 'dp'), may hold values from -1 to 8, as said below
- root_prev: bfloat16 [64, 8, 512, 512], P(None, 'dp', 'mp'), may hold values from -1 to 2, as said below
- plan: int32 [8, 64], P('dp'), may hold values from 0 to 64, as said below
Outputs:
- new_factors: float32 [64, 8, 512, 512], P('mp', 'dp')
- new_roots: bfloat16 [64, 8, 512, 512], P(None, 'dp', 'mp')
Inputs may be any that keep to these rules, and one draw needn't show every extreme that they name: In each row of plan no worker is named more than 3 times and one is named exactly 3 times; at least 32 entries of a row are below 64. `factors`: each factor is symmetric. `root_prev`: each root is symmetric.
All inputs are finite; a program needn't handle non-finite values.
Results may differ from a plain program's by a relative error of at most 0.0055.
Values may be sent and summed in bfloat16 or wider, within the bound.
No kernel may reach another device: no remote copies, remote signals or barrier semaphores. Data moves between devices by JAX's collectives and lax.ppermute only.
A program may use at most 64 MiB of HBM per device.

v0:
```python
import jax
import jax.numpy as jnp
from jax import lax
from jax.sharding import PartitionSpec as P

keep_rate = 0.8


def in_blocks(value, dim, length):
    before, after = (value.shape[:dim], value.shape[dim + 1 :])
    return jnp.moveaxis(value.reshape(*before, length, -1, *after), dim, 0)


def sum_at_owner(value, axis, dim):
    length = lax.axis_size(axis)
    pieces = lax.all_to_all(in_blocks(value, dim, length), axis, 0, 0, tiled=True)
    return jnp.sum(pieces.astype(jnp.float32), axis=0)


def swapped(value, axis, bit):
    return lax.ppermute(value, axis, [(i, i ^ 1 << bit) for i in range(lax.axis_size(axis))])


def newton(initial, factor):
    identity = jnp.eye(factor.shape[-1], dtype=jnp.float32)
    square = jnp.einsum("sij,sjk->sik", initial, initial, preferred_element_type=jnp.float32)
    fourth = jnp.einsum("sij,sjk->sik", square, square, precision=lax.Precision.HIGHEST)
    coupled = jnp.einsum("sij,sjk->sik", fourth, factor, precision=lax.Precision.HIGHEST)
    update = (5.0 * identity - coupled) * 0.25
    return jnp.einsum(
        "sij,sjk->sik", initial.astype(jnp.float32), update, precision=lax.Precision.HIGHEST
    )


def to_pieces(matrix):
    return lax.all_to_all(matrix, "mp", split_axis=0, concat_axis=0, tiled=True)


def local(grad_parts, factors, root_prev, plan):
    workers = lax.axis_size("mp")
    block_size = factors.shape[-1]
    piece_len = block_size * block_size // workers
    partial_grads = grad_parts.astype(jnp.float32).reshape(
        2 * grad_parts.shape[2], block_size // 2, block_size
    )
    my_half = sum_at_owner(partial_grads.astype(jnp.bfloat16), "dp", 0)[0]
    partner_half = swapped(my_half.astype(jnp.bfloat16), "dp", 0).astype(my_half.dtype)
    my_side = lax.axis_index("dp") % 2
    upper_rows = jnp.where(my_side == 0, my_half, partner_half)
    lower_rows = jnp.where(my_side == 0, partner_half, my_half)
    full_block = jnp.concatenate([upper_rows, lower_rows], axis=0)
    leading = jnp.where(my_side == 0, full_block, full_block.T)
    gram_new = jnp.dot(leading, leading.T, precision=lax.Precision.HIGHEST)
    fresh_factor = keep_rate * factors[0, 0] + (1.0 - keep_rate) * gram_new
    plan_row = plan[0]
    refresh = plan_row < workers
    old_pieces = root_prev.reshape(workers, piece_len)
    gathered = lax.all_to_all(old_pieces, "mp", split_axis=0, concat_axis=0, tiled=True)
    initial = gathered.reshape(1, block_size, block_size)
    own_entry = lax.dynamic_index_in_dim(plan_row, lax.axis_index("mp"), 0, keepdims=False)

    def refine_own():
        return newton(initial, fresh_factor[None])[0].astype(jnp.bfloat16)

    def keep_own():
        return initial[0]

    refined = lax.cond(own_entry < workers, refine_own, keep_own)
    fresh_roots = to_pieces(refined.reshape(workers, piece_len))
    new_roots = jnp.where(refresh[:, None], fresh_roots, old_pieces).reshape(root_prev.shape)
    return (fresh_factor[None, None], new_roots)


def solution(mesh):
    return jax.shard_map(
        local,
        mesh=mesh,
        in_specs=(
            P("dp", "mp", None, None, None),
            P("mp", "dp", None, None),
            P(None, "dp", "mp", None),
            P("dp", None),
        ),
        out_specs=(P("mp", "dp", None, None), P(None, "dp", "mp", None)),
        check_vma=False,
    )
```

profile of v0, /device:TPU:8, one launch (start us, length us, event | category | flops | bytes accessed | tf_op | source)
XLA Modules:
  0.0 120.5 jit_solution(11253967783212388652)
XLA Ops:
  0.6 4.3 %all-to-all-start = ((bf16[8,1,256,512]{3,2,1,0:T(8,128)(2,1)}), bf16[8,1,256,512]{3,2,1,0:T(8,128)(2,1)S(1)}, u32[]{:S(2)}, u32[]{:S(2)}) async-start(bf16[8,1,256,512]{3,2,1,0:T(8,128)(2,1)} %bitcast.33), calls=%async_computation | async-start | bytes 4194304 | tf_op jit(solution)/shard_map/all_to_all | solution.py:16
  4.9 3.4 %all_to_all.26 = bf16[64,1,4096]{2,1,0:T(2,128)(2,1)S(1)} reshape(bf16[64,1,8,512]{3,2,1,0:T(8,128)(2,1)} %param.8) | data formatting | bytes 1048576 | tf_op jit(solution)/shard_map/all_to_all | solution.py:58
  8.3 0.6 broadcast.31
  8.9 4.6 %reduce.4 = bf16[64,4096]{1,0:T(8,128)(2,1)} reduce(bf16[64,1,4096]{2,1,0:T(2,128)(2,1)S(1)} %all_to_all.26, bf16[]{:T(256)} %broadcast.31), dimensions={1}, to_apply=%all_to_all.26.reduce_sub_computation | reduce | bytes 1048578 | tf_op jit(solution)/shard_map/all_to_all | solution.py:58
  13.6 2.2 %reshape.84 = bf16[64,2,2048]{2,1,0:T(2,128)(2,1)} reshape(bf16[64,4096]{1,0:T(8,128)(2,1)} %reduce.4) | data formatting | bytes 1048576
  15.8 16.4 %all-to-all-done = bf16[8,1,256,512]{3,2,1,0:T(8,128)(2,1)S(1)} async-done(((bf16[8,1,256,512]{3,2,1,0:T(8,128)(2,1)}), bf16[8,1,256,512]{3,2,1,0:T(8,128)(2,1)S(1)}, u32[]{:S(2)}, u32[]{:S(2)}) %all-to-all-start) | async-done | bytes 2097184 | tf_op jit(solution)/shard_map/all_to_all | solution.py:16
  32.1 16.6 %all-to-all-start.1 = ((bf16[64,2,2048]{2,1,0:T(2,128)(2,1)}), bf16[64,2,2048]{2,1,0:T(2,128)(2,1)S(1)}, u32[]{:S(2)}, u32[]{:S(2)}) async-start(bf16[64,2,2048]{2,1,0:T(2,128)(2,1)} %reshape.84), calls=%async_computation.1 | async-start | bytes 1048576 | tf_op jit(solution)/shard_map/all_to_all | solution.py:58
  49.1 1.9 %collective-permute-start = (bf16[256,512]{1,0:T(8,128)(2,1)S(1)}, bf16[256,512]{1,0:T(8,128)(2,1)S(1)}, u32[]{:S(2)}, u32[]{:S(2)}) collective-permute-start(bf16[256,512]{1,0:T(8,128)(2,1)S(1)} %convert_element_type.37), channel_id=1, source_target_pairs={{0,64},{64,0},{128,192},{192,128},{256,320},{320,256},{384,448},{4... | collective-permute-start | bytes 786440 | tf_op jit(solution)/shard_map/ppermute | solution.py:21
  51.0 0.6 fusion.4
  52.3 15.7 %all-to-all-done.1 = bf16[64,2,2048]{2,1,0:T(2,128)(2,1)S(1)} async-done(((bf16[64,2,2048]{2,1,0:T(2,128)(2,1)}), bf16[64,2,2048]{2,1,0:T(2,128)(2,1)S(1)}, u32[]{:S(2)}, u32[]{:S(2)}) %all-to-all-start.1) | async-done | bytes 524320 | tf_op jit(solution)/shard_map/all_to_all | solution.py:58
  68.6 1.0 pad_maximum_fusion
  69.7 1.6 %copy.22 = f32[512,512]{0,1:T(8,128)S(1)} copy(f32[512,512]{1,0:T(8,128)} %pad_maximum_fusion) | data formatting | bytes 2097152 | tf_op jit(solution)/shard_map/concatenate | solution.py:51
  71.2 4.1 %fusion.2 = f32[512,512]{1,0:T(8,128)} fusion(f32[512,512]{0,1:T(8,128)S(1)} %copy.22, f32[1,1,512,512]{3,2,1,0:T(8,128)} %param.7, pred[]{:T(512)S(6)} %eq.10, f32[256,512]{1,0:T(8,128)S(1)} %get-tuple-element.22, f32[256,512]{1,0:T(8,128)S(1)} %get-tuple-element.21), kind=kOutput, calls=%fused_computation.7 | convolution fusion | flops 1611923456 | bytes 4194305 | tf_op jit(solution)/shard_map/dot_general | solution.py:53
  75.4 10.8 %conditional.1 = (bf16[512,512]{0,1:T(8,128)(2,1)S(1)}) conditional(s32[]{:T(128)} %bitcast.7, (bf16[64,1,4096]{2,1,0:T(2,128)(2,1)S(1)}) %tuple.19, (bf16[64,1,4096]{2,1,0:T(2,128)(2,1)S(1)}, f32[512,512]{1,0:T(8,128)}) %tuple.14), branch_computations={%region_1.2_spmd, %region_2.3_spmd} | conditional | flops 5101584384 | bytes 11010058 | solution.py:68
  75.4 3.1 %reduce.2 = bf16[64,4096]{1,0:T(8,128)(2,1)S(1)} reduce(bf16[64,1,4096]{2,1,0:T(2,128)(2,1)S(1)} %get-tuple-element.16, bf16[]{:T(256)} %constant.50), dimensions={1}, to_apply=%get-tuple-element.16.reduce_sub_computation | reduce | bytes 1048578 | tf_op jit(solution)/shard_map
  79.2 1.8 %fusion.6 = f32[512,512]{1,0:T(8,128)S(1)} fusion(f32[512,512]{1,0:T(8,128)S(1)} %fusion.5), kind=kOutput, calls=%fused_computation.18 | convolution fusion | flops 1610612736 | bytes 2097152 | tf_op jit(solution)/shard_map/cond/branch_1_fun/sij,sjk->sik/dot_general | solution.py:27
  81.1 3.1 %fusion = f32[512,512]{1,0:T(8,128)S(1)} fusion(f32[512,512]{1,0:T(8,128)S(1)} %fusion.6, f32[512,512]{1,0:T(8,128)} %get-tuple-element.11), kind=kOutput, calls=%fused_computation.1 | convolution fusion | flops 1611661312 | bytes 3145728 | tf_op jit(solution)/shard_map/cond/branch_1_fun/sij,sjk->sik/dot_general | solution.py:28
  84.1 1.9 %fusion.1 = bf16[512,512]{0,1:T(8,128)(2,1)S(1)} fusion(f32[512,512]{1,0:T(8,128)S(1)} %fusion, bf16[512,512]{1,0:T(8,128)(2,1)S(1)} %reshape.77), kind=kOutput, calls=%fused_computation.3 | convolution fusion | flops 1610874880 | bytes 2097152 | tf_op jit(solution)/shard_map/cond/branch_1_fun/sij,sjk->sik/dot_general | solution.py:30
  86.8 3.8 %reduce.5 = bf16[64,4096]{1,0:T(8,128)(2,1)S(1)} reduce(bf16[64,1,4096]{2,1,0:T(2,128)(2,1)S(1)} %all_to_all.27, bf16[]{:T(256)} %broadcast.31), dimensions={1}, to_apply=%all_to_all.27.reduce_sub_computation | reduce | bytes 1048578 | tf_op jit(solution)/shard_map/all_to_all | solution.py:36
  90.6 1.2 reshape.86
  91.8 5.2 %all-to-all-start.2 = ((bf16[64,2,2048]{2,1,0:T(2,128)(2,1)}), bf16[64,2,2048]{2,1,0:T(2,128)(2,1)S(1)}, u32[]{:S(2)}, u32[]{:S(2)}) async-start(bf16[64,2,2048]{2,1,0:T(2,128)(2,1)} %reshape.86), calls=%async_computation.2 | async-start | bytes 1048576 | tf_op jit(solution)/shard_map/all_to_all | solution.py:36
  97.0 18.6 %all-to-all-done.2 = bf16[64,2,2048]{2,1,0:T(2,128)(2,1)S(1)} async-done(((bf16[64,2,2048]{2,1,0:T(2,128)(2,1)}), bf16[64,2,2048]{2,1,0:T(2,128)(2,1)S(1)}, u32[]{:S(2)}, u32[]{:S(2)}) %all-to-all-start.2) | async-done | bytes 524320 | tf_op jit(solution)/shard_map/all_to_all | solution.py:36
  116.2 3.1 %reduce.3 = bf16[64,4096]{1,0:T(8,128)(2,1)S(1)} reduce(bf16[64,1,4096]{2,1,0:T(2,128)(2,1)S(1)} %reshape.87, bf16[]{:T(256)} %constant.51), dimensions={1}, to_apply=%all_to_all.24.reduce_sub_computation | reduce | bytes 1048578 | tf_op jit(solution)/shard_map/all_to_all | solution.py:36
  119.5 1.0 bitcast_select_fusion.2
  (16 shorter events, 2.9 us)
Async XLA Ops:
  0.6 31.5 %all-to-all-start = ((bf16[8,1,256,512]{3,2,1,0:T(8,128)(2,1)}), bf16[8,1,256,512]{3,2,1,0:T(8,128)(2,1)S(1)}, u32[]{:S(2)}, u32[]{:S(2)}) async-start(bf16[8,1,256,512]{3,2,1,0:T(8,128)(2,1)} %bitcast.33), calls=%async_computation | async-start | bytes 4194304 | tf_op jit(solution)/shard_map/all_to_all | solution.py:16
  15.8 35.2 %copy-start.1 = (s32[1,64]{1,0:T(1,128)S(1)}, s32[1,64]{1,0:T(1,128)}, u32[]{:S(2)}) copy-start(s32[1,64]{1,0:T(1,128)} %param.9) | copy-start | bytes 772
  32.1 35.8 %all-to-all-start.1 = ((bf16[64,2,2048]{2,1,0:T(2,128)(2,1)}), bf16[64,2,2048]{2,1,0:T(2,128)(2,1)S(1)}, u32[]{:S(2)}, u32[]{:S(2)}) async-start(bf16[64,2,2048]{2,1,0:T(2,128)(2,1)} %reshape.84), calls=%async_computation.1 | async-start | bytes 1048576 | tf_op jit(solution)/shard_map/all_to_all | solution.py:58
  49.1 19.4 %collective-permute-start = (bf16[256,512]{1,0:T(8,128)(2,1)S(1)}, bf16[256,512]{1,0:T(8,128)(2,1)S(1)}, u32[]{:S(2)}, u32[]{:S(2)}) collective-permute-start(bf16[256,512]{1,0:T(8,128)(2,1)S(1)} %convert_element_type.37), channel_id=1, source_target_pairs={{0,64},{64,0},{128,192},{192,128},{256,320},{320,256},{384,448},{4... | collective-permute-start | bytes 786440 | tf_op jit(solution)/shard_map/ppermute | solution.py:21
  91.8 23.9 %all-to-all-start.2 = ((bf16[64,2,2048]{2,1,0:T(2,128)(2,1)}), bf16[64,2,2048]{2,1,0:T(2,128)(2,1)S(1)}, u32[]{:S(2)}, u32[]{:S(2)}) async-start(bf16[64,2,2048]{2,1,0:T(2,128)(2,1)} %reshape.86), calls=%async_computation.2 | async-start | bytes 1048576 | tf_op jit(solution)/shard_map/all_to_all | solution.py:36
  97.0 22.5 %copy-start = (bf16[64,1,8,512]{3,2,1,0:T(8,128)(2,1)S(1)}, bf16[64,1,8,512]{3,2,1,0:T(8,128)(2,1)}, u32[]{:S(2)}) copy-start(bf16[64,1,8,512]{3,2,1,0:T(8,128)(2,1)} %param.8) | copy-start | bytes 1572868
where the time goes:
time: 121 us; the launch traced here: 120 us
  waiting for transfers between devices  50.7 us (42%)
  starting transfers between devices  28 us (23%)
  other arithmetic  17.8 us (15%)
  matrix products  11.3 us (9%)
  local copies, waits for them, and re-layouts  10.9 us (9%)
  between operations  1.46 us (1%)
    all_to_all x1, waiting for transfers between devices, to_pieces(): return lax.all_to_all(matrix, 'mp', split_axis=0, concat_axis=0, tiled=True)  18.6 us
    all_to_all x1, starting transfers between devices, local(): lax.all_to_all(old_pieces, 'mp', split_axis=0, concat_axis=0, tiled=True)  16.6 us
    all_to_all x1, waiting for transfers between devices, sum_at_owner(): lax.all_to_all(in_blocks(value, dim, length), axis, 0, 0, tiled=True)  16.4 us
    all_to_all x1, waiting for transfers between devices, local(): lax.all_to_all(old_pieces, 'mp', split_axis=0, concat_axis=0, tiled=True)  15.7 us
    all_to_all x2, other arithmetic, to_pieces(): return lax.all_to_all(matrix, 'mp', split_axis=0, concat_axis=0, tiled=True)  6.98 us
    all_to_all x1, starting transfers between devices, to_pieces(): return lax.all_to_all(matrix, 'mp', split_axis=0, concat_axis=0, tiled=True)  5.21 us
    all_to_all x1, other arithmetic, local(): lax.all_to_all(old_pieces, 'mp', split_axis=0, concat_axis=0, tiled=True)  4.63 us
    unnamed x9, local copies, waits for them, and re-layouts  4.62 us
  transfers between devices with their start and end apart: 4, of which 3 were waited for; matrix products, arithmetic and copies ran while one was open for 7% of the time, Pallas kernels for 0%

commit v1 on v0

--- a/solution.py
+++ b/solution.py
@@ -39,7 +39,7 @@
 def local(grad_parts, factors, root_prev, plan):
     workers = lax.axis_size("mp")
     block_size = factors.shape[-1]
-    piece_len = block_size * block_size // workers
+    rows = block_size // workers
     partial_grads = grad_parts.astype(jnp.float32).reshape(
         2 * grad_parts.shape[2], block_size // 2, block_size
     )
@@ -54,7 +54,7 @@
     fresh_factor = keep_rate * factors[0, 0] + (1.0 - keep_rate) * gram_new
     plan_row = plan[0]
     refresh = plan_row < workers
-    old_pieces = root_prev.reshape(workers, piece_len)
+    old_pieces = root_prev.reshape(workers, rows, block_size)
     gathered = lax.all_to_all(old_pieces, "mp", split_axis=0, concat_axis=0, tiled=True)
     initial = gathered.reshape(1, block_size, block_size)
     own_entry = lax.dynamic_index_in_dim(plan_row, lax.axis_index("mp"), 0, keepdims=False)
@@ -66,8 +66,8 @@
         return initial[0]
 
     refined = lax.cond(own_entry < workers, refine_own, keep_own)
-    fresh_roots = to_pieces(refined.reshape(workers, piece_len))
-    new_roots = jnp.where(refresh[:, None], fresh_roots, old_pieces).reshape(root_prev.shape)
+    fresh_roots = to_pieces(refined.reshape(workers, rows, block_size))
+    new_roots = jnp.where(refresh[:, None, None], fresh_roots, old_pieces).reshape(root_prev.shape)
     return (fresh_factor[None, None], new_roots)
 
 

time: 121 us -> 103 us (0.85)
  blocking collectives: 0 us -> 31.8 us
  waiting for transfers between devices: 50.7 us -> 27.2 us
  other arithmetic: 17.8 us -> 4.07 us
  local copies, waits for them, and re-layouts: 10.9 us -> 2.56 us
  starting transfers between devices: 28 us -> 23.8 us
    all_to_all x0 -> x1, blocking collectives: none -> 31.8 us  [sum_at_owner(): lax.all_to_all(in_blocks(value, dim, length), axis, 0, 0, tiled=True)]
    all_to_all x1 -> x0, waiting for transfers between devices: 16.4 us -> none  [sum_at_owner(): lax.all_to_all(in_blocks(value, dim, length), axis, 0, 0, tiled=True)]
    all_to_all x3 -> x0, other arithmetic: 11.6 us -> none  [the longest x2 6.98 us: to_pieces(): return lax.all_to_all(matrix, 'mp', split_axis=0, concat_axis=0, tiled=True)]
    all_to_all x1, waiting for transfers between devices: 15.7 us -> 8.51 us  [local(): lax.all_to_all(old_pieces, 'mp', split_axis=0, concat_axis=0, tiled=True)]
    unnamed x9 -> x2, local copies, waits for them, and re-layouts: 4.62 us -> 0.01 us
    all_to_all x1 -> x0, starting transfers between devices: 4.31 us -> none  [sum_at_owner(): lax.all_to_all(in_blocks(value, dim, length), axis, 0, 0, tiled=True)]
    all_to_all x3 -> x0, local copies, waits for them, and re-layouts: 4.31 us -> none  [the longest x2 3.98 us: local(): lax.all_to_all(old_pieces, 'mp', split_axis=0, concat_axis=0, tiled=True)]
    another operation x1 -> x0, other arithmetic: 3.15 us -> none
  transfers between devices with their start and end apart: 4 -> 3, of which waited for: 3 -> 3; matrix products, arithmetic and copies ran while one was open for 7% -> 8% of each run, Pallas kernels for 0% -> 0%
where the time goes in v1:
time: 103 us; the launch traced here: 102 us
  blocking collectives  31.8 us (31%)
  waiting for transfers between devices  27.2 us (26%)
  starting transfers between devices  23.8 us (23%)
  matrix products  11.3 us (11%)
  other arithmetic  4.07 us (4%)
  local copies, waits for them, and re-layouts  2.56 us (2%)
  between operations  1.37 us (1%)
    all_to_all x1, blocking collectives, sum_at_owner(): lax.all_to_all(in_blocks(value, dim, length), axis, 0, 0, tiled=True)  31.8 us
    all_to_all x1, waiting for transfers between devices, to_pieces(): return lax.all_to_all(matrix, 'mp', split_axis=0, concat_axis=0, tiled=True)  18.5 us
    all_to_all x1, starting transfers between devices, local(): lax.all_to_all(old_pieces, 'mp', split_axis=0, concat_axis=0, tiled=True)  16.7 us
    all_to_all x1, waiting for transfers between devices, local(): lax.all_to_all(old_pieces, 'mp', split_axis=0, concat_axis=0, tiled=True)  8.51 us
    all_to_all x1, starting transfers between devices, to_pieces(): return lax.all_to_all(matrix, 'mp', split_axis=0, concat_axis=0, tiled=True)  5.19 us
    dot_general x1, matrix products, local(): gram_new = jnp.dot(leading, leading.T, precision=lax.Precision.HIGHEST)  4.14 us
    dot_general x1, matrix products, newton(): jnp.einsum('sij,sjk->sik', fourth, factor, precision=lax.Precision.HIGHEST)  3.07 us
  transfers between devices with their start and end apart: 3, of which 3 were waited for; matrix products, arithmetic and copies ran while one was open for 8% of the time, Pallas kernels for 0%

profile of v1, /device:TPU:8, one launch (start us, length us, event | category | flops | bytes accessed | tf_op | source)
XLA Modules:
  0.0 102.2 jit_solution(17336974410992875270)
XLA Ops:
  0.6 31.8 %all_to_all.18 = bf16[8,1,256,512]{3,2,1,0:T(8,128)(2,1)S(1)} all-to-all(bf16[8,1,256,512]{3,2,1,0:T(8,128)(2,1)} %bitcast.32), channel_id=1, replica_groups=mesh['dp'=8,'mp'=64] {'dp'}, dimensions={0} | all-to-all | bytes 4194304 | tf_op jit(solution)/shard_map/all_to_all | solution.py:16
  32.4 0.0 copy-start
  32.5 16.7 %all-to-all-start.1 = ((bf16[64,8,512]{2,1,0:T(8,128)(2,1)}), bf16[64,8,512]{2,1,0:T(8,128)(2,1)S(1)}, u32[]{:S(2)}, u32[]{:S(2)}) async-start(bf16[64,8,512]{2,1,0:T(8,128)(2,1)} %bitcast.10), calls=%async_computation.1 | async-start | bytes 1048576 | tf_op jit(solution)/shard_map/all_to_all | solution.py:58
  49.2 0.3 convert_reduce_fusion
  49.5 1.9 %collective-permute-start = (bf16[256,512]{1,0:T(8,128)(2,1)S(1)}, bf16[256,512]{1,0:T(8,128)(2,1)S(1)}, u32[]{:S(2)}, u32[]{:S(2)}) collective-permute-start(bf16[256,512]{1,0:T(8,128)(2,1)S(1)} %convert_element_type.37), channel_id=1, source_target_pairs={{0,64},{64,0},{128,192},{192,128},{256,320},{320,256},{384,448},{4... | collective-permute-start | bytes 786440 | tf_op jit(solution)/shard_map/ppermute | solution.py:21
  51.5 0.0 copy-done
  51.5 0.6 fusion.7
  52.7 0.2 collective-permute-done
  52.9 0.1 convert_select_fusion.1
  53.1 1.0 %pad_maximum_fusion = f32[512,512]{1,0:T(8,128)} fusion(f32[256,512]{1,0:T(8,128)S(1)} %get-tuple-element.14, f32[256,512]{1,0:T(8,128)S(1)} %get-tuple-element.13), kind=kLoop, calls=%fused_computation.11 | loop fusion | flops 262144 | bytes 2097152 | tf_op jit(solution)/shard_map/concatenate | solution.py:51
  54.1 1.6 %copy.14 = f32[512,512]{0,1:T(8,128)S(1)} copy(f32[512,512]{1,0:T(8,128)} %pad_maximum_fusion) | data formatting | bytes 2097152 | tf_op jit(solution)/shard_map/concatenate | solution.py:51
  55.7 4.1 %fusion.5 = f32[512,512]{1,0:T(8,128)} fusion(f32[512,512]{0,1:T(8,128)S(1)} %copy.14, f32[1,1,512,512]{3,2,1,0:T(8,128)} %param.7, pred[]{:T(512)S(6)} %eq.10, f32[256,512]{1,0:T(8,128)S(1)} %get-tuple-element.14, f32[256,512]{1,0:T(8,128)S(1)} %get-tuple-element.13), kind=kOutput, calls=%fused_computation.10 | convolution fusion | flops 1611923456 | bytes 4194305 | tf_op jit(solution)/shard_map/dot_general | solution.py:53
  59.8 8.5 %all-to-all-done.1 = bf16[64,8,512]{2,1,0:T(8,128)(2,1)S(1)} async-done(((bf16[64,8,512]{2,1,0:T(8,128)(2,1)}), bf16[64,8,512]{2,1,0:T(8,128)(2,1)S(1)}, u32[]{:S(2)}, u32[]{:S(2)}) %all-to-all-start.1) | async-done | bytes 524320 | tf_op jit(solution)/shard_map/all_to_all | solution.py:58
  68.3 7.2 %conditional.1 = (bf16[512,512]{0,1:T(8,128)(2,1)S(1)}) conditional(s32[]{:T(128)} %bitcast.9, bf16[64,8,512]{2,1,0:T(8,128)(2,1)S(1)} %all-to-all-done.1, (bf16[64,8,512]{2,1,0:T(8,128)(2,1)S(1)}, f32[512,512]{1,0:T(8,128)}) %tuple.14), branch_computations={%region_1.2_spmd, %region_2.3_spmd} | conditional | flops 5101584384 | bytes 8912904 | solution.py:68
  68.3 0.4 fusion.3
  68.8 1.8 %fusion.8 = f32[512,512]{1,0:T(8,128)S(1)} fusion(f32[512,512]{1,0:T(8,128)S(1)} %fusion.3), kind=kOutput, calls=%fused_computation.20 | convolution fusion | flops 1610612736 | bytes 2097152 | tf_op jit(solution)/shard_map/cond/branch_1_fun/sij,sjk->sik/dot_general | solution.py:27
  70.6 3.1 %fusion = f32[512,512]{1,0:T(8,128)S(1)} fusion(f32[512,512]{1,0:T(8,128)S(1)} %fusion.8, f32[512,512]{1,0:T(8,128)} %get-tuple-element.10), kind=kOutput, calls=%fused_computation.1 | convolution fusion | flops 1611661312 | bytes 3145728 | tf_op jit(solution)/shard_map/cond/branch_1_fun/sij,sjk->sik/dot_general | solution.py:28
  73.7 1.9 %fusion.1 = bf16[512,512]{0,1:T(8,128)(2,1)S(1)} fusion(f32[512,512]{1,0:T(8,128)S(1)} %fusion, bf16[64,8,512]{2,1,0:T(8,128)(2,1)S(1)} %get-tuple-element.9), kind=kOutput, calls=%fused_computation.3 | convolution fusion | flops 1610874880 | bytes 2097152 | tf_op jit(solution)/shard_map/cond/branch_1_fun/sij,sjk->sik/dot_general | solution.py:30
  75.6 1.0 copy.15
  76.6 5.2 %all-to-all-start.2 = ((bf16[64,8,512]{2,1,0:T(8,128)(2,1)}), bf16[64,8,512]{2,1,0:T(8,128)(2,1)S(1)}, u32[]{:S(2)}, u32[]{:S(2)}) async-start(bf16[64,8,512]{2,1,0:T(8,128)(2,1)} %bitcast.11), calls=%async_computation.2 | async-start | bytes 1048576 | tf_op jit(solution)/shard_map/all_to_all | solution.py:36
  81.8 18.5 %all-to-all-done.2 = bf16[64,8,512]{2,1,0:T(8,128)(2,1)S(1)} async-done(((bf16[64,8,512]{2,1,0:T(8,128)(2,1)}), bf16[64,8,512]{2,1,0:T(8,128)(2,1)S(1)}, u32[]{:S(2)}, u32[]{:S(2)}) %all-to-all-start.2) | async-done | bytes 524320 | tf_op jit(solution)/shard_map/all_to_all | solution.py:36
  100.3 2.0 %select_bitcast_fusion = bf16[64,1,8,512]{3,2,1,0:T(8,128)(2,1)} fusion(bf16[64,8,512]{2,1,0:T(8,128)(2,1)S(1)} %all-to-all-done.2, pred[64]{0:T(512)(128)(4,1)S(1)} %compare_bitcast_fusion, bf16[64,1,8,512]{3,2,1,0:T(8,128)(2,1)} %param.8), kind=kLoop, calls=%fused_computation.15 | loop fusion | flops 262144 | bytes 1572928 | tf_op jit(solution)/shard_map/reshape | solution.py:70
  (2 shorter events, 0.0 us)
Async XLA Ops:
  32.4 19.0 %copy-start = (s32[1,64]{1,0:T(1,128)S(1)}, s32[1,64]{1,0:T(1,128)}, u32[]{:S(2)}) copy-start(s32[1,64]{1,0:T(1,128)} %param.9) | copy-start | bytes 772
  32.5 35.9 %all-to-all-start.1 = ((bf16[64,8,512]{2,1,0:T(8,128)(2,1)}), bf16[64,8,512]{2,1,0:T(8,128)(2,1)S(1)}, u32[]{:S(2)}, u32[]{:S(2)}) async-start(bf16[64,8,512]{2,1,0:T(8,128)(2,1)} %bitcast.10), calls=%async_computation.1 | async-start | bytes 1048576 | tf_op jit(solution)/shard_map/all_to_all | solution.py:58
  49.5 3.4 %collective-permute-start = (bf16[256,512]{1,0:T(8,128)(2,1)S(1)}, bf16[256,512]{1,0:T(8,128)(2,1)S(1)}, u32[]{:S(2)}, u32[]{:S(2)}) collective-permute-start(bf16[256,512]{1,0:T(8,128)(2,1)S(1)} %convert_element_type.37), channel_id=1, source_target_pairs={{0,64},{64,0},{128,192},{192,128},{256,320},{320,256},{384,448},{4... | collective-permute-start | bytes 786440 | tf_op jit(solution)/shard_map/ppermute | solution.py:21
  76.6 23.7 %all-to-all-start.2 = ((bf16[64,8,512]{2,1,0:T(8,128)(2,1)}), bf16[64,8,512]{2,1,0:T(8,128)(2,1)S(1)}, u32[]{:S(2)}, u32[]{:S(2)}) async-start(bf16[64,8,512]{2,1,0:T(8,128)(2,1)} %bitcast.11), calls=%async_computation.2 | async-start | bytes 1048576 | tf_op jit(solution)/shard_map/all_to_all | solution.py:36

commit v2 on v1

v2 whole, which is shorter than its diff:
```python
import jax
import jax.numpy as jnp
from jax import lax
from jax.experimental import pallas as pl
from jax.experimental.pallas import tpu as pltpu
from jax.sharding import PartitionSpec as P

keep_rate = 0.8
VMEM = pl.BlockSpec(memory_space=pltpu.VMEM)
ANY = pl.BlockSpec(memory_space=pl.ANY)
SMEM = pl.BlockSpec(memory_space=pltpu.SMEM)
PARAMS = pltpu.CompilerParams(vmem_limit_bytes=20 * 1024 * 1024)


def dot(a, b):
    return jnp.dot(a, b, preferred_element_type=jnp.float32)


def split(value):
    high = value.astype(jnp.bfloat16)
    return high, (value - high.astype(jnp.float32)).astype(jnp.bfloat16)


def fifth_kernel(root_ref, high_ref, low_ref):
    root = root_ref[...]
    high, low = split(dot(root, root))
    high, low = split(dot(high, high) + (dot(high, low) + dot(low, high)))
    high_ref[...], low_ref[...] = split(dot(root, high) + dot(root, low))


def prepare_kernel(x_ref, blocks_ref, plus_ref, minus_ref, sems):
    ring, size, _ = blocks_ref.shape
    half = size // 2
    x = x_ref[0]
    wanted = ((2, 0, plus_ref, 0), (1, half, plus_ref, 1), (2, half, minus_ref, 0), (3, 0, minus_ref, 1))
    copies = []
    for at, (step, row, target, slot) in enumerate(wanted):
        source = blocks_ref.at[lax.rem(x + step, ring), pl.ds(row, half)]
        copies.append(pltpu.make_async_copy(source, target.at[slot], sems.at[at]))
    for copy in copies:
        copy.start()
    for copy in copies:
        copy.wait()


def add(*values):
    return sum(value.astype(jnp.float32) for value in values).astype(jnp.bfloat16)


def relay_kernel(x_ref, right_ref, left_ref, from_left_ref, from_right_ref, upper_ref, lower_ref):
    upper_ref[...] = add(right_ref[0], from_left_ref[...])
    lower_ref[...] = add(left_ref[0], from_right_ref[...])


def finish_kernel(x_ref, own_ref, from_left_ref, from_right_ref, upper_ref, lower_ref, mine_ref):
    half = upper_ref.shape[0]
    mine_ref[:half] = add(own_ref[0, :half], from_right_ref[...], upper_ref[...])
    mine_ref[half:] = add(own_ref[0, half:], from_left_ref[...], lower_ref[...])


def refresh_kernel(side_ref, mine_ref, other_ref, factor_ref, root_ref, high_ref, low_ref, fresh_ref, refined_ref):
    summed = add(mine_ref[...], other_ref[...])

    def update(gram):
        fresh_ref[...] = keep_rate * factor_ref[...] + (1.0 - keep_rate) * gram

    @pl.when(side_ref[0] == 0)
    def _():
        update(lax.dot_general(summed, summed, (((1,), (1,)), ((), ())), preferred_element_type=jnp.float32))

    @pl.when(side_ref[0] != 0)
    def _():
        update(lax.dot_general(summed, summed, (((0,), (0,)), ((), ())), preferred_element_type=jnp.float32))

    high, low = split(fresh_ref[...])
    coupled = dot(high_ref[...], high) + (dot(high_ref[...], low) + dot(low_ref[...], high))
    refined_ref[...] = (1.25 * root_ref[...].astype(jnp.float32) - 0.25 * coupled).astype(jnp.bfloat16)


def cost(flops, moved):
    return pl.CostEstimate(flops=flops, bytes_accessed=moved, transcendentals=0)


def local(grad_parts, factors, root_prev, plan):
    workers = lax.axis_size("mp")
    replicas = lax.axis_size("dp")
    size = factors.shape[-1]
    half = size // 2
    blocks = grad_parts[0, 0]
    ring = blocks.shape[0]
    dp = lax.axis_index("dp")
    x, side = dp // 2, dp % 2

    def shifted(value, step):
        return lax.ppermute(value, "dp", [(i, (i // 2 + step) % ring * 2 + i % 2) for i in range(replicas)])

    pair = jax.ShapeDtypeStruct((2, half, size), jnp.bfloat16)
    part = jax.ShapeDtypeStruct((half, size), jnp.bfloat16)
    matrix = jax.ShapeDtypeStruct((size, size), jnp.bfloat16)
    place = x.reshape(1)
    plus, minus = pl.pallas_call(
        prepare_kernel,
        out_shape=(pair, pair),
        in_specs=[SMEM, ANY],
        out_specs=(ANY, ANY),
        scratch_shapes=[pltpu.SemaphoreType.DMA((4,))],
        compiler_params=pltpu.CompilerParams(vmem_limit_bytes=60 * 1024 * 1024),
        cost_estimate=cost(0, 1),
    )(place, blocks)
    from_left = shifted(plus, 1)
    from_right = shifted(minus, -1)
    old_pieces = root_prev.reshape(workers, size // workers, size)
    initial = lax.all_to_all(old_pieces, "mp", split_axis=0, concat_axis=0, tiled=True).reshape(size, size)

    def piece(slot):
        return pl.BlockSpec((None, half, size), lambda i, place: (slot, 0, 0))

    def own(step, row, rows):
        return pl.BlockSpec((1, rows, size), lambda i, place: ((place[0] + step) % ring, row, 0))

    whole = pl.BlockSpec((half, size), lambda i, place: (0, 0))
    upper, lower = pl.pallas_call(
        relay_kernel,
        out_shape=(part, part),
        grid_spec=pltpu.PrefetchScalarGridSpec(
            num_scalar_prefetch=1,
            grid=(1,),
            in_specs=[own(1, 0, half), own(3, 1, half), piece(0), piece(0)],
            out_specs=(whole, whole),
        ),
        compiler_params=PARAMS,
        cost_estimate=cost(0, 1),
    )(place, blocks, blocks, from_left, from_right)
    upper, lower = shifted(upper, 1), shifted(lower, -1)
    mine = pl.pallas_call(
        finish_kernel,
        out_shape=matrix,
        grid_spec=pltpu.PrefetchScalarGridSpec(
            num_scalar_prefetch=1,
            grid=(1,),
            in_specs=[own(0, 0, size), piece(1), piece(1), whole, whole],
            out_specs=pl.BlockSpec((size, size), lambda i, place: (0, 0)),
        ),
        compiler_params=PARAMS,
        cost_estimate=cost(0, 1),
    )(place, blocks, from_left, from_right, upper, lower)
    other = lax.ppermute(mine, "dp", [(i, i ^ 1) for i in range(replicas)])

    flops = 2 * size**3
    high, low = pl.pallas_call(
        fifth_kernel,
        out_shape=(matrix, matrix),
        in_specs=[VMEM],
        out_specs=(VMEM, VMEM),
        compiler_params=PARAMS,
        cost_estimate=cost(6 * flops, 6 * size**2),
    )(initial)
    fresh, refined = pl.pallas_call(
        refresh_kernel,
        out_shape=(jax.ShapeDtypeStruct((size, size), jnp.float32), matrix),
        in_specs=[SMEM] + [VMEM] * 6,
        out_specs=(VMEM, VMEM),
        compiler_params=PARAMS,
        cost_estimate=cost(4 * flops, 22 * size**2),
    )(side.reshape(1), mine, other, factors[0, 0], initial, high, low)

    pieces = lax.all_to_all(refined.reshape(old_pieces.shape), "mp", split_axis=0, concat_axis=0, tiled=True)
    refresh = plan[0] < workers
    new_roots = jnp.where(refresh[:, None, None], pieces, old_pieces).reshape(root_prev.shape)
    return fresh[None, None], new_roots


def solution(mesh):
    return jax.shard_map(
        local,
        mesh=mesh,
        in_specs=(
            P("dp", "mp", None, None, None),
            P("mp", "dp", None, None),
            P(None, "dp", "mp", None),
            P("dp", None),
        ),
        out_specs=(P("mp", "dp", None, None), P(None, "dp", "mp", None)),
        check_vma=False,
    )
```

time: 103 us -> 114 us (1.11)
  the two profiles are of different devices: /device:TPU:8 before, /device:TPU:14 now
where the time goes in v2:
time: 114 us; the launch traced here: 113 us
  Pallas kernels  41.1 us (36%)
  starting transfers between devices  40.7 us (36%)
  waiting for transfers between devices  29.8 us (26%)
    pallas_call x1, Pallas kernels, local(): pl.pallas_call(prepare_kernel, out_shape=(pair, pair), in_specs=[SMEM, AN...  32.9 us
    all_to_all x1, waiting for transfers between devices, local(): lax.all_to_all(refined.reshape(old_pieces.shape), 'mp', split_axis=0, con...  20 us
    all_to_all x1, starting transfers between devices, local(): lax.all_to_all(old_pieces, 'mp', split_axis=0, concat_axis=0, tiled=True)  16.8 us
    ppermute x4, starting transfers between devices, shifted(): lax.ppermute(value, 'dp', [(i, (i // 2 + step) % ring * 2 + i % 2) for i...  11.7 us
    all_to_all x1, starting transfers between devices, local(): lax.all_to_all(refined.reshape(old_pieces.shape), 'mp', split_axis=0, con...  10.4 us
    ppermute x4, waiting for transfers between devices, shifted(): lax.ppermute(value, 'dp', [(i, (i // 2 + step) % ring * 2 + i % 2) for i...  7.5 us
    pallas_call x1, Pallas kernels, local(): pl.pallas_call(refresh_kernel, out_shape=(jax.ShapeDtypeStruct((size, siz...  3.99 us
    pallas_call x1, Pallas kernels, local(): pl.pallas_call(fifth_kernel, out_shape=(matrix, matrix), in_specs=[VMEM],...  3.07 us
  transfers between devices with their start and end apart: 7, of which 4 were waited for; matrix products, arithmetic and copies ran while one was open for 0% of the time, Pallas kernels for 4%

profile of v2, /device:TPU:14, one launch (start us, length us, event | category | flops | bytes accessed | tf_op | source)
XLA Modules:
  0.0 113.4 jit_solution(14881697179510238940)
XLA Ops:
  0.6 0.0 copy-start
  0.7 32.9 %shard_map.59 = (bf16[2,256,512]{2,1,0:T(8,128)(2,1)}, bf16[2,256,512]{2,1,0:T(8,128)(2,1)}) custom-call(s32[1]{0:T(128)} %bitcast.1.x_ref, bf16[4,512,512]{2,1,0:T(8,128)(2,1)} %bitcast.13), custom_call_target="tpu_custom_call" | custom-call | bytes 1 | tf_op jit(solution)/shard_map/pallas_call | solution.py:101
  33.6 2.4 %collective-permute-start = (bf16[2,256,512]{2,1,0:T(8,128)(2,1)}, bf16[2,256,512]{2,1,0:T(8,128)(2,1)S(1)}, u32[]{:S(2)}, u32[]{:S(2)}) collective-permute-start(bf16[2,256,512]{2,1,0:T(8,128)(2,1)} %get-tuple-element.10), channel_id=1, source_target_pairs={{0,128},{64,192},{128,256},{192,320},{256,384},{320,448},{384,0},{... | collective-permute-start | bytes 1572872 | tf_op jit(solution)/shard_map/ppermute | solution.py:95
  36.0 3.5 %collective-permute-start.1 = (bf16[2,256,512]{2,1,0:T(8,128)(2,1)}, bf16[2,256,512]{2,1,0:T(8,128)(2,1)S(1)}, u32[]{:S(2)}, u32[]{:S(2)}) collective-permute-start(bf16[2,256,512]{2,1,0:T(8,128)(2,1)} %get-tuple-element.11), channel_id=1, source_target_pairs={{0,384},{64,448},{128,0},{192,64},{256,128},{320,192},{384,256},{4... | collective-permute-start | bytes 1572872 | tf_op jit(solution)/shard_map/ppermute | solution.py:95
  39.4 16.8 %all-to-all-start = ((bf16[64,8,512]{2,1,0:T(8,128)(2,1)}), bf16[64,8,512]{2,1,0:T(8,128)(2,1)}, u32[]{:S(2)}, u32[]{:S(2)}) async-start(bf16[64,8,512]{2,1,0:T(8,128)(2,1)} %bitcast.18), calls=%async_computation | async-start | bytes 1048576 | tf_op jit(solution)/shard_map/all_to_all | solution.py:113
  56.2 0.0 collective-permute-done.from_left_ref
  56.2 0.0 collective-permute-done.1.from_right_ref
  56.2 0.0 copy-done
  56.2 0.1 shard_map.60
  56.4 3.6 %collective-permute-start.2 = (bf16[256,512]{1,0:T(8,128)(2,1)S(1)}, bf16[256,512]{1,0:T(8,128)(2,1)S(1)}, u32[]{:S(2)}, u32[]{:S(2)}) collective-permute-start(bf16[256,512]{1,0:T(8,128)(2,1)S(1)} %get-tuple-element.12), channel_id=1, source_target_pairs={{0,128},{64,192},{128,256},{192,320},{256,384},{320,448},{384,0},{... | collective-permute-start | bytes 786440 | tf_op jit(solution)/shard_map/ppermute | solution.py:95
  60.0 2.2 %collective-permute-start.3 = (bf16[256,512]{1,0:T(8,128)(2,1)S(1)}, bf16[256,512]{1,0:T(8,128)(2,1)S(1)}, u32[]{:S(2)}, u32[]{:S(2)}) collective-permute-start(bf16[256,512]{1,0:T(8,128)(2,1)S(1)} %get-tuple-element.13), channel_id=1, source_target_pairs={{0,384},{64,448},{128,0},{192,64},{256,128},{320,192},{384,256},{4... | collective-permute-start | bytes 786440 | tf_op jit(solution)/shard_map/ppermute | solution.py:95
  62.2 3.0 %collective-permute-done.2.upper_ref = bf16[256,512]{1,0:T(8,128)(2,1)S(1)} collective-permute-done((bf16[256,512]{1,0:T(8,128)(2,1)S(1)}, bf16[256,512]{1,0:T(8,128)(2,1)S(1)}, u32[]{:S(2)}, u32[]{:S(2)}) %collective-permute-start.2) | collective-permute-done | bytes 262176 | tf_op jit(solution)/shard_map/ppermute | solution.py:95
  65.2 4.5 %collective-permute-done.3.lower_ref = bf16[256,512]{1,0:T(8,128)(2,1)S(1)} collective-permute-done((bf16[256,512]{1,0:T(8,128)(2,1)S(1)}, bf16[256,512]{1,0:T(8,128)(2,1)S(1)}, u32[]{:S(2)}, u32[]{:S(2)}) %collective-permute-start.3) | collective-permute-done | bytes 262176 | tf_op jit(solution)/shard_map/ppermute | solution.py:95
  69.7 1.0 shard_map.61.mine_ref
  70.7 1.9 %collective-permute-start.4 = (bf16[512,512]{1,0:T(8,128)(2,1)}, bf16[512,512]{1,0:T(8,128)(2,1)S(1)}, u32[]{:S(2)}, u32[]{:S(2)}) collective-permute-start(bf16[512,512]{1,0:T(8,128)(2,1)} %shard_map.61.mine_ref), channel_id=1, source_target_pairs={{0,64},{64,0},{128,192},{192,128},{256,320},{320,256},{384,448},{4... | collective-permute-start | bytes 1572872 | tf_op jit(solution)/shard_map/ppermute | solution.py:147
  72.7 2.4 %all-to-all-done = bf16[64,8,512]{2,1,0:T(8,128)(2,1)} async-done(((bf16[64,8,512]{2,1,0:T(8,128)(2,1)}), bf16[64,8,512]{2,1,0:T(8,128)(2,1)}, u32[]{:S(2)}, u32[]{:S(2)}) %all-to-all-start) | async-done | bytes 524320 | tf_op jit(solution)/shard_map/all_to_all | solution.py:113
  75.0 3.1 %shard_map.62 = (bf16[512,512]{1,0:T(8,128)(2,1)S(1)}, bf16[512,512]{1,0:T(8,128)(2,1)S(1)}) custom-call(bf16[512,512]{1,0:T(8,128)(2,1)} %bitcast.5.root_ref), custom_call_target="tpu_custom_call" | custom-call | flops 1610612736 | bytes 1572864 | tf_op jit(solution)/shard_map/pallas_call | solution.py:150
  78.1 0.0 collective-permute-done.4.other_ref
  78.1 0.0 copy-start.3
  78.1 0.0 copy-start.2
  78.1 4.0 %shard_map.63 = (f32[512,512]{1,0:T(8,128)}, bf16[512,512]{1,0:T(8,128)(2,1)}) custom-call(s32[1]{0:T(128)} %bitcast.side_ref, bf16[512,512]{1,0:T(8,128)(2,1)} %shard_map.61.mine_ref, bf16[512,512]{1,0:T(8,128)(2,1)S(1)} %collective-permute-done.4.other_ref, f32[512,512]{1,0:T(8,128)S(1)} %bitcast.17, bf16[512,512]{1,0:T(8,128)(2,1)} %bitcast.5.root_ref, ...), custom_call_target="tpu_custom_call" | custom-call | flops 1073741824 | bytes 5767168 | tf_op jit(solution)/shard_map/pallas_call | solution.py:158
  82.1 10.4 %all-to-all-start.1 = ((bf16[64,8,512]{2,1,0:T(8,128)(2,1)}), bf16[64,8,512]{2,1,0:T(8,128)(2,1)S(1)}, u32[]{:S(2)}, u32[]{:S(2)}) async-start(bf16[64,8,512]{2,1,0:T(8,128)(2,1)} %bitcast.8), calls=%async_computation.1 | async-start | bytes 1048576 | tf_op jit(solution)/shard_map/all_to_all | solution.py:167
  92.5 20.0 %all-to-all-done.1 = bf16[64,8,512]{2,1,0:T(8,128)(2,1)S(1)} async-done(((bf16[64,8,512]{2,1,0:T(8,128)(2,1)}), bf16[64,8,512]{2,1,0:T(8,128)(2,1)S(1)}, u32[]{:S(2)}, u32[]{:S(2)}) %all-to-all-start.1) | async-done | bytes 524320 | tf_op jit(solution)/shard_map/all_to_all | solution.py:167
  112.5 0.9 select_bitcast_fusion
  (5 shorter events, 0.0 us)
Async XLA Ops:
  0.6 55.6 %copy-start = (bf16[1,1,4,512,512]{4,3,2,1,0:T(8,128)(2,1)S(1)}, bf16[1,1,4,512,512]{4,3,2,1,0:T(8,128)(2,1)}, u32[]{:S(2)}) copy-start(bf16[1,1,4,512,512]{4,3,2,1,0:T(8,128)(2,1)} %param.4) | copy-start | bytes 6291460
  33.6 22.7 %collective-permute-start = (bf16[2,256,512]{2,1,0:T(8,128)(2,1)}, bf16[2,256,512]{2,1,0:T(8,128)(2,1)S(1)}, u32[]{:S(2)}, u32[]{:S(2)}) collective-permute-start(bf16[2,256,512]{2,1,0:T(8,128)(2,1)} %get-tuple-element.10), channel_id=1, source_target_pairs={{0,128},{64,192},{128,256},{192,320},{256,384},{320,448},{384,0},{... | collective-permute-start | bytes 1572872 | tf_op jit(solution)/shard_map/ppermute | solution.py:95
  36.0 20.3 %collective-permute-start.1 = (bf16[2,256,512]{2,1,0:T(8,128)(2,1)}, bf16[2,256,512]{2,1,0:T(8,128)(2,1)S(1)}, u32[]{:S(2)}, u32[]{:S(2)}) collective-permute-start(bf16[2,256,512]{2,1,0:T(8,128)(2,1)} %get-tuple-element.11), channel_id=1, source_target_pairs={{0,384},{64,448},{128,0},{192,64},{256,128},{320,192},{384,256},{4... | collective-permute-start | bytes 1572872 | tf_op jit(solution)/shard_map/ppermute | solution.py:95
  39.4 35.6 %all-to-all-start = ((bf16[64,8,512]{2,1,0:T(8,128)(2,1)}), bf16[64,8,512]{2,1,0:T(8,128)(2,1)}, u32[]{:S(2)}, u32[]{:S(2)}) async-start(bf16[64,8,512]{2,1,0:T(8,128)(2,1)} %bitcast.18), calls=%async_computation | async-start | bytes 1048576 | tf_op jit(solution)/shard_map/all_to_all | solution.py:113
  56.4 8.8 %collective-permute-start.2 = (bf16[256,512]{1,0:T(8,128)(2,1)S(1)}, bf16[256,512]{1,0:T(8,128)(2,1)S(1)}, u32[]{:S(2)}, u32[]{:S(2)}) collective-permute-start(bf16[256,512]{1,0:T(8,128)(2,1)S(1)} %get-tuple-element.12), channel_id=1, source_target_pairs={{0,128},{64,192},{128,256},{192,320},{256,384},{320,448},{384,0},{... | collective-permute-start | bytes 786440 | tf_op jit(solution)/shard_map/ppermute | solution.py:95
  60.0 9.8 %collective-permute-start.3 = (bf16[256,512]{1,0:T(8,128)(2,1)S(1)}, bf16[256,512]{1,0:T(8,128)(2,1)S(1)}, u32[]{:S(2)}, u32[]{:S(2)}) collective-permute-start(bf16[256,512]{1,0:T(8,128)(2,1)S(1)} %get-tuple-element.13), channel_id=1, source_target_pairs={{0,384},{64,448},{128,0},{192,64},{256,128},{320,192},{384,256},{4... | collective-permute-start | bytes 786440 | tf_op jit(solution)/shard_map/ppermute | solution.py:95
  70.7 7.4 %collective-permute-start.4 = (bf16[512,512]{1,0:T(8,128)(2,1)}, bf16[512,512]{1,0:T(8,128)(2,1)S(1)}, u32[]{:S(2)}, u32[]{:S(2)}) collective-permute-start(bf16[512,512]{1,0:T(8,128)(2,1)} %shard_map.61.mine_ref), channel_id=1, source_target_pairs={{0,64},{64,0},{128,192},{192,128},{256,320},{320,256},{384,448},{4... | collective-permute-start | bytes 1572872 | tf_op jit(solution)/shard_map/ppermute | solution.py:147
  75.0 3.1 %copy-start.1 = (f32[1,1,512,512]{3,2,1,0:T(8,128)S(1)}, f32[1,1,512,512]{3,2,1,0:T(8,128)}, u32[]{:S(2)}) copy-start(f32[1,1,512,512]{3,2,1,0:T(8,128)} %param.5) | copy-start | bytes 3145732
  78.1 14.4 %copy-start.3 = (s32[1,64]{1,0:T(1,128)S(1)}, s32[1,64]{1,0:T(1,128)}, u32[]{:S(2)}) copy-start(s32[1,64]{1,0:T(1,128)} %param.7) | copy-start | bytes 772
  78.1 34.3 %copy-start.2 = (bf16[64,1,8,512]{3,2,1,0:T(8,128)(2,1)S(1)}, bf16[64,1,8,512]{3,2,1,0:T(8,128)(2,1)}, u32[]{:S(2)}) copy-start(bf16[64,1,8,512]{3,2,1,0:T(8,128)(2,1)} %param.6) | copy-start | bytes 1572868
  82.1 30.3 %all-to-all-start.1 = ((bf16[64,8,512]{2,1,0:T(8,128)(2,1)}), bf16[64,8,512]{2,1,0:T(8,128)(2,1)S(1)}, u32[]{:S(2)}, u32[]{:S(2)}) async-start(bf16[64,8,512]{2,1,0:T(8,128)(2,1)} %bitcast.8), calls=%async_computation.1 | async-start | bytes 1048576 | tf_op jit(solution)/shard_map/all_to_all | solution.py:167

commit v3 on v2

--- a/solution.py
+++ b/solution.py
@@ -28,19 +28,9 @@
     high_ref[...], low_ref[...] = split(dot(root, high) + dot(root, low))
 
 
-def prepare_kernel(x_ref, blocks_ref, plus_ref, minus_ref, sems):
-    ring, size, _ = blocks_ref.shape
-    half = size // 2
-    x = x_ref[0]
-    wanted = ((2, 0, plus_ref, 0), (1, half, plus_ref, 1), (2, half, minus_ref, 0), (3, 0, minus_ref, 1))
-    copies = []
-    for at, (step, row, target, slot) in enumerate(wanted):
-        source = blocks_ref.at[lax.rem(x + step, ring), pl.ds(row, half)]
-        copies.append(pltpu.make_async_copy(source, target.at[slot], sems.at[at]))
-    for copy in copies:
-        copy.start()
-    for copy in copies:
-        copy.wait()
+def prepare_kernel(x_ref, relay_up_ref, right_ref, relay_low_ref, left_ref, plus_ref, minus_ref):
+    plus_ref[0], plus_ref[1] = relay_up_ref[0], right_ref[0]
+    minus_ref[0], minus_ref[1] = relay_low_ref[0], left_ref[0]
 
 
 def add(*values):
@@ -98,25 +88,30 @@
     part = jax.ShapeDtypeStruct((half, size), jnp.bfloat16)
     matrix = jax.ShapeDtypeStruct((size, size), jnp.bfloat16)
     place = x.reshape(1)
-    plus, minus = pl.pallas_call(
-        prepare_kernel,
-        out_shape=(pair, pair),
-        in_specs=[SMEM, ANY],
-        out_specs=(ANY, ANY),
-        scratch_shapes=[pltpu.SemaphoreType.DMA((4,))],
-        compiler_params=pltpu.CompilerParams(vmem_limit_bytes=60 * 1024 * 1024),
-        cost_estimate=cost(0, 1),
-    )(place, blocks)
-    from_left = shifted(plus, 1)
-    from_right = shifted(minus, -1)
-    old_pieces = root_prev.reshape(workers, size // workers, size)
-    initial = lax.all_to_all(old_pieces, "mp", split_axis=0, concat_axis=0, tiled=True).reshape(size, size)
 
     def piece(slot):
         return pl.BlockSpec((None, half, size), lambda i, place: (slot, 0, 0))
 
     def own(step, row, rows):
         return pl.BlockSpec((1, rows, size), lambda i, place: ((place[0] + step) % ring, row, 0))
+
+    both = pl.BlockSpec((2, half, size), lambda i, place: (0, 0, 0))
+    plus, minus = pl.pallas_call(
+        prepare_kernel,
+        out_shape=(pair, pair),
+        grid_spec=pltpu.PrefetchScalarGridSpec(
+            num_scalar_prefetch=1,
+            grid=(1,),
+            in_specs=[own(2, 0, half), own(1, 1, half), own(2, 1, half), own(3, 0, half)],
+            out_specs=(both, both),
+        ),
+        compiler_params=pltpu.CompilerParams(vmem_limit_bytes=60 * 1024 * 1024),
+        cost_estimate=cost(0, 1),
+    )(place, blocks, blocks, blocks, blocks)
+    from_left = shifted(plus, 1)
+    from_right = shifted(minus, -1)
+    old_pieces = root_prev.reshape(workers, size // workers, size)
+    initial = lax.all_to_all(old_pieces, "mp", split_axis=0, concat_axis=0, tiled=True).reshape(size, size)
 
     whole = pl.BlockSpec((half, size), lambda i, place: (0, 0))
     upper, lower = pl.pallas_call(

time: 114 us -> 83.3 us (0.73)
  Pallas kernels: 41.1 us -> 10.5 us
    pallas_call x1, Pallas kernels: 32.9 us -> 2.34 us  [local(): pl.pallas_call(prepare_kernel, out_shape=(pair, pair), grid_spec=pltpu.Pr...]
  transfers between devices with their start and end apart: 7 -> 7, of which waited for: 4 -> 4; matrix products, arithmetic and copies ran while one was open for 0% -> 0% of each run, Pallas kernels for 4% -> 5%
where the time goes in v3:
time: 83.3 us; the launch traced here: 82.8 us
  starting transfers between devices  40.7 us (49%)
  waiting for transfers between devices  29.8 us (36%)
  Pallas kernels  10.5 us (13%)
  other arithmetic  0.94 us (1%)
    all_to_all x1, waiting for transfers between devices, local(): lax.all_to_all(refined.reshape(old_pieces.shape), 'mp', split_axis=0, con...  20 us
    all_to_all x1, starting transfers between devices, local(): lax.all_to_all(old_pieces, 'mp', split_axis=0, concat_axis=0, tiled=True)  16.8 us
    ppermute x4, starting transfers between devices, shifted(): lax.ppermute(value, 'dp', [(i, (i // 2 + step) % ring * 2 + i % 2) for i...  11.7 us
    all_to_all x1, starting transfers between devices, local(): lax.all_to_all(refined.reshape(old_pieces.shape), 'mp', split_axis=0, con...  10.4 us
    ppermute x4, waiting for transfers between devices, shifted(): lax.ppermute(value, 'dp', [(i, (i // 2 + step) % ring * 2 + i % 2) for i...  7.5 us
    pallas_call x1, Pallas kernels, local(): pl.pallas_call(refresh_kernel, out_shape=(jax.ShapeDtypeStruct((size, siz...  3.98 us
    pallas_call x1, Pallas kernels, local(): pl.pallas_call(fifth_kernel, out_shape=(matrix, matrix), in_specs=[VMEM],...  3.06 us
    all_to_all x1, waiting for transfers between devices, local(): lax.all_to_all(old_pieces, 'mp', split_axis=0, concat_axis=0, tiled=True)  2.36 us
  transfers between devices with their start and end apart: 7, of which 4 were waited for; matrix products, arithmetic and copies ran while one was open for 0% of the time, Pallas kernels for 5%

profile of v3, /device:TPU:14, one launch (start us, length us, event | category | flops | bytes accessed | tf_op | source)
XLA Modules:
  0.0 82.8 jit_solution(9824609657661503504)
XLA Ops:
  0.7 2.3 %shard_map.59 = (bf16[2,256,512]{2,1,0:T(8,128)(2,1)}, bf16[2,256,512]{2,1,0:T(8,128)(2,1)}) custom-call(s32[1]{0:T(128)} %bitcast.1.x_ref, bf16[4,512,512]{2,1,0:T(8,128)(2,1)} %bitcast.13, bf16[4,512,512]{2,1,0:T(8,128)(2,1)} %bitcast.14, bf16[4,512,512]{2,1,0:T(8,128)(2,1)} %bitcast.15, bf16[4,512,512]{2,1,0:T(8,128)(2,1)} %bitcast.16), custom_call_target="tpu_custom_call" | custom-call | bytes 1 | tf_op jit(solution)/shard_map/pallas_call | solution.py:99
  3.0 2.4 %collective-permute-start = (bf16[2,256,512]{2,1,0:T(8,128)(2,1)}, bf16[2,256,512]{2,1,0:T(8,128)(2,1)S(1)}, u32[]{:S(2)}, u32[]{:S(2)}) collective-permute-start(bf16[2,256,512]{2,1,0:T(8,128)(2,1)} %get-tuple-element.10), channel_id=1, source_target_pairs={{0,128},{64,192},{128,256},{192,320},{256,384},{320,448},{384,0},{... | collective-permute-start | bytes 1572872 | tf_op jit(solution)/shard_map/ppermute | solution.py:85
  5.4 3.5 %collective-permute-start.1 = (bf16[2,256,512]{2,1,0:T(8,128)(2,1)}, bf16[2,256,512]{2,1,0:T(8,128)(2,1)S(1)}, u32[]{:S(2)}, u32[]{:S(2)}) collective-permute-start(bf16[2,256,512]{2,1,0:T(8,128)(2,1)} %get-tuple-element.11), channel_id=1, source_target_pairs={{0,384},{64,448},{128,0},{192,64},{256,128},{320,192},{384,256},{4... | collective-permute-start | bytes 1572872 | tf_op jit(solution)/shard_map/ppermute | solution.py:85
  8.8 16.8 %all-to-all-start = ((bf16[64,8,512]{2,1,0:T(8,128)(2,1)}), bf16[64,8,512]{2,1,0:T(8,128)(2,1)}, u32[]{:S(2)}, u32[]{:S(2)}) async-start(bf16[64,8,512]{2,1,0:T(8,128)(2,1)} %bitcast.21), calls=%async_computation | async-start | bytes 1048576 | tf_op jit(solution)/shard_map/all_to_all | solution.py:114
  25.6 0.0 collective-permute-done.from_left_ref
  25.6 0.0 collective-permute-done.1.from_right_ref
  25.7 0.1 shard_map.60
  25.8 3.6 %collective-permute-start.2 = (bf16[256,512]{1,0:T(8,128)(2,1)S(1)}, bf16[256,512]{1,0:T(8,128)(2,1)S(1)}, u32[]{:S(2)}, u32[]{:S(2)}) collective-permute-start(bf16[256,512]{1,0:T(8,128)(2,1)S(1)} %get-tuple-element.12), channel_id=1, source_target_pairs={{0,128},{64,192},{128,256},{192,320},{256,384},{320,448},{384,0},{... | collective-permute-start | bytes 786440 | tf_op jit(solution)/shard_map/ppermute | solution.py:85
  29.4 2.2 %collective-permute-start.3 = (bf16[256,512]{1,0:T(8,128)(2,1)S(1)}, bf16[256,512]{1,0:T(8,128)(2,1)S(1)}, u32[]{:S(2)}, u32[]{:S(2)}) collective-permute-start(bf16[256,512]{1,0:T(8,128)(2,1)S(1)} %get-tuple-element.13), channel_id=1, source_target_pairs={{0,384},{64,448},{128,0},{192,64},{256,128},{320,192},{384,256},{4... | collective-permute-start | bytes 786440 | tf_op jit(solution)/shard_map/ppermute | solution.py:85
  31.7 3.0 %collective-permute-done.2.upper_ref = bf16[256,512]{1,0:T(8,128)(2,1)S(1)} collective-permute-done((bf16[256,512]{1,0:T(8,128)(2,1)S(1)}, bf16[256,512]{1,0:T(8,128)(2,1)S(1)}, u32[]{:S(2)}, u32[]{:S(2)}) %collective-permute-start.2) | collective-permute-done | bytes 262176 | tf_op jit(solution)/shard_map/ppermute | solution.py:85
  34.6 4.5 %collective-permute-done.3.lower_ref = bf16[256,512]{1,0:T(8,128)(2,1)S(1)} collective-permute-done((bf16[256,512]{1,0:T(8,128)(2,1)S(1)}, bf16[256,512]{1,0:T(8,128)(2,1)S(1)}, u32[]{:S(2)}, u32[]{:S(2)}) %collective-permute-start.3) | collective-permute-done | bytes 262176 | tf_op jit(solution)/shard_map/ppermute | solution.py:85
  39.2 1.0 %shard_map.61.mine_ref = bf16[512,512]{1,0:T(8,128)(2,1)} custom-call(s32[1]{0:T(128)} %bitcast.1.x_ref, bf16[4,512,512]{2,1,0:T(8,128)(2,1)S(1)} %bitcast.19, bf16[2,256,512]{2,1,0:T(8,128)(2,1)S(1)} %collective-permute-done.from_left_ref, bf16[2,256,512]{2,1,0:T(8,128)(2,1)S(1)} %collective-permute-done.1.from_right_ref, ...), custom_call_target="tpu_custom_call" | custom-call | bytes 1 | tf_op jit(solution)/shard_map/pallas_call | solution.py:130
  40.1 1.9 %collective-permute-start.4 = (bf16[512,512]{1,0:T(8,128)(2,1)}, bf16[512,512]{1,0:T(8,128)(2,1)S(1)}, u32[]{:S(2)}, u32[]{:S(2)}) collective-permute-start(bf16[512,512]{1,0:T(8,128)(2,1)} %shard_map.61.mine_ref), channel_id=1, source_target_pairs={{0,64},{64,0},{128,192},{192,128},{256,320},{320,256},{384,448},{4... | collective-permute-start | bytes 1572872 | tf_op jit(solution)/shard_map/ppermute | solution.py:142
  42.1 2.4 %all-to-all-done = bf16[64,8,512]{2,1,0:T(8,128)(2,1)} async-done(((bf16[64,8,512]{2,1,0:T(8,128)(2,1)}), bf16[64,8,512]{2,1,0:T(8,128)(2,1)}, u32[]{:S(2)}, u32[]{:S(2)}) %all-to-all-start) | async-done | bytes 524320 | tf_op jit(solution)/shard_map/all_to_all | solution.py:114
  44.4 3.1 %shard_map.62 = (bf16[512,512]{1,0:T(8,128)(2,1)S(1)}, bf16[512,512]{1,0:T(8,128)(2,1)S(1)}) custom-call(bf16[512,512]{1,0:T(8,128)(2,1)} %bitcast.5.root_ref), custom_call_target="tpu_custom_call" | custom-call | flops 1610612736 | bytes 1572864 | tf_op jit(solution)/shard_map/pallas_call | solution.py:145
  47.5 0.0 collective-permute-done.4.other_ref
  47.5 0.0 copy-done.1
  47.5 0.0 copy-start.3
  47.5 0.0 copy-start.2
  47.5 4.0 %shard_map.63 = (f32[512,512]{1,0:T(8,128)}, bf16[512,512]{1,0:T(8,128)(2,1)}) custom-call(s32[1]{0:T(128)} %bitcast.side_ref, bf16[512,512]{1,0:T(8,128)(2,1)} %shard_map.61.mine_ref, bf16[512,512]{1,0:T(8,128)(2,1)S(1)} %collective-permute-done.4.other_ref, f32[512,512]{1,0:T(8,128)S(1)} %bitcast.20, bf16[512,512]{1,0:T(8,128)(2,1)} %bitcast.5.root_ref, ...), custom_call_target="tpu_custom_call" | custom-call | flops 1073741824 | bytes 5767168 | tf_op jit(solution)/shard_map/pallas_call | solution.py:153
  51.5 10.4 %all-to-all-start.1 = ((bf16[64,8,512]{2,1,0:T(8,128)(2,1)}), bf16[64,8,512]{2,1,0:T(8,128)(2,1)S(1)}, u32[]{:S(2)}, u32[]{:S(2)}) async-start(bf16[64,8,512]{2,1,0:T(8,128)(2,1)} %bitcast.8), calls=%async_computation.1 | async-start | bytes 1048576 | tf_op jit(solution)/shard_map/all_to_all | solution.py:162
  61.9 0.0 copy-done.3
  61.9 20.0 %all-to-all-done.1 = bf16[64,8,512]{2,1,0:T(8,128)(2,1)S(1)} async-done(((bf16[64,8,512]{2,1,0:T(8,128)(2,1)}), bf16[64,8,512]{2,1,0:T(8,128)(2,1)S(1)}, u32[]{:S(2)}, u32[]{:S(2)}) %all-to-all-start.1) | async-done | bytes 524320 | tf_op jit(solution)/shard_map/all_to_all | solution.py:162
  81.9 0.9 %select_bitcast_fusion = bf16[64,1,8,512]{3,2,1,0:T(8,128)(2,1)} fusion(bf16[64,8,512]{2,1,0:T(8,128)(2,1)S(1)} %all-to-all-done.1, pred[64]{0:T(512)(128)(4,1)S(1)} %compare_bitcast_fusion, bf16[64,1,8,512]{3,2,1,0:T(8,128)(2,1)S(1)} %copy-done.2), kind=kLoop, calls=%fused_computation | loop fusion | flops 262144 | bytes 1572928 | tf_op jit(solution)/shard_map/reshape | solution.py:164
  (5 shorter events, 0.0 us)
Async XLA Ops:
  0.6 25.0 %copy-start = (bf16[1,1,4,512,512]{4,3,2,1,0:T(8,128)(2,1)S(1)}, bf16[1,1,4,512,512]{4,3,2,1,0:T(8,128)(2,1)}, u32[]{:S(2)}) copy-start(bf16[1,1,4,512,512]{4,3,2,1,0:T(8,128)(2,1)} %param.4) | copy-start | bytes 6291460
  3.0 22.6 %collective-permute-start = (bf16[2,256,512]{2,1,0:T(8,128)(2,1)}, bf16[2,256,512]{2,1,0:T(8,128)(2,1)S(1)}, u32[]{:S(2)}, u32[]{:S(2)}) collective-permute-start(bf16[2,256,512]{2,1,0:T(8,128)(2,1)} %get-tuple-element.10), channel_id=1, source_target_pairs={{0,128},{64,192},{128,256},{192,320},{256,384},{320,448},{384,0},{... | collective-permute-start | bytes 1572872 | tf_op jit(solution)/shard_map/ppermute | solution.py:85
  5.4 20.3 %collective-permute-start.1 = (bf16[2,256,512]{2,1,0:T(8,128)(2,1)}, bf16[2,256,512]{2,1,0:T(8,128)(2,1)S(1)}, u32[]{:S(2)}, u32[]{:S(2)}) collective-permute-start(bf16[2,256,512]{2,1,0:T(8,128)(2,1)} %get-tuple-element.11), channel_id=1, source_target_pairs={{0,384},{64,448},{128,0},{192,64},{256,128},{320,192},{384,256},{4... | collective-permute-start | bytes 1572872 | tf_op jit(solution)/shard_map/ppermute | solution.py:85
  8.8 35.6 %all-to-all-start = ((bf16[64,8,512]{2,1,0:T(8,128)(2,1)}), bf16[64,8,512]{2,1,0:T(8,128)(2,1)}, u32[]{:S(2)}, u32[]{:S(2)}) async-start(bf16[64,8,512]{2,1,0:T(8,128)(2,1)} %bitcast.21), calls=%async_computation | async-start | bytes 1048576 | tf_op jit(solution)/shard_map/all_to_all | solution.py:114
  25.8 8.8 %collective-permute-start.2 = (bf16[256,512]{1,0:T(8,128)(2,1)S(1)}, bf16[256,512]{1,0:T(8,128)(2,1)S(1)}, u32[]{:S(2)}, u32[]{:S(2)}) collective-permute-start(bf16[256,512]{1,0:T(8,128)(2,1)S(1)} %get-tuple-element.12), channel_id=1, source_target_pairs={{0,128},{64,192},{128,256},{192,320},{256,384},{320,448},{384,0},{... | collective-permute-start | bytes 786440 | tf_op jit(solution)/shard_map/ppermute | solution.py:85
  29.4 9.8 %collective-permute-start.3 = (bf16[256,512]{1,0:T(8,128)(2,1)S(1)}, bf16[256,512]{1,0:T(8,128)(2,1)S(1)}, u32[]{:S(2)}, u32[]{:S(2)}) collective-permute-start(bf16[256,512]{1,0:T(8,128)(2,1)S(1)} %get-tuple-element.13), channel_id=1, source_target_pairs={{0,384},{64,448},{128,0},{192,64},{256,128},{320,192},{384,256},{4... | collective-permute-start | bytes 786440 | tf_op jit(solution)/shard_map/ppermute | solution.py:85
  40.1 7.4 %collective-permute-start.4 = (bf16[512,512]{1,0:T(8,128)(2,1)}, bf16[512,512]{1,0:T(8,128)(2,1)S(1)}, u32[]{:S(2)}, u32[]{:S(2)}) collective-permute-start(bf16[512,512]{1,0:T(8,128)(2,1)} %shard_map.61.mine_ref), channel_id=1, source_target_pairs={{0,64},{64,0},{128,192},{192,128},{256,320},{320,256},{384,448},{4... | collective-permute-start | bytes 1572872 | tf_op jit(solution)/shard_map/ppermute | solution.py:142
  44.4 3.1 %copy-start.1 = (f32[1,1,512,512]{3,2,1,0:T(8,128)S(1)}, f32[1,1,512,512]{3,2,1,0:T(8,128)}, u32[]{:S(2)}) copy-start(f32[1,1,512,512]{3,2,1,0:T(8,128)} %param.5) | copy-start | bytes 3145732
  47.5 14.4 %copy-start.3 = (s32[1,64]{1,0:T(1,128)S(1)}, s32[1,64]{1,0:T(1,128)}, u32[]{:S(2)}) copy-start(s32[1,64]{1,0:T(1,128)} %param.7) | copy-start | bytes 772
  47.5 34.3 %copy-start.2 = (bf16[64,1,8,512]{3,2,1,0:T(8,128)(2,1)S(1)}, bf16[64,1,8,512]{3,2,1,0:T(8,128)(2,1)}, u32[]{:S(2)}) copy-start(bf16[64,1,8,512]{3,2,1,0:T(8,128)(2,1)} %param.6) | copy-start | bytes 1572868
  51.5 30.4 %all-to-all-start.1 = ((bf16[64,8,512]{2,1,0:T(8,128)(2,1)}), bf16[64,8,512]{2,1,0:T(8,128)(2,1)S(1)}, u32[]{:S(2)}, u32[]{:S(2)}) async-start(bf16[64,8,512]{2,1,0:T(8,128)(2,1)} %bitcast.8), calls=%async_computation.1 | async-start | bytes 1048576 | tf_op jit(solution)/shard_map/all_to_all | solution.py:162

commit v4 on v3

v4 whole, which is shorter than its diff:
```python
import jax
import jax.numpy as jnp
from jax import lax
from jax.experimental import pallas as pl
from jax.experimental.pallas import tpu as pltpu
from jax.sharding import PartitionSpec as P

keep_rate = 0.8
VMEM = pl.BlockSpec(memory_space=pltpu.VMEM)
ANY = pl.BlockSpec(memory_space=pl.ANY)
SMEM = pl.BlockSpec(memory_space=pltpu.SMEM)
PARAMS = pltpu.CompilerParams(vmem_limit_bytes=20 * 1024 * 1024)


def dot(a, b):
    return jnp.dot(a, b, preferred_element_type=jnp.float32)


def split(value):
    high = value.astype(jnp.bfloat16)
    return high, (value - high.astype(jnp.float32)).astype(jnp.bfloat16)


def fifth_kernel(root_ref, high_ref, low_ref):
    root = root_ref[...]
    high, low = split(dot(root, root))
    high, low = split(dot(high, high) + (dot(high, low) + dot(low, high)))
    high_ref[...], low_ref[...] = split(dot(root, high) + dot(root, low))


def add(*values):
    return sum(value.astype(jnp.float32) for value in values).astype(jnp.bfloat16)


def chip_kernel(place_ref, *refs):
    ring = len(refs) // 3
    for k in range(ring):
        refs[2 * ring + k][...] = add(refs[k][0], refs[ring + k][0])


def finish_kernel(*refs):
    refs[-1][...] = add(*[ref[...] for ref in refs[:-1]])


def refresh_kernel(side_ref, mine_ref, other_ref, factor_ref, root_ref, high_ref, low_ref, fresh_ref, refined_ref):
    summed = jnp.concatenate([mine_ref[...], other_ref[...]], axis=0)

    def update(gram):
        fresh_ref[...] = keep_rate * factor_ref[...] + (1.0 - keep_rate) * gram

    @pl.when(side_ref[0] == 0)
    def _():
        update(lax.dot_general(summed, summed, (((1,), (1,)), ((), ())), preferred_element_type=jnp.float32))

    @pl.when(side_ref[0] != 0)
    def _():
        update(lax.dot_general(summed, summed, (((0,), (0,)), ((), ())), preferred_element_type=jnp.float32))

    high, low = split(fresh_ref[...])
    coupled = dot(high_ref[...], high) + (dot(high_ref[...], low) + dot(low_ref[...], high))
    refined_ref[...] = (1.25 * root_ref[...].astype(jnp.float32) - 0.25 * coupled).astype(jnp.bfloat16)


def cost(flops, moved):
    return pl.CostEstimate(flops=flops, bytes_accessed=moved, transcendentals=0)


def local(grad_parts, factors, root_prev, plan):
    workers = lax.axis_size("mp")
    replicas = lax.axis_size("dp")
    size = factors.shape[-1]
    half = size // 2
    blocks = grad_parts[0, 0]
    ring = blocks.shape[0]
    dp = lax.axis_index("dp")
    x, side = dp // 2, dp % 2

    def swapped(value):
        return lax.ppermute(value, "dp", [(i, i ^ 1) for i in range(replicas)])

    def around(value, step):
        pairs = [(i, (i // 2 + (1 - 2 * (i % 2)) * step) % ring * 2 + i % 2) for i in range(replicas)]
        return lax.ppermute(value, "dp", pairs)

    theirs = swapped(blocks)
    old_pieces = root_prev.reshape(workers, size // workers, size)
    initial = lax.all_to_all(old_pieces, "mp", split_axis=0, concat_axis=0, tiled=True).reshape(size, size)

    matrix = jax.ShapeDtypeStruct((size, size), jnp.bfloat16)
    part = jax.ShapeDtypeStruct((half, size), jnp.bfloat16)

    def my_half(step):
        def index(i, place):
            return (place[0] + (1 - 2 * place[1]) * step + ring) % ring, place[1], 0

        return pl.BlockSpec((1, half, size), index)

    specs = [my_half(step) for step in range(ring)]
    sums = pl.pallas_call(
        chip_kernel,
        out_shape=(part,) * ring,
        grid_spec=pltpu.PrefetchScalarGridSpec(
            num_scalar_prefetch=1,
            grid=(1,),
            in_specs=specs * 2,
            out_specs=(pl.BlockSpec((half, size), lambda i, place: (0, 0)),) * ring,
        ),
        compiler_params=PARAMS,
        cost_estimate=cost(0, 1),
    )(jnp.stack([x, side]), *[blocks] * ring, *[theirs] * ring)
    received = [around(sums[step], step) for step in range(1, ring)]
    mine = pl.pallas_call(
        finish_kernel,
        out_shape=part,
        in_specs=[VMEM] * ring,
        out_specs=VMEM,
        compiler_params=PARAMS,
        cost_estimate=cost(0, 1),
    )(sums[0], *received)
    other = swapped(mine)

    flops = 2 * size**3
    high, low = pl.pallas_call(
        fifth_kernel,
        out_shape=(matrix, matrix),
        in_specs=[VMEM],
        out_specs=(VMEM, VMEM),
        compiler_params=PARAMS,
        cost_estimate=cost(6 * flops, 6 * size**2),
    )(initial)
    fresh, refined = pl.pallas_call(
        refresh_kernel,
        out_shape=(jax.ShapeDtypeStruct((size, size), jnp.float32), matrix),
        in_specs=[SMEM] + [VMEM] * 6,
        out_specs=(VMEM, VMEM),
        compiler_params=PARAMS,
        cost_estimate=cost(4 * flops, 22 * size**2),
    )(side.reshape(1), mine, other, factors[0, 0], initial, high, low)

    fresh_roots = lax.all_to_all(refined.reshape(old_pieces.shape), "mp", split_axis=0, concat_axis=0, tiled=True)
    refresh = plan[0] < workers
    new_roots = jnp.where(refresh[:, None, None], fresh_roots, old_pieces).reshape(root_prev.shape)
    return fresh[None, None], new_roots


def solution(mesh):
    return jax.shard_map(
        local,
        mesh=mesh,
        in_specs=(
            P("dp", "mp", None, None, None),
            P("mp", "dp", None, None),
            P(None, "dp", "mp", None),
            P("dp", None),
        ),
        out_specs=(P("mp", "dp", None, None), P(None, "dp", "mp", None)),
        check_vma=False,
    )
```

time: 83.3 us -> 80.3 us (0.964)
  the two profiles are of different devices: /device:TPU:14 before, /device:TPU:8 now
where the time goes in v4:
time: 80.3 us; the launch traced here: 79.8 us
  starting transfers between devices  46.3 us (58%)
  waiting for transfers between devices  25 us (31%)
  Pallas kernels  5.15 us (6%)
  local copies, waits for them, and re-layouts  1.61 us (2%)
  other arithmetic  1.01 us (1%)
    all_to_all x1, waiting for transfers between devices, local(): lax.all_to_all(refined.reshape(old_pieces.shape), 'mp', split_axis=0, con...  19.5 us
    all_to_all x1, starting transfers between devices, local(): lax.all_to_all(old_pieces, 'mp', split_axis=0, concat_axis=0, tiled=True)  16.6 us
    all_to_all x1, starting transfers between devices, local(): lax.all_to_all(refined.reshape(old_pieces.shape), 'mp', split_axis=0, con...  12.7 us
    ppermute x3, starting transfers between devices, around(): return lax.ppermute(value, 'dp', pairs)  11.4 us
    ppermute x2, starting transfers between devices, swapped(): return lax.ppermute(value, 'dp', [(i, i ^ 1) for i in range(replicas)])  5.63 us
    ppermute x3, waiting for transfers between devices, around(): return lax.ppermute(value, 'dp', pairs)  5.49 us
    pallas_call x1, Pallas kernels, local(): pl.pallas_call(refresh_kernel, out_shape=(jax.ShapeDtypeStruct((size, siz...  2.29 us
    pallas_call x1, Pallas kernels, local(): pl.pallas_call(fifth_kernel, out_shape=(matrix, matrix), in_specs=[VMEM],...  1.94 us
  transfers between devices with their start and end apart: 7, of which 3 were waited for; matrix products, arithmetic and copies ran while one was open for 0% of the time, Pallas kernels for 4%

profile of v4, /device:TPU:8, one launch (start us, length us, event | category | flops | bytes accessed | tf_op | source)
XLA Modules:
  0.0 79.8 jit_solution(16896459862014908953)
XLA Ops:
  0.6 1.9 %collective-permute-start = (bf16[4,512,512]{2,1,0:T(8,128)(2,1)}, bf16[4,512,512]{2,1,0:T(8,128)(2,1)S(1)}, u32[]{:S(2)}, u32[]{:S(2)}) collective-permute-start(bf16[4,512,512]{2,1,0:T(8,128)(2,1)} %bitcast.13), channel_id=1, source_target_pairs={{0,64},{64,0},{128,192},{192,128},{256,320},{320,256},{384,448},{4... | collective-permute-start | bytes 6291464 | tf_op jit(solution)/shard_map/ppermute | solution.py:79
  2.6 16.6 %all-to-all-start = ((bf16[64,8,512]{2,1,0:T(8,128)(2,1)}), bf16[64,8,512]{2,1,0:T(8,128)(2,1)S(1)}, u32[]{:S(2)}, u32[]{:S(2)}) async-start(bf16[64,8,512]{2,1,0:T(8,128)(2,1)} %bitcast.21), calls=%async_computation | async-start | bytes 1048576 | tf_op jit(solution)/shard_map/all_to_all | solution.py:87
  19.2 0.1 pad_add_fusion.place_ref
  19.3 0.0 collective-permute-done.refs_4_.refs_5_.refs_6_.refs_7_
  19.3 1.6 %copy-done = bf16[1,1,4,512,512]{4,3,2,1,0:T(8,128)(2,1)S(1)} copy-done((bf16[1,1,4,512,512]{4,3,2,1,0:T(8,128)(2,1)S(1)}, bf16[1,1,4,512,512]{4,3,2,1,0:T(8,128)(2,1)}, u32[]{:S(2)}) %copy-start) | copy-done | bytes 2097176
  20.9 0.8 shard_map.59
  21.6 3.4 %collective-permute-start.1 = (bf16[256,512]{1,0:T(8,128)(2,1)S(1)}, bf16[256,512]{1,0:T(8,128)(2,1)S(1)}, u32[]{:S(2)}, u32[]{:S(2)}) collective-permute-start(bf16[256,512]{1,0:T(8,128)(2,1)S(1)} %get-tuple-element.11), channel_id=1, source_target_pairs={{0,128},{64,448},{128,256},{192,64},{256,384},{320,192},{384,0},{4... | collective-permute-start | bytes 786440 | tf_op jit(solution)/shard_map/ppermute | solution.py:83
  25.1 4.6 %collective-permute-start.2 = (bf16[256,512]{1,0:T(8,128)(2,1)S(1)}, bf16[256,512]{1,0:T(8,128)(2,1)S(1)}, u32[]{:S(2)}, u32[]{:S(2)}) collective-permute-start(bf16[256,512]{1,0:T(8,128)(2,1)S(1)} %get-tuple-element.12), channel_id=1, source_target_pairs={{0,256},{64,320},{128,384},{192,448},{256,0},{320,64},{384,128},{4... | collective-permute-start | bytes 786440 | tf_op jit(solution)/shard_map/ppermute | solution.py:83
  29.7 3.3 %collective-permute-start.3 = (bf16[256,512]{1,0:T(8,128)(2,1)S(1)}, bf16[256,512]{1,0:T(8,128)(2,1)S(1)}, u32[]{:S(2)}, u32[]{:S(2)}) collective-permute-start(bf16[256,512]{1,0:T(8,128)(2,1)S(1)} %get-tuple-element.13), channel_id=1, source_target_pairs={{0,384},{64,192},{128,0},{192,320},{256,128},{320,448},{384,256},{... | collective-permute-start | bytes 786440 | tf_op jit(solution)/shard_map/ppermute | solution.py:83
  33.1 0.0 collective-permute-done.1.refs_1_
  33.1 4.8 %collective-permute-done.2.refs_2_ = bf16[256,512]{1,0:T(8,128)(2,1)S(1)} collective-permute-done((bf16[256,512]{1,0:T(8,128)(2,1)S(1)}, bf16[256,512]{1,0:T(8,128)(2,1)S(1)}, u32[]{:S(2)}, u32[]{:S(2)}) %collective-permute-start.2) | collective-permute-done | bytes 262176 | tf_op jit(solution)/shard_map/ppermute | solution.py:83
  37.8 0.7 collective-permute-done.3.refs_3_
  38.6 0.1 shard_map.60.mine_ref
  38.7 3.7 %collective-permute-start.4 = (bf16[256,512]{1,0:T(8,128)(2,1)S(1)}, bf16[256,512]{1,0:T(8,128)(2,1)S(1)}, u32[]{:S(2)}, u32[]{:S(2)}) collective-permute-start(bf16[256,512]{1,0:T(8,128)(2,1)S(1)} %shard_map.60.mine_ref), channel_id=1, source_target_pairs={{0,64},{64,0},{128,192},{192,128},{256,320},{320,256},{384,448},{4... | collective-permute-start | bytes 786440 | tf_op jit(solution)/shard_map/ppermute | solution.py:79
  42.4 0.0 all-to-all-done
  42.4 0.0 copy-start.1
  42.4 1.9 %shard_map.61 = (bf16[512,512]{1,0:T(8,128)(2,1)S(1)}, bf16[512,512]{1,0:T(8,128)(2,1)S(1)}) custom-call(bf16[512,512]{1,0:T(8,128)(2,1)S(1)} %bitcast.18), custom_call_target="tpu_custom_call" | custom-call | flops 1610612736 | bytes 1572864 | tf_op jit(solution)/shard_map/pallas_call | solution.py:123
  44.4 0.0 collective-permute-done.4.other_ref
  44.4 0.0 copy-start.3
  44.4 0.0 copy-start.2
  44.4 2.3 %shard_map.62 = (f32[512,512]{1,0:T(8,128)}, bf16[512,512]{1,0:T(8,128)(2,1)}) custom-call(s32[1]{0:T(128)} %bitcast.side_ref, bf16[256,512]{1,0:T(8,128)(2,1)S(1)} %shard_map.60.mine_ref, bf16[256,512]{1,0:T(8,128)(2,1)S(1)} %collective-permute-done.4.other_ref, f32[512,512]{1,0:T(8,128)S(1)} %bitcast.20, bf16[512,512]{1,0:T(8,128)(2,1)S(1)} %bitcast.19, ...), custom_call_target="tpu_custom_call" | custom-call | flops 1073741824 | bytes 5767168 | tf_op jit(solution)/shard_map/pallas_call | solution.py:131
  46.7 12.7 %all-to-all-start.1 = ((bf16[64,8,512]{2,1,0:T(8,128)(2,1)}), bf16[64,8,512]{2,1,0:T(8,128)(2,1)S(1)}, u32[]{:S(2)}, u32[]{:S(2)}) async-start(bf16[64,8,512]{2,1,0:T(8,128)(2,1)} %bitcast.8), calls=%async_computation.1 | async-start | bytes 1048576 | tf_op jit(solution)/shard_map/all_to_all | solution.py:140
  59.4 19.5 %all-to-all-done.1 = bf16[64,8,512]{2,1,0:T(8,128)(2,1)S(1)} async-done(((bf16[64,8,512]{2,1,0:T(8,128)(2,1)}), bf16[64,8,512]{2,1,0:T(8,128)(2,1)S(1)}, u32[]{:S(2)}, u32[]{:S(2)}) %all-to-all-start.1) | async-done | bytes 524320 | tf_op jit(solution)/shard_map/all_to_all | solution.py:140
  78.9 0.9 %select_bitcast_fusion = bf16[64,1,8,512]{3,2,1,0:T(8,128)(2,1)} fusion(bf16[64,8,512]{2,1,0:T(8,128)(2,1)S(1)} %all-to-all-done.1, pred[64]{0:T(512)(128)(4,1)S(1)} %compare_bitcast_fusion, bf16[64,1,8,512]{3,2,1,0:T(8,128)(2,1)S(1)} %copy-done.2), kind=kLoop, calls=%fused_computation | loop fusion | flops 262144 | bytes 1572928 | tf_op jit(solution)/shard_map/reshape | solution.py:142
  (5 shorter events, 0.0 us)
Async XLA Ops:
  0.6 18.6 %collective-permute-start = (bf16[4,512,512]{2,1,0:T(8,128)(2,1)}, bf16[4,512,512]{2,1,0:T(8,128)(2,1)S(1)}, u32[]{:S(2)}, u32[]{:S(2)}) collective-permute-start(bf16[4,512,512]{2,1,0:T(8,128)(2,1)} %bitcast.13), channel_id=1, source_target_pairs={{0,64},{64,0},{128,192},{192,128},{256,320},{320,256},{384,448},{4... | collective-permute-start | bytes 6291464 | tf_op jit(solution)/shard_map/ppermute | solution.py:79
  2.6 39.9 %all-to-all-start = ((bf16[64,8,512]{2,1,0:T(8,128)(2,1)}), bf16[64,8,512]{2,1,0:T(8,128)(2,1)S(1)}, u32[]{:S(2)}, u32[]{:S(2)}) async-start(bf16[64,8,512]{2,1,0:T(8,128)(2,1)} %bitcast.21), calls=%async_computation | async-start | bytes 1048576 | tf_op jit(solution)/shard_map/all_to_all | solution.py:87
  19.3 1.6 %copy-start = (bf16[1,1,4,512,512]{4,3,2,1,0:T(8,128)(2,1)S(1)}, bf16[1,1,4,512,512]{4,3,2,1,0:T(8,128)(2,1)}, u32[]{:S(2)}) copy-start(bf16[1,1,4,512,512]{4,3,2,1,0:T(8,128)(2,1)} %param.4) | copy-start | bytes 6291460
  21.6 11.4 %collective-permute-start.1 = (bf16[256,512]{1,0:T(8,128)(2,1)S(1)}, bf16[256,512]{1,0:T(8,128)(2,1)S(1)}, u32[]{:S(2)}, u32[]{:S(2)}) collective-permute-start(bf16[256,512]{1,0:T(8,128)(2,1)S(1)} %get-tuple-element.11), channel_id=1, source_target_pairs={{0,128},{64,448},{128,256},{192,64},{256,384},{320,192},{384,0},{4... | collective-permute-start | bytes 786440 | tf_op jit(solution)/shard_map/ppermute | solution.py:83
  25.1 12.8 %collective-permute-start.2 = (bf16[256,512]{1,0:T(8,128)(2,1)S(1)}, bf16[256,512]{1,0:T(8,128)(2,1)S(1)}, u32[]{:S(2)}, u32[]{:S(2)}) collective-permute-start(bf16[256,512]{1,0:T(8,128)(2,1)S(1)} %get-tuple-element.12), channel_id=1, source_target_pairs={{0,256},{64,320},{128,384},{192,448},{256,0},{320,64},{384,128},{4... | collective-permute-start | bytes 786440 | tf_op jit(solution)/shard_map/ppermute | solution.py:83
  29.7 8.9 %collective-permute-start.3 = (bf16[256,512]{1,0:T(8,128)(2,1)S(1)}, bf16[256,512]{1,0:T(8,128)(2,1)S(1)}, u32[]{:S(2)}, u32[]{:S(2)}) collective-permute-start(bf16[256,512]{1,0:T(8,128)(2,1)S(1)} %get-tuple-element.13), channel_id=1, source_target_pairs={{0,384},{64,192},{128,0},{192,320},{256,128},{320,448},{384,256},{... | collective-permute-start | bytes 786440 | tf_op jit(solution)/shard_map/ppermute | solution.py:83
  38.7 5.7 %collective-permute-start.4 = (bf16[256,512]{1,0:T(8,128)(2,1)S(1)}, bf16[256,512]{1,0:T(8,128)(2,1)S(1)}, u32[]{:S(2)}, u32[]{:S(2)}) collective-permute-start(bf16[256,512]{1,0:T(8,128)(2,1)S(1)} %shard_map.60.mine_ref), channel_id=1, source_target_pairs={{0,64},{64,0},{128,192},{192,128},{256,320},{320,256},{384,448},{4... | collective-permute-start | bytes 786440 | tf_op jit(solution)/shard_map/ppermute | solution.py:79
  42.4 2.0 %copy-start.1 = (f32[1,1,512,512]{3,2,1,0:T(8,128)S(1)}, f32[1,1,512,512]{3,2,1,0:T(8,128)}, u32[]{:S(2)}) copy-start(f32[1,1,512,512]{3,2,1,0:T(8,128)} %param.5) | copy-start | bytes 3145732
  44.4 15.0 %copy-start.3 = (s32[1,64]{1,0:T(1,128)S(1)}, s32[1,64]{1,0:T(1,128)}, u32[]{:S(2)}) copy-start(s32[1,64]{1,0:T(1,128)} %param.7) | copy-start | bytes 772
  44.4 34.5 %copy-start.2 = (bf16[64,1,8,512]{3,2,1,0:T(8,128)(2,1)S(1)}, bf16[64,1,8,512]{3,2,1,0:T(8,128)(2,1)}, u32[]{:S(2)}) copy-start(bf16[64,1,8,512]{3,2,1,0:T(8,128)(2,1)} %param.6) | copy-start | bytes 1572868
  46.7 32.2 %all-to-all-start.1 = ((bf16[64,8,512]{2,1,0:T(8,128)(2,1)}), bf16[64,8,512]{2,1,0:T(8,128)(2,1)S(1)}, u32[]{:S(2)}, u32[]{:S(2)}) async-start(bf16[64,8,512]{2,1,0:T(8,128)(2,1)} %bitcast.8), calls=%async_computation.1 | async-start | bytes 1048576 | tf_op jit(solution)/shard_map/all_to_all | solution.py:140

commit v5 on v4

--- a/solution.py
+++ b/solution.py
@@ -32,18 +32,8 @@
     return sum(value.astype(jnp.float32) for value in values).astype(jnp.bfloat16)
 
 
-def chip_kernel(place_ref, *refs):
-    ring = len(refs) // 3
-    for k in range(ring):
-        refs[2 * ring + k][...] = add(refs[k][0], refs[ring + k][0])
-
-
-def finish_kernel(*refs):
-    refs[-1][...] = add(*[ref[...] for ref in refs[:-1]])
-
-
 def refresh_kernel(side_ref, mine_ref, other_ref, factor_ref, root_ref, high_ref, low_ref, fresh_ref, refined_ref):
-    summed = jnp.concatenate([mine_ref[...], other_ref[...]], axis=0)
+    summed = add(mine_ref[...], other_ref[...])
 
     def update(gram):
         fresh_ref[...] = keep_rate * factor_ref[...] + (1.0 - keep_rate) * gram
@@ -69,7 +59,6 @@
     workers = lax.axis_size("mp")
     replicas = lax.axis_size("dp")
     size = factors.shape[-1]
-    half = size // 2
     blocks = grad_parts[0, 0]
     ring = blocks.shape[0]
     dp = lax.axis_index("dp")
@@ -78,47 +67,25 @@
     def swapped(value):
         return lax.ppermute(value, "dp", [(i, i ^ 1) for i in range(replicas)])
 
-    def around(value, step):
-        pairs = [(i, (i // 2 + (1 - 2 * (i % 2)) * step) % ring * 2 + i % 2) for i in range(replicas)]
-        return lax.ppermute(value, "dp", pairs)
+    def block(values, step):
+        return lax.dynamic_index_in_dim(values, (x + step + ring) % ring, 0, keepdims=False)
 
     theirs = swapped(blocks)
+    opposite = [(i, (i // 2 + 2) % ring * 2 + i % 2) for i in range(replicas)]
+    from_opposite = lax.ppermute(block(blocks, 2), "dp", opposite)
     old_pieces = root_prev.reshape(workers, size // workers, size)
     initial = lax.all_to_all(old_pieces, "mp", split_axis=0, concat_axis=0, tiled=True).reshape(size, size)
 
-    matrix = jax.ShapeDtypeStruct((size, size), jnp.bfloat16)
-    part = jax.ShapeDtypeStruct((half, size), jnp.bfloat16)
-
-    def my_half(step):
-        def index(i, place):
-            return (place[0] + (1 - 2 * place[1]) * step + ring) % ring, place[1], 0
-
-        return pl.BlockSpec((1, half, size), index)
-
-    specs = [my_half(step) for step in range(ring)]
-    sums = pl.pallas_call(
-        chip_kernel,
-        out_shape=(part,) * ring,
-        grid_spec=pltpu.PrefetchScalarGridSpec(
-            num_scalar_prefetch=1,
-            grid=(1,),
-            in_specs=specs * 2,
-            out_specs=(pl.BlockSpec((half, size), lambda i, place: (0, 0)),) * ring,
-        ),
-        compiler_params=PARAMS,
-        cost_estimate=cost(0, 1),
-    )(jnp.stack([x, side]), *[blocks] * ring, *[theirs] * ring)
-    received = [around(sums[step], step) for step in range(1, ring)]
-    mine = pl.pallas_call(
-        finish_kernel,
-        out_shape=part,
-        in_specs=[VMEM] * ring,
-        out_specs=VMEM,
-        compiler_params=PARAMS,
-        cost_estimate=cost(0, 1),
-    )(sums[0], *received)
+    theirs, from_opposite = lax.optimization_barrier((theirs, from_opposite))
+    ahead = 1 - 2 * side
+    for_next = add(block(blocks, ahead), block(theirs, ahead))
+    onward = [(i, (i // 2 + 1 - 2 * (i % 2)) % ring * 2 + i % 2) for i in range(replicas)]
+    cut = size * 3 // 4
+    from_last = jnp.concatenate([lax.ppermute(rows, "dp", onward) for rows in (for_next[:cut], for_next[cut:])])
+    mine = add(block(blocks, 0), from_opposite, from_last)
     other = swapped(mine)
 
+    matrix = jax.ShapeDtypeStruct((size, size), jnp.bfloat16)
     flops = 2 * size**3
     high, low = pl.pallas_call(
         fifth_kernel,

time: 80.3 us -> 83 us (1.034)
  starting transfers between devices: 46.3 us -> 41.3 us
  waiting for transfers between devices: 25 us -> 29 us
  other arithmetic: 1.01 us -> 3.56 us
  local copies, waits for them, and re-layouts: 1.61 us -> 3.34 us
    convert_element_type x0 -> x2, other arithmetic: none -> 2.62 us  [add(): sum((value.astype(jnp.float32) for value in values)).astype(jnp.bfloat16)]
    ppermute x3, starting transfers between devices: 11.4 us -> 9.32 us  [the longest x1 4.92 us: local(): from_opposite = lax.ppermute(block(blocks, 2), 'dp', opposite)]
    ppermute x3, waiting for transfers between devices: 5.49 us -> 7.49 us  [the longest x2 7.49 us: local(): lax.ppermute(rows, 'dp', onward)]
    squeeze x0 -> x1, local copies, waits for them, and re-layouts: none -> 1.87 us  [block(): lax.dynamic_index_in_dim(values, (x + step + ring) % ring, 0, keepdims=Fa...]
    ppermute x2, starting transfers between devices: 5.63 us -> 3.97 us  [swapped(): return lax.ppermute(value, 'dp', [(i, i ^ 1) for i in range(replicas)])]
    unnamed x8 -> x10, local copies, waits for them, and re-layouts: 1.61 us -> 0.03 us
    all_to_all x1, waiting for transfers between devices: 0.01 us -> 1.55 us  [local(): lax.all_to_all(old_pieces, 'mp', split_axis=0, concat_axis=0, tiled=True)]
    slice x0 -> x2, local copies, waits for them, and re-layouts: none -> 1.44 us  [the longest x1 0.77 us: local(): for_next[:cut]]
  transfers between devices with their start and end apart: 7 -> 7, of which waited for: 3 -> 3; matrix products, arithmetic and copies ran while one was open for 0% -> 7% of each run, Pallas kernels for 4% -> 2%
where the time goes in v5:
time: 83 us; the launch traced here: 82.5 us
  starting transfers between devices  41.3 us (50%)
  waiting for transfers between devices  29 us (35%)
  Pallas kernels  4.44 us (5%)
  other arithmetic  3.56 us (4%)
  local copies, waits for them, and re-layouts  3.34 us (4%)
  between operations  0.88 us (1%)
    all_to_all x1, waiting for transfers between devices, local(): lax.all_to_all(refined.reshape(old_pieces.shape), 'mp', split_axis=0, con...  20 us
    all_to_all x1, starting transfers between devices, local(): lax.all_to_all(old_pieces, 'mp', split_axis=0, concat_axis=0, tiled=True)  16.6 us
    all_to_all x1, starting transfers between devices, local(): lax.all_to_all(refined.reshape(old_pieces.shape), 'mp', split_axis=0, con...  11.4 us
    ppermute x2, waiting for transfers between devices, local(): lax.ppermute(rows, 'dp', onward)  7.49 us
    ppermute x1, starting transfers between devices, local(): from_opposite = lax.ppermute(block(blocks, 2), 'dp', opposite)  4.92 us
    ppermute x2, starting transfers between devices, local(): lax.ppermute(rows, 'dp', onward)  4.4 us
    ppermute x2, starting transfers between devices, swapped(): return lax.ppermute(value, 'dp', [(i, i ^ 1) for i in range(replicas)])  3.97 us
    convert_element_type x2, other arithmetic, add(): sum((value.astype(jnp.float32) for value in values)).astype(jnp.bfloat16)  2.62 us
  transfers between devices with their start and end apart: 7, of which 3 were waited for; matrix products, arithmetic and copies ran while one was open for 7% of the time, Pallas kernels for 2%

profile of v5, /device:TPU:8, one launch (start us, length us, event | category | flops | bytes accessed | tf_op | source)
XLA Modules:
  0.0 82.5 jit_solution(10954242247444709917)
XLA Ops:
  0.6 2.1 %collective-permute-start = (bf16[4,512,512]{2,1,0:T(8,128)(2,1)}, bf16[4,512,512]{2,1,0:T(8,128)(2,1)}, u32[]{:S(2)}, u32[]{:S(2)}) collective-permute-start(bf16[4,512,512]{2,1,0:T(8,128)(2,1)} %bitcast.27), channel_id=1, source_target_pairs={{0,64},{64,0},{128,192},{192,128},{256,320},{320,256},{384,448},{4... | collective-permute-start | bytes 6291464 | tf_op jit(solution)/shard_map/ppermute | solution.py:68
  2.7 1.9 %dynamic-slice_bitcast_fusion = bf16[512,512]{1,0:T(8,128)(2,1)} fusion(bf16[1,1,4,512,512]{4,3,2,1,0:T(8,128)(2,1)} %param.4, s32[]{:T(128)S(6)} %select_n.45), kind=kLoop, calls=%fused_computation.6 | loop fusion | bytes 1048580 | tf_op jit(solution)/shard_map/jit(dynamic_index_in_dim)/squeeze | solution.py:71
  4.6 4.9 %collective-permute-start.1 = (bf16[512,512]{1,0:T(8,128)(2,1)}, bf16[512,512]{1,0:T(8,128)(2,1)S(1)}, u32[]{:S(2)}, u32[]{:S(2)}) collective-permute-start(bf16[512,512]{1,0:T(8,128)(2,1)} %dynamic-slice_bitcast_fusion), channel_id=1, source_target_pairs={{0,256},{64,320},{128,384},{192,448},{256,0},{320,64},{384,128},{4... | collective-permute-start | bytes 1572872 | tf_op jit(solution)/shard_map/ppermute | solution.py:75
  9.5 16.6 %all-to-all-start = ((bf16[64,8,512]{2,1,0:T(8,128)(2,1)}), bf16[64,8,512]{2,1,0:T(8,128)(2,1)S(1)}, u32[]{:S(2)}, u32[]{:S(2)}) async-start(bf16[64,8,512]{2,1,0:T(8,128)(2,1)} %bitcast.26), calls=%async_computation | async-start | bytes 1048576 | tf_op jit(solution)/shard_map/all_to_all | solution.py:77
  26.2 0.0 collective-permute-done.1
  26.2 0.0 copy-start.3
  26.2 0.0 collective-permute-done
  26.2 1.4 %fusion = bf16[512,512]{1,0:T(8,128)(2,1)S(1)} fusion(bf16[4,512,512]{2,1,0:T(8,128)(2,1)} %collective-permute-done, s32[]{:T(128)S(6)} %select_n.47, bf16[1,1,4,512,512]{4,3,2,1,0:T(8,128)(2,1)S(1)} %copy-done.2), kind=kLoop, calls=%fused_computation.1 | loop fusion | flops 1048576 | bytes 1572868 | tf_op jit(solution)/shard_map/convert_element_type | solution.py:32
  27.6 0.8 slice.8
  28.3 2.5 %collective-permute-start.2 = (bf16[384,512]{1,0:T(8,128)(2,1)}, bf16[384,512]{1,0:T(8,128)(2,1)S(1)}, u32[]{:S(2)}, u32[]{:S(2)}) collective-permute-start(bf16[384,512]{1,0:T(8,128)(2,1)} %slice.8), channel_id=1, source_target_pairs={{0,128},{64,448},{128,256},{192,64},{256,384},{320,192},{384,0},{4... | collective-permute-start | bytes 1179656 | tf_op jit(solution)/shard_map/ppermute | solution.py:84
  30.8 0.7 slice.9
  31.5 1.9 %collective-permute-start.3 = (bf16[128,512]{1,0:T(8,128)(2,1)}, bf16[128,512]{1,0:T(8,128)(2,1)}, u32[]{:S(2)}, u32[]{:S(2)}) collective-permute-start(bf16[128,512]{1,0:T(8,128)(2,1)} %slice.9), channel_id=1, source_target_pairs={{0,128},{64,448},{128,256},{192,64},{256,384},{320,192},{384,0},{4... | collective-permute-start | bytes 393224 | tf_op jit(solution)/shard_map/ppermute | solution.py:84
  33.4 7.5 %collective-permute-done.3 = bf16[128,512]{1,0:T(8,128)(2,1)} collective-permute-done((bf16[128,512]{1,0:T(8,128)(2,1)}, bf16[128,512]{1,0:T(8,128)(2,1)}, u32[]{:S(2)}, u32[]{:S(2)}) %collective-permute-start.3) | collective-permute-done | bytes 131104 | tf_op jit(solution)/shard_map/ppermute | solution.py:84
  40.9 1.3 %fusion.2.mine_ref = bf16[512,512]{1,0:T(8,128)(2,1)S(1)} fusion(bf16[512,512]{1,0:T(8,128)(2,1)} %copy-done.3, bf16[128,512]{1,0:T(8,128)(2,1)} %collective-permute-done.3, bf16[384,512]{1,0:T(8,128)(2,1)S(1)} %collective-permute-done.2, bf16[1,1,4,512,512]{4,3,2,1,0:T(8,128)(2,1)S(1)} %copy-done.2, s32[]{:T(128)S(6)} %select_n.43), kind=kLoop, calls=%fused_computation.4 | loop fusion | flops 2359296 | bytes 2097156 | tf_op jit(solution)/shard_map/convert_element_type | solution.py:32
  42.2 1.9 %collective-permute-start.4 = (bf16[512,512]{1,0:T(8,128)(2,1)S(1)}, bf16[512,512]{1,0:T(8,128)(2,1)S(1)}, u32[]{:S(2)}, u32[]{:S(2)}) collective-permute-start(bf16[512,512]{1,0:T(8,128)(2,1)S(1)} %fusion.2.mine_ref), channel_id=1, source_target_pairs={{0,64},{64,0},{128,192},{192,128},{256,320},{320,256},{384,448},{4... | collective-permute-start | bytes 1572872 | tf_op jit(solution)/shard_map/ppermute | solution.py:68
  44.1 1.5 %all-to-all-done = bf16[64,8,512]{2,1,0:T(8,128)(2,1)S(1)} async-done(((bf16[64,8,512]{2,1,0:T(8,128)(2,1)}), bf16[64,8,512]{2,1,0:T(8,128)(2,1)S(1)}, u32[]{:S(2)}, u32[]{:S(2)}) %all-to-all-start) | async-done | bytes 524320 | tf_op jit(solution)/shard_map/all_to_all | solution.py:77
  45.7 1.9 %shard_map.59 = (bf16[512,512]{1,0:T(8,128)(2,1)S(1)}, bf16[512,512]{1,0:T(8,128)(2,1)S(1)}) custom-call(bf16[512,512]{1,0:T(8,128)(2,1)S(1)} %bitcast.23), custom_call_target="tpu_custom_call" | custom-call | flops 1610612736 | bytes 1572864 | tf_op jit(solution)/shard_map/pallas_call | solution.py:90
  47.6 0.0 collective-permute-done.4.other_ref
  47.7 0.0 copy-start.4
  47.7 0.0 copy-start.1
  47.7 2.5 %shard_map.60 = (f32[512,512]{1,0:T(8,128)}, bf16[512,512]{1,0:T(8,128)(2,1)}) custom-call(s32[1]{0:T(128)} %bitcast.side_ref, bf16[512,512]{1,0:T(8,128)(2,1)S(1)} %fusion.2.mine_ref, bf16[512,512]{1,0:T(8,128)(2,1)S(1)} %collective-permute-done.4.other_ref, f32[512,512]{1,0:T(8,128)S(1)} %bitcast.25, bf16[512,512]{1,0:T(8,128)(2,1)S(1)} %bitcast.24, ...), custom_call_target="tpu_custom_call" | custom-call | flops 1073741824 | bytes 5767168 | tf_op jit(solution)/shard_map/pallas_call | solution.py:98
  50.2 11.4 %all-to-all-start.1 = ((bf16[64,8,512]{2,1,0:T(8,128)(2,1)}), bf16[64,8,512]{2,1,0:T(8,128)(2,1)S(1)}, u32[]{:S(2)}, u32[]{:S(2)}) async-start(bf16[64,8,512]{2,1,0:T(8,128)(2,1)} %bitcast.11), calls=%async_computation.1 | async-start | bytes 1048576 | tf_op jit(solution)/shard_map/all_to_all | solution.py:107
  61.6 20.0 %all-to-all-done.1 = bf16[64,8,512]{2,1,0:T(8,128)(2,1)S(1)} async-done(((bf16[64,8,512]{2,1,0:T(8,128)(2,1)}), bf16[64,8,512]{2,1,0:T(8,128)(2,1)S(1)}, u32[]{:S(2)}, u32[]{:S(2)}) %all-to-all-start.1) | async-done | bytes 524320 | tf_op jit(solution)/shard_map/all_to_all | solution.py:107
  81.6 0.9 %select_bitcast_fusion = bf16[64,1,8,512]{3,2,1,0:T(8,128)(2,1)} fusion(bf16[64,8,512]{2,1,0:T(8,128)(2,1)S(1)} %all-to-all-done.1, pred[64]{0:T(512)(128)(4,1)S(1)} %compare_bitcast_fusion, bf16[64,1,8,512]{3,2,1,0:T(8,128)(2,1)S(1)} %copy-done.1), kind=kLoop, calls=%fused_computation.5 | loop fusion | flops 262144 | bytes 1572928 | tf_op jit(solution)/shard_map/reshape | solution.py:109
  (9 shorter events, 0.0 us)
Async XLA Ops:
  0.6 25.6 %copy-start.2 = (bf16[1,1,4,512,512]{4,3,2,1,0:T(8,128)(2,1)S(1)}, bf16[1,1,4,512,512]{4,3,2,1,0:T(8,128)(2,1)}, u32[]{:S(2)}) copy-start(bf16[1,1,4,512,512]{4,3,2,1,0:T(8,128)(2,1)} %param.4) | copy-start | bytes 6291460
  0.6 25.6 %collective-permute-start = (bf16[4,512,512]{2,1,0:T(8,128)(2,1)}, bf16[4,512,512]{2,1,0:T(8,128)(2,1)}, u32[]{:S(2)}, u32[]{:S(2)}) collective-permute-start(bf16[4,512,512]{2,1,0:T(8,128)(2,1)} %bitcast.27), channel_id=1, source_target_pairs={{0,64},{64,0},{128,192},{192,128},{256,320},{320,256},{384,448},{4... | collective-permute-start | bytes 6291464 | tf_op jit(solution)/shard_map/ppermute | solution.py:68
  4.6 21.6 %collective-permute-start.1 = (bf16[512,512]{1,0:T(8,128)(2,1)}, bf16[512,512]{1,0:T(8,128)(2,1)S(1)}, u32[]{:S(2)}, u32[]{:S(2)}) collective-permute-start(bf16[512,512]{1,0:T(8,128)(2,1)} %dynamic-slice_bitcast_fusion), channel_id=1, source_target_pairs={{0,256},{64,320},{128,384},{192,448},{256,0},{320,64},{384,128},{4... | collective-permute-start | bytes 1572872 | tf_op jit(solution)/shard_map/ppermute | solution.py:75
  9.5 36.1 %all-to-all-start = ((bf16[64,8,512]{2,1,0:T(8,128)(2,1)}), bf16[64,8,512]{2,1,0:T(8,128)(2,1)S(1)}, u32[]{:S(2)}, u32[]{:S(2)}) async-start(bf16[64,8,512]{2,1,0:T(8,128)(2,1)} %bitcast.26), calls=%async_computation | async-start | bytes 1048576 | tf_op jit(solution)/shard_map/all_to_all | solution.py:77
  26.2 14.8 %copy-start.3 = (bf16[512,512]{1,0:T(8,128)(2,1)}, bf16[512,512]{1,0:T(8,128)(2,1)S(1)}, u32[]{:S(2)}) copy-start(bf16[512,512]{1,0:T(8,128)(2,1)S(1)} %collective-permute-done.1) | copy-start | bytes 1572868
  28.3 12.6 %collective-permute-start.2 = (bf16[384,512]{1,0:T(8,128)(2,1)}, bf16[384,512]{1,0:T(8,128)(2,1)S(1)}, u32[]{:S(2)}, u32[]{:S(2)}) collective-permute-start(bf16[384,512]{1,0:T(8,128)(2,1)} %slice.8), channel_id=1, source_target_pairs={{0,128},{64,448},{128,256},{192,64},{256,384},{320,192},{384,0},{4... | collective-permute-start | bytes 1179656 | tf_op jit(solution)/shard_map/ppermute | solution.py:84
  31.5 9.4 %collective-permute-start.3 = (bf16[128,512]{1,0:T(8,128)(2,1)}, bf16[128,512]{1,0:T(8,128)(2,1)}, u32[]{:S(2)}, u32[]{:S(2)}) collective-permute-start(bf16[128,512]{1,0:T(8,128)(2,1)} %slice.9), channel_id=1, source_target_pairs={{0,128},{64,448},{128,256},{192,64},{256,384},{320,192},{384,0},{4... | collective-permute-start | bytes 393224 | tf_op jit(solution)/shard_map/ppermute | solution.py:84
  42.2 5.4 %collective-permute-start.4 = (bf16[512,512]{1,0:T(8,128)(2,1)S(1)}, bf16[512,512]{1,0:T(8,128)(2,1)S(1)}, u32[]{:S(2)}, u32[]{:S(2)}) collective-permute-start(bf16[512,512]{1,0:T(8,128)(2,1)S(1)} %fusion.2.mine_ref), channel_id=1, source_target_pairs={{0,64},{64,0},{128,192},{192,128},{256,320},{320,256},{384,448},{4... | collective-permute-start | bytes 1572872 | tf_op jit(solution)/shard_map/ppermute | solution.py:68
  45.7 2.0 %copy-start = (f32[1,1,512,512]{3,2,1,0:T(8,128)S(1)}, f32[1,1,512,512]{3,2,1,0:T(8,128)}, u32[]{:S(2)}) copy-start(f32[1,1,512,512]{3,2,1,0:T(8,128)} %param.5) | copy-start | bytes 3145732
  47.7 13.9 %copy-start.4 = (s32[1,64]{1,0:T(1,128)S(1)}, s32[1,64]{1,0:T(1,128)}, u32[]{:S(2)}) copy-start(s32[1,64]{1,0:T(1,128)} %param.7) | copy-start | bytes 772
  47.7 33.9 %copy-start.1 = (bf16[64,1,8,512]{3,2,1,0:T(8,128)(2,1)S(1)}, bf16[64,1,8,512]{3,2,1,0:T(8,128)(2,1)}, u32[]{:S(2)}) copy-start(bf16[64,1,8,512]{3,2,1,0:T(8,128)(2,1)} %param.6) | copy-start | bytes 1572868
  50.2 31.4 %all-to-all-start.1 = ((bf16[64,8,512]{2,1,0:T(8,128)(2,1)}), bf16[64,8,512]{2,1,0:T(8,128)(2,1)S(1)}, u32[]{:S(2)}, u32[]{:S(2)}) async-start(bf16[64,8,512]{2,1,0:T(8,128)(2,1)} %bitcast.11), calls=%async_computation.1 | async-start | bytes 1048576 | tf_op jit(solution)/shard_map/all_to_all | solution.py:107

commit v6 on v4

--- a/solution.py
+++ b/solution.py
@@ -7,7 +7,7 @@
 
 keep_rate = 0.8
 VMEM = pl.BlockSpec(memory_space=pltpu.VMEM)
-ANY = pl.BlockSpec(memory_space=pl.ANY)
+HBM = pl.BlockSpec(memory_space=pltpu.HBM)
 SMEM = pl.BlockSpec(memory_space=pltpu.SMEM)
 PARAMS = pltpu.CompilerParams(vmem_limit_bytes=20 * 1024 * 1024)
 
@@ -21,11 +21,18 @@
     return high, (value - high.astype(jnp.float32)).astype(jnp.bfloat16)
 
 
-def fifth_kernel(root_ref, high_ref, low_ref):
+def base_kernel(root_ref, factor_ref, fifth_ref, base_ref, old, sem):
+    load = pltpu.make_async_copy(factor_ref, old, sem)
+    load.start()
     root = root_ref[...]
     high, low = split(dot(root, root))
     high, low = split(dot(high, high) + (dot(high, low) + dot(low, high)))
-    high_ref[...], low_ref[...] = split(dot(root, high) + dot(root, low))
+    high, low = split(dot(root, high) + dot(root, low))
+    fifth_ref[...] = high
+    load.wait()
+    factor, rest = split(old[...])
+    coupled = dot(high, factor) + (dot(high, rest) + dot(low, factor))
+    base_ref[...] = 1.25 * root.astype(jnp.float32) - 0.25 * keep_rate * coupled
 
 
 def add(*values):
@@ -42,23 +49,29 @@
     refs[-1][...] = add(*[ref[...] for ref in refs[:-1]])
 
 
-def refresh_kernel(side_ref, mine_ref, other_ref, factor_ref, root_ref, high_ref, low_ref, fresh_ref, refined_ref):
+def refresh_kernel(dp_ref, mine_ref, other_ref, factor_ref, fifth_ref, base_ref, fresh_ref, refined_ref, old, held, sems):
+    load = pltpu.make_async_copy(factor_ref, old, sems.at[0])
+    store = pltpu.make_async_copy(held, fresh_ref, sems.at[1])
+    load.start()
     summed = jnp.concatenate([mine_ref[...], other_ref[...]], axis=0)
 
-    def update(gram):
-        fresh_ref[...] = keep_rate * factor_ref[...] + (1.0 - keep_rate) * gram
+    def update(contract):
+        gram = lax.dot_general(summed, summed, (((contract,), (contract,)), ((), ())), preferred_element_type=jnp.float32)
+        load.wait()
+        held[...] = keep_rate * old[...] + (1.0 - keep_rate) * gram
+        store.start()
+        coupled = dot(fifth_ref[...], gram.astype(jnp.bfloat16))
+        refined_ref[...] = (base_ref[...] - 0.25 * (1.0 - keep_rate) * coupled).astype(jnp.bfloat16)
 
-    @pl.when(side_ref[0] == 0)
+    @pl.when(lax.rem(dp_ref[0], 2) == 0)
     def _():
-        update(lax.dot_general(summed, summed, (((1,), (1,)), ((), ())), preferred_element_type=jnp.float32))
+        update(1)
 
-    @pl.when(side_ref[0] != 0)
+    @pl.when(lax.rem(dp_ref[0], 2) != 0)
     def _():
-        update(lax.dot_general(summed, summed, (((0,), (0,)), ((), ())), preferred_element_type=jnp.float32))
+        update(0)
 
-    high, low = split(fresh_ref[...])
-    coupled = dot(high_ref[...], high) + (dot(high_ref[...], low) + dot(low_ref[...], high))
-    refined_ref[...] = (1.25 * root_ref[...].astype(jnp.float32) - 0.25 * coupled).astype(jnp.bfloat16)
+    store.wait()
 
 
 def cost(flops, moved):
@@ -73,7 +86,6 @@
     blocks = grad_parts[0, 0]
     ring = blocks.shape[0]
     dp = lax.axis_index("dp")
-    x, side = dp // 2, dp % 2
 
     def swapped(value):
         return lax.ppermute(value, "dp", [(i, i ^ 1) for i in range(replicas)])
@@ -91,10 +103,12 @@
 
     def my_half(step):
         def index(i, place):
-            return (place[0] + (1 - 2 * place[1]) * step + ring) % ring, place[1], 0
+            core = lax.rem(place[0], 2)
+            return lax.rem(lax.div(place[0], 2) + (1 - 2 * core) * step + ring, ring), core, 0
 
         return pl.BlockSpec((1, half, size), index)
 
+    held = pltpu.with_memory_space_constraint(blocks, pltpu.HBM)
     specs = [my_half(step) for step in range(ring)]
     sums = pl.pallas_call(
         chip_kernel,
@@ -107,8 +121,8 @@
         ),
         compiler_params=PARAMS,
         cost_estimate=cost(0, 1),
-    )(jnp.stack([x, side]), *[blocks] * ring, *[theirs] * ring)
-    received = [around(sums[step], step) for step in range(1, ring)]
+    )(dp.reshape(1), *[held] * ring, *[theirs] * ring)
+    received = [around(sums[step], step) for step in (2, 1, 3)]
     mine = pl.pallas_call(
         finish_kernel,
         out_shape=part,
@@ -120,22 +134,26 @@
     other = swapped(mine)
 
     flops = 2 * size**3
-    high, low = pl.pallas_call(
-        fifth_kernel,
-        out_shape=(matrix, matrix),
-        in_specs=[VMEM],
+    old_factor = pltpu.with_memory_space_constraint(factors[0, 0], pltpu.HBM)
+    whole = jax.ShapeDtypeStruct((size, size), jnp.float32)
+    fifth, base = pl.pallas_call(
+        base_kernel,
+        out_shape=(matrix, whole),
+        in_specs=[VMEM, HBM],
         out_specs=(VMEM, VMEM),
+        scratch_shapes=[pltpu.VMEM((size, size), jnp.float32), pltpu.SemaphoreType.DMA],
         compiler_params=PARAMS,
-        cost_estimate=cost(6 * flops, 6 * size**2),
-    )(initial)
+        cost_estimate=cost(9 * flops, 12 * size**2),
+    )(initial, old_factor)
     fresh, refined = pl.pallas_call(
         refresh_kernel,
-        out_shape=(jax.ShapeDtypeStruct((size, size), jnp.float32), matrix),
-        in_specs=[SMEM] + [VMEM] * 6,
-        out_specs=(VMEM, VMEM),
+        out_shape=(whole, matrix),
+        in_specs=[SMEM, VMEM, VMEM, HBM, VMEM, VMEM],
+        out_specs=(HBM, VMEM),
+        scratch_shapes=[pltpu.VMEM((size, size), jnp.float32)] * 2 + [pltpu.SemaphoreType.DMA((2,))],
         compiler_params=PARAMS,
-        cost_estimate=cost(4 * flops, 22 * size**2),
-    )(side.reshape(1), mine, other, factors[0, 0], initial, high, low)
+        cost_estimate=cost(2 * flops, 16 * size**2),
+    )(dp.reshape(1), mine, other, old_factor, fifth, base)
 
     fresh_roots = lax.all_to_all(refined.reshape(old_pieces.shape), "mp", split_axis=0, concat_axis=0, tiled=True)
     refresh = plan[0] < workers

time: 80.3 us -> 80.7 us (level)
  Pallas kernels: 5.15 us -> 8.22 us
  local copies, waits for them, and re-layouts: 1.61 us -> 0.01 us
  starting transfers between devices: 46.3 us -> 45.1 us
    pallas_call x2, Pallas kernels: 4.23 us -> 6.64 us  [the longest x1 3.7 us: local(): pl.pallas_call(refresh_kernel, out_shape=(whole, matrix), in_specs=[SMEM,...]
    ppermute x2, starting transfers between devices: 5.63 us -> 3.88 us  [swapped(): return lax.ppermute(value, 'dp', [(i, i ^ 1) for i in range(replicas)])]
    unnamed x8 -> x4, local copies, waits for them, and re-layouts: 1.61 us -> 0.01 us
  transfers between devices with their start and end apart: 7 -> 7, of which waited for: 3 -> 3; matrix products, arithmetic and copies ran while one was open for 0% -> 0% of each run, Pallas kernels for 4% -> 6%
where the time goes in v6:
time: 80.7 us; the launch traced here: 80.3 us
  starting transfers between devices  45.1 us (56%)
  waiting for transfers between devices  25.2 us (31%)
  Pallas kernels  8.22 us (10%)
  other arithmetic  0.94 us (1%)
    all_to_all x1, waiting for transfers between devices, local(): lax.all_to_all(refined.reshape(old_pieces.shape), 'mp', split_axis=0, con...  19.9 us
    all_to_all x1, starting transfers between devices, local(): lax.all_to_all(old_pieces, 'mp', split_axis=0, concat_axis=0, tiled=True)  16.6 us
    all_to_all x1, starting transfers between devices, local(): lax.all_to_all(refined.reshape(old_pieces.shape), 'mp', split_axis=0, con...  12.7 us
    ppermute x3, starting transfers between devices, around(): return lax.ppermute(value, 'dp', pairs)  12 us
    ppermute x3, waiting for transfers between devices, around(): return lax.ppermute(value, 'dp', pairs)  5.27 us
    ppermute x2, starting transfers between devices, swapped(): return lax.ppermute(value, 'dp', [(i, i ^ 1) for i in range(replicas)])  3.88 us
    pallas_call x1, Pallas kernels, local(): pl.pallas_call(refresh_kernel, out_shape=(whole, matrix), in_specs=[SMEM,...  3.7 us
    pallas_call x1, Pallas kernels, local(): pl.pallas_call(base_kernel, out_shape=(matrix, whole), in_specs=[VMEM, HB...  2.94 us
  transfers between devices with their start and end apart: 7, of which 3 were waited for; matrix products, arithmetic and copies ran while one was open for 0% of the time, Pallas kernels for 6%

profile of v6, /device:TPU:8, one launch (start us, length us, event | category | flops | bytes accessed | tf_op | source)
XLA Modules:
  0.0 80.3 jit_solution(15210884120453791546)
XLA Ops:
  0.6 1.9 %collective-permute-start = (bf16[4,512,512]{2,1,0:T(8,128)(2,1)}, bf16[4,512,512]{2,1,0:T(8,128)(2,1)S(1)}, u32[]{:S(2)}, u32[]{:S(2)}) collective-permute-start(bf16[4,512,512]{2,1,0:T(8,128)(2,1)} %bitcast.13), channel_id=1, source_target_pairs={{0,64},{64,0},{128,192},{192,128},{256,320},{320,256},{384,448},{4... | collective-permute-start | bytes 6291464 | tf_op jit(solution)/shard_map/ppermute | solution.py:91
  2.6 16.6 %all-to-all-start = ((bf16[64,8,512]{2,1,0:T(8,128)(2,1)}), bf16[64,8,512]{2,1,0:T(8,128)(2,1)S(1)}, u32[]{:S(2)}, u32[]{:S(2)}) async-start(bf16[64,8,512]{2,1,0:T(8,128)(2,1)} %bitcast.18), calls=%async_computation | async-start | bytes 1048576 | tf_op jit(solution)/shard_map/all_to_all | solution.py:99
  19.2 0.0 collective-permute-done.refs_4_.refs_5_.refs_6_.refs_7_
  19.2 1.4 %shard_map.59 = (bf16[256,512]{1,0:T(8,128)(2,1)S(1)}, bf16[256,512]{1,0:T(8,128)(2,1)S(1)}, bf16[256,512]{1,0:T(8,128)(2,1)S(1)}, bf16[256,512]{1,0:T(8,128)(2,1)S(1)}) custom-call(s32[1]{0:T(128)} %bitcast.place_ref.dp_ref, bf16[4,512,512]{2,1,0:T(8,128)(2,1)} %bitcast.14, bf16[4,512,512]{2,1,0:T(8,128)(2,1)} %bitcast.15, bf16[4,512,512]{2,1,0:T(8,128)(2,1)} %bitcast.16, ...), custom_call_target="tpu_custom_call" | custom-call | bytes 1 | tf_op jit(solution)/shard_map/pallas_call | solution.py:113
  20.6 4.9 %collective-permute-start.1 = (bf16[256,512]{1,0:T(8,128)(2,1)S(1)}, bf16[256,512]{1,0:T(8,128)(2,1)S(1)}, u32[]{:S(2)}, u32[]{:S(2)}) collective-permute-start(bf16[256,512]{1,0:T(8,128)(2,1)S(1)} %get-tuple-element.11), channel_id=1, source_target_pairs={{0,256},{64,320},{128,384},{192,448},{256,0},{320,64},{384,128},{4... | collective-permute-start | bytes 786440 | tf_op jit(solution)/shard_map/ppermute | solution.py:95
  25.6 2.5 %collective-permute-start.2 = (bf16[256,512]{1,0:T(8,128)(2,1)S(1)}, bf16[256,512]{1,0:T(8,128)(2,1)S(1)}, u32[]{:S(2)}, u32[]{:S(2)}) collective-permute-start(bf16[256,512]{1,0:T(8,128)(2,1)S(1)} %get-tuple-element.12), channel_id=1, source_target_pairs={{0,128},{64,448},{128,256},{192,64},{256,384},{320,192},{384,0},{4... | collective-permute-start | bytes 786440 | tf_op jit(solution)/shard_map/ppermute | solution.py:95
  28.1 4.6 %collective-permute-start.3 = (bf16[256,512]{1,0:T(8,128)(2,1)S(1)}, bf16[256,512]{1,0:T(8,128)(2,1)S(1)}, u32[]{:S(2)}, u32[]{:S(2)}) collective-permute-start(bf16[256,512]{1,0:T(8,128)(2,1)S(1)} %get-tuple-element.13), channel_id=1, source_target_pairs={{0,384},{64,192},{128,0},{192,320},{256,128},{320,448},{384,256},{... | collective-permute-start | bytes 786440 | tf_op jit(solution)/shard_map/ppermute | solution.py:95
  32.6 0.0 collective-permute-done.1.refs_1_
  32.6 4.2 %collective-permute-done.2.refs_2_ = bf16[256,512]{1,0:T(8,128)(2,1)S(1)} collective-permute-done((bf16[256,512]{1,0:T(8,128)(2,1)S(1)}, bf16[256,512]{1,0:T(8,128)(2,1)S(1)}, u32[]{:S(2)}, u32[]{:S(2)}) %collective-permute-start.2) | collective-permute-done | bytes 262176 | tf_op jit(solution)/shard_map/ppermute | solution.py:95
  36.9 1.0 %collective-permute-done.3.refs_3_ = bf16[256,512]{1,0:T(8,128)(2,1)S(1)} collective-permute-done((bf16[256,512]{1,0:T(8,128)(2,1)S(1)}, bf16[256,512]{1,0:T(8,128)(2,1)S(1)}, u32[]{:S(2)}, u32[]{:S(2)}) %collective-permute-start.3) | collective-permute-done | bytes 262176 | tf_op jit(solution)/shard_map/ppermute | solution.py:95
  37.9 0.1 shard_map.60.mine_ref
  38.0 2.0 %collective-permute-start.4 = (bf16[256,512]{1,0:T(8,128)(2,1)S(1)}, bf16[256,512]{1,0:T(8,128)(2,1)S(1)}, u32[]{:S(2)}, u32[]{:S(2)}) collective-permute-start(bf16[256,512]{1,0:T(8,128)(2,1)S(1)} %shard_map.60.mine_ref), channel_id=1, source_target_pairs={{0,64},{64,0},{128,192},{192,128},{256,320},{320,256},{384,448},{4... | collective-permute-start | bytes 786440 | tf_op jit(solution)/shard_map/ppermute | solution.py:91
  40.0 0.0 all-to-all-done
  40.0 2.9 %shard_map.61 = (bf16[512,512]{1,0:T(8,128)(2,1)S(1)}, f32[512,512]{1,0:T(8,128)S(1)}) custom-call(bf16[512,512]{1,0:T(8,128)(2,1)S(1)} %bitcast.12, f32[512,512]{1,0:T(8,128)} %bitcast.19), custom_call_target="tpu_custom_call" | custom-call | flops 2415919104 | bytes 3145728 | tf_op jit(solution)/shard_map/pallas_call | solution.py:139
  43.0 0.0 collective-permute-done.4.other_ref
  43.0 0.0 copy-start.1
  43.0 0.0 copy-start
  43.0 3.7 %shard_map.62 = (f32[512,512]{1,0:T(8,128)}, bf16[512,512]{1,0:T(8,128)(2,1)}) custom-call(s32[1]{0:T(128)} %bitcast.place_ref.dp_ref, bf16[256,512]{1,0:T(8,128)(2,1)S(1)} %shard_map.60.mine_ref, bf16[256,512]{1,0:T(8,128)(2,1)S(1)} %collective-permute-done.4.other_ref, f32[512,512]{1,0:T(8,128)} %bitcast.20, ...), custom_call_target="tpu_custom_call" | custom-call | flops 536870912 | bytes 4194304 | tf_op jit(solution)/shard_map/pallas_call | solution.py:148
  46.7 12.7 %all-to-all-start.1 = ((bf16[64,8,512]{2,1,0:T(8,128)(2,1)}), bf16[64,8,512]{2,1,0:T(8,128)(2,1)S(1)}, u32[]{:S(2)}, u32[]{:S(2)}) async-start(bf16[64,8,512]{2,1,0:T(8,128)(2,1)} %bitcast.7), calls=%async_computation.1 | async-start | bytes 1048576 | tf_op jit(solution)/shard_map/all_to_all | solution.py:158
  59.4 0.0 copy-done.1
  59.4 19.9 %all-to-all-done.1 = bf16[64,8,512]{2,1,0:T(8,128)(2,1)S(1)} async-done(((bf16[64,8,512]{2,1,0:T(8,128)(2,1)}), bf16[64,8,512]{2,1,0:T(8,128)(2,1)S(1)}, u32[]{:S(2)}, u32[]{:S(2)}) %all-to-all-start.1) | async-done | bytes 524320 | tf_op jit(solution)/shard_map/all_to_all | solution.py:158
  79.4 0.0 copy-done
  79.4 0.9 %select_bitcast_fusion = bf16[64,1,8,512]{3,2,1,0:T(8,128)(2,1)} fusion(bf16[64,8,512]{2,1,0:T(8,128)(2,1)S(1)} %all-to-all-done.1, pred[64]{0:T(512)(128)(4,1)S(1)} %compare_bitcast_fusion, bf16[64,1,8,512]{3,2,1,0:T(8,128)(2,1)S(1)} %copy-done), kind=kLoop, calls=%fused_computation | loop fusion | flops 262144 | bytes 1572928 | tf_op jit(solution)/shard_map/reshape | solution.py:160
  (1 shorter events, 0.0 us)
Async XLA Ops:
  0.6 18.5 %collective-permute-start = (bf16[4,512,512]{2,1,0:T(8,128)(2,1)}, bf16[4,512,512]{2,1,0:T(8,128)(2,1)S(1)}, u32[]{:S(2)}, u32[]{:S(2)}) collective-permute-start(bf16[4,512,512]{2,1,0:T(8,128)(2,1)} %bitcast.13), channel_id=1, source_target_pairs={{0,64},{64,0},{128,192},{192,128},{256,320},{320,256},{384,448},{4... | collective-permute-start | bytes 6291464 | tf_op jit(solution)/shard_map/ppermute | solution.py:91
  2.6 37.5 %all-to-all-start = ((bf16[64,8,512]{2,1,0:T(8,128)(2,1)}), bf16[64,8,512]{2,1,0:T(8,128)(2,1)S(1)}, u32[]{:S(2)}, u32[]{:S(2)}) async-start(bf16[64,8,512]{2,1,0:T(8,128)(2,1)} %bitcast.18), calls=%async_computation | async-start | bytes 1048576 | tf_op jit(solution)/shard_map/all_to_all | solution.py:99
  20.6 12.0 %collective-permute-start.1 = (bf16[256,512]{1,0:T(8,128)(2,1)S(1)}, bf16[256,512]{1,0:T(8,128)(2,1)S(1)}, u32[]{:S(2)}, u32[]{:S(2)}) collective-permute-start(bf16[256,512]{1,0:T(8,128)(2,1)S(1)} %get-tuple-element.11), channel_id=1, source_target_pairs={{0,256},{64,320},{128,384},{192,448},{256,0},{320,64},{384,128},{4... | collective-permute-start | bytes 786440 | tf_op jit(solution)/shard_map/ppermute | solution.py:95
  25.6 11.3 %collective-permute-start.2 = (bf16[256,512]{1,0:T(8,128)(2,1)S(1)}, bf16[256,512]{1,0:T(8,128)(2,1)S(1)}, u32[]{:S(2)}, u32[]{:S(2)}) collective-permute-start(bf16[256,512]{1,0:T(8,128)(2,1)S(1)} %get-tuple-element.12), channel_id=1, source_target_pairs={{0,128},{64,448},{128,256},{192,64},{256,384},{320,192},{384,0},{4... | collective-permute-start | bytes 786440 | tf_op jit(solution)/shard_map/ppermute | solution.py:95
  28.1 9.8 %collective-permute-start.3 = (bf16[256,512]{1,0:T(8,128)(2,1)S(1)}, bf16[256,512]{1,0:T(8,128)(2,1)S(1)}, u32[]{:S(2)}, u32[]{:S(2)}) collective-permute-start(bf16[256,512]{1,0:T(8,128)(2,1)S(1)} %get-tuple-element.13), channel_id=1, source_target_pairs={{0,384},{64,192},{128,0},{192,320},{256,128},{320,448},{384,256},{... | collective-permute-start | bytes 786440 | tf_op jit(solution)/shard_map/ppermute | solution.py:95
  38.0 4.9 %collective-permute-start.4 = (bf16[256,512]{1,0:T(8,128)(2,1)S(1)}, bf16[256,512]{1,0:T(8,128)(2,1)S(1)}, u32[]{:S(2)}, u32[]{:S(2)}) collective-permute-start(bf16[256,512]{1,0:T(8,128)(2,1)S(1)} %shard_map.60.mine_ref), channel_id=1, source_target_pairs={{0,64},{64,0},{128,192},{192,128},{256,320},{320,256},{384,448},{4... | collective-permute-start | bytes 786440 | tf_op jit(solution)/shard_map/ppermute | solution.py:91
  43.0 16.4 %copy-start.1 = (s32[1,64]{1,0:T(1,128)S(1)}, s32[1,64]{1,0:T(1,128)}, u32[]{:S(2)}) copy-start(s32[1,64]{1,0:T(1,128)} %param.7) | copy-start | bytes 772
  43.0 36.4 %copy-start = (bf16[64,1,8,512]{3,2,1,0:T(8,128)(2,1)S(1)}, bf16[64,1,8,512]{3,2,1,0:T(8,128)(2,1)}, u32[]{:S(2)}) copy-start(bf16[64,1,8,512]{3,2,1,0:T(8,128)(2,1)} %param.6) | copy-start | bytes 1572868
  46.7 32.6 %all-to-all-start.1 = ((bf16[64,8,512]{2,1,0:T(8,128)(2,1)}), bf16[64,8,512]{2,1,0:T(8,128)(2,1)S(1)}, u32[]{:S(2)}, u32[]{:S(2)}) async-start(bf16[64,8,512]{2,1,0:T(8,128)(2,1)} %bitcast.7), calls=%async_computation.1 | async-start | bytes 1048576 | tf_op jit(solution)/shard_map/all_to_all | solution.py:158

commit v7 on v6

--- a/solution.py
+++ b/solution.py
@@ -49,17 +49,12 @@
     refs[-1][...] = add(*[ref[...] for ref in refs[:-1]])
 
 
-def refresh_kernel(dp_ref, mine_ref, other_ref, factor_ref, fifth_ref, base_ref, fresh_ref, refined_ref, old, held, sems):
-    load = pltpu.make_async_copy(factor_ref, old, sems.at[0])
-    store = pltpu.make_async_copy(held, fresh_ref, sems.at[1])
-    load.start()
+def refresh_kernel(dp_ref, mine_ref, other_ref, factor_ref, fifth_ref, base_ref, fresh_ref, refined_ref):
     summed = jnp.concatenate([mine_ref[...], other_ref[...]], axis=0)
 
     def update(contract):
         gram = lax.dot_general(summed, summed, (((contract,), (contract,)), ((), ())), preferred_element_type=jnp.float32)
-        load.wait()
-        held[...] = keep_rate * old[...] + (1.0 - keep_rate) * gram
-        store.start()
+        fresh_ref[...] = keep_rate * factor_ref[...] + (1.0 - keep_rate) * gram
         coupled = dot(fifth_ref[...], gram.astype(jnp.bfloat16))
         refined_ref[...] = (base_ref[...] - 0.25 * (1.0 - keep_rate) * coupled).astype(jnp.bfloat16)
 
@@ -70,8 +65,6 @@
     @pl.when(lax.rem(dp_ref[0], 2) != 0)
     def _():
         update(0)
-
-    store.wait()
 
 
 def cost(flops, moved):
@@ -122,17 +115,7 @@
         compiler_params=PARAMS,
         cost_estimate=cost(0, 1),
     )(dp.reshape(1), *[held] * ring, *[theirs] * ring)
-    received = [around(sums[step], step) for step in (2, 1, 3)]
-    mine = pl.pallas_call(
-        finish_kernel,
-        out_shape=part,
-        in_specs=[VMEM] * ring,
-        out_specs=VMEM,
-        compiler_params=PARAMS,
-        cost_estimate=cost(0, 1),
-    )(sums[0], *received)
-    other = swapped(mine)
-
+    received = [around(sums[step], step) for step in range(1, ring)]
     flops = 2 * size**3
     old_factor = pltpu.with_memory_space_constraint(factors[0, 0], pltpu.HBM)
     whole = jax.ShapeDtypeStruct((size, size), jnp.float32)
@@ -145,15 +128,25 @@
         compiler_params=PARAMS,
         cost_estimate=cost(9 * flops, 12 * size**2),
     )(initial, old_factor)
+    fifth, base, *received = lax.optimization_barrier((fifth, base, *received))
+    mine = pl.pallas_call(
+        finish_kernel,
+        out_shape=part,
+        in_specs=[VMEM] * ring,
+        out_specs=VMEM,
+        compiler_params=PARAMS,
+        cost_estimate=cost(0, 1),
+    )(sums[0], *received)
+    other = swapped(mine)
+
     fresh, refined = pl.pallas_call(
         refresh_kernel,
         out_shape=(whole, matrix),
-        in_specs=[SMEM, VMEM, VMEM, HBM, VMEM, VMEM],
-        out_specs=(HBM, VMEM),
-        scratch_shapes=[pltpu.VMEM((size, size), jnp.float32)] * 2 + [pltpu.SemaphoreType.DMA((2,))],
+        in_specs=[SMEM] + [VMEM] * 5,
+        out_specs=(VMEM, VMEM),
         compiler_params=PARAMS,
         cost_estimate=cost(2 * flops, 16 * size**2),
-    )(dp.reshape(1), mine, other, old_factor, fifth, base)
+    )(dp.reshape(1), mine, other, factors[0, 0], fifth, base)
 
     fresh_roots = lax.all_to_all(refined.reshape(old_pieces.shape), "mp", split_axis=0, concat_axis=0, tiled=True)
     refresh = plan[0] < workers

time: 80.7 us -> 79.3 us (0.983)
  starting transfers between devices: 45.1 us -> 42.2 us
  waiting for transfers between devices: 25.2 us -> 27.8 us
  Pallas kernels: 8.22 us -> 7.06 us
    all_to_all x1, waiting for transfers between devices: 0.01 us -> 6.59 us  [local(): lax.all_to_all(old_pieces, 'mp', split_axis=0, concat_axis=0, tiled=True)]
    ppermute x3, waiting for transfers between devices: 5.27 us -> 0.01 us  [around(): return lax.ppermute(value, 'dp', pairs)]
    all_to_all x1, starting transfers between devices: 12.7 us -> 10.3 us  [local(): lax.all_to_all(refined.reshape(old_pieces.shape), 'mp', split_axis=0, con...]
    pallas_call x1, Pallas kernels: 3.7 us -> 2.02 us  [local(): pl.pallas_call(refresh_kernel, out_shape=(whole, matrix), in_specs=[SMEM]...]
    ppermute x2, waiting for transfers between devices: 0.01 us -> 1.5 us  [swapped(): return lax.ppermute(value, 'dp', [(i, i ^ 1) for i in range(replicas)])]
where the time goes in v7:
time: 79.3 us; the launch traced here: 78.8 us
  starting transfers between devices  42.2 us (53%)
  waiting for transfers between devices  27.8 us (35%)
  Pallas kernels  7.06 us (9%)
  other arithmetic  0.94 us (1%)
    all_to_all x1, waiting for transfers between devices, local(): lax.all_to_all(refined.reshape(old_pieces.shape), 'mp', split_axis=0, con...  19.7 us
    all_to_all x1, starting transfers between devices, local(): lax.all_to_all(old_pieces, 'mp', split_axis=0, concat_axis=0, tiled=True)  16.6 us
    ppermute x3, starting transfers between devices, around(): return lax.ppermute(value, 'dp', pairs)  11.4 us
    all_to_all x1, starting transfers between devices, local(): lax.all_to_all(refined.reshape(old_pieces.shape), 'mp', split_axis=0, con...  10.3 us
    all_to_all x1, waiting for transfers between devices, local(): lax.all_to_all(old_pieces, 'mp', split_axis=0, concat_axis=0, tiled=True)  6.59 us
    ppermute x2, starting transfers between devices, swapped(): return lax.ppermute(value, 'dp', [(i, i ^ 1) for i in range(replicas)])  3.97 us
    pallas_call x1, Pallas kernels, local(): pl.pallas_call(base_kernel, out_shape=(matrix, whole), in_specs=[VMEM, HB...  2.93 us
    pallas_call x1, Pallas kernels, local(): pl.pallas_call(refresh_kernel, out_shape=(whole, matrix), in_specs=[SMEM]...  2.02 us
  transfers between devices with their start and end apart: 7, of which 3 were waited for; matrix products, arithmetic and copies ran while one was open for 0% of the time, Pallas kernels for 6%

profile of v7, /device:TPU:8, one launch (start us, length us, event | category | flops | bytes accessed | tf_op | source)
XLA Modules:
  0.0 78.8 jit_solution(13283842707431883292)
XLA Ops:
  0.6 1.9 %collective-permute-start = (bf16[4,512,512]{2,1,0:T(8,128)(2,1)}, bf16[4,512,512]{2,1,0:T(8,128)(2,1)S(1)}, u32[]{:S(2)}, u32[]{:S(2)}) collective-permute-start(bf16[4,512,512]{2,1,0:T(8,128)(2,1)} %bitcast.15), channel_id=1, source_target_pairs={{0,64},{64,0},{128,192},{192,128},{256,320},{320,256},{384,448},{4... | collective-permute-start | bytes 6291464 | tf_op jit(solution)/shard_map/ppermute | solution.py:84
  2.6 16.6 %all-to-all-start = ((bf16[64,8,512]{2,1,0:T(8,128)(2,1)}), bf16[64,8,512]{2,1,0:T(8,128)(2,1)S(1)}, u32[]{:S(2)}, u32[]{:S(2)}) async-start(bf16[64,8,512]{2,1,0:T(8,128)(2,1)} %bitcast.20), calls=%async_computation | async-start | bytes 1048576 | tf_op jit(solution)/shard_map/all_to_all | solution.py:92
  19.2 0.0 collective-permute-done.refs_4_.refs_5_.refs_6_.refs_7_
  19.2 2.0 %shard_map.59 = (bf16[256,512]{1,0:T(8,128)(2,1)S(1)}, bf16[256,512]{1,0:T(8,128)(2,1)}, bf16[256,512]{1,0:T(8,128)(2,1)S(1)}, bf16[256,512]{1,0:T(8,128)(2,1)S(1)}) custom-call(s32[1]{0:T(128)} %bitcast.place_ref.dp_ref, bf16[4,512,512]{2,1,0:T(8,128)(2,1)} %bitcast.16, bf16[4,512,512]{2,1,0:T(8,128)(2,1)} %bitcast.17, bf16[4,512,512]{2,1,0:T(8,128)(2,1)} %bitcast.18, ...), custom_call_target="tpu_custom_call" | custom-call | bytes 1 | tf_op jit(solution)/shard_map/pallas_call | solution.py:106
  21.1 3.4 %collective-permute-start.1 = (bf16[256,512]{1,0:T(8,128)(2,1)}, bf16[256,512]{1,0:T(8,128)(2,1)S(1)}, u32[]{:S(2)}, u32[]{:S(2)}) collective-permute-start(bf16[256,512]{1,0:T(8,128)(2,1)} %get-tuple-element.18), channel_id=1, source_target_pairs={{0,128},{64,448},{128,256},{192,64},{256,384},{320,192},{384,0},{4... | collective-permute-start | bytes 786440 | tf_op jit(solution)/shard_map/ppermute | solution.py:88
  24.5 4.6 %collective-permute-start.2 = (bf16[256,512]{1,0:T(8,128)(2,1)S(1)}, bf16[256,512]{1,0:T(8,128)(2,1)S(1)}, u32[]{:S(2)}, u32[]{:S(2)}) collective-permute-start(bf16[256,512]{1,0:T(8,128)(2,1)S(1)} %get-tuple-element.19), channel_id=1, source_target_pairs={{0,256},{64,320},{128,384},{192,448},{256,0},{320,64},{384,128},{4... | collective-permute-start | bytes 786440 | tf_op jit(solution)/shard_map/ppermute | solution.py:88
  29.2 3.3 %collective-permute-start.3 = (bf16[256,512]{1,0:T(8,128)(2,1)S(1)}, bf16[256,512]{1,0:T(8,128)(2,1)S(1)}, u32[]{:S(2)}, u32[]{:S(2)}) collective-permute-start(bf16[256,512]{1,0:T(8,128)(2,1)S(1)} %get-tuple-element.20), channel_id=1, source_target_pairs={{0,384},{64,192},{128,0},{192,320},{256,128},{320,448},{384,256},{... | collective-permute-start | bytes 786440 | tf_op jit(solution)/shard_map/ppermute | solution.py:88
  32.5 6.6 %all-to-all-done = bf16[64,8,512]{2,1,0:T(8,128)(2,1)S(1)} async-done(((bf16[64,8,512]{2,1,0:T(8,128)(2,1)}), bf16[64,8,512]{2,1,0:T(8,128)(2,1)S(1)}, u32[]{:S(2)}, u32[]{:S(2)}) %all-to-all-start) | async-done | bytes 524320 | tf_op jit(solution)/shard_map/all_to_all | solution.py:92
  39.1 2.9 %shard_map.60 = (bf16[512,512]{1,0:T(8,128)(2,1)S(1)}, f32[512,512]{1,0:T(8,128)S(1)}) custom-call(bf16[512,512]{1,0:T(8,128)(2,1)S(1)} %bitcast.14, f32[512,512]{1,0:T(8,128)} %bitcast.12), custom_call_target="tpu_custom_call" | custom-call | flops 2415919104 | bytes 3145728 | tf_op jit(solution)/shard_map/pallas_call | solution.py:122
  42.1 0.0 collective-permute-done.1.refs_1_
  42.1 0.0 collective-permute-done.2.refs_2_
  42.1 0.0 collective-permute-done.3.refs_3_
  42.1 0.1 shard_map.61.mine_ref
  42.2 0.0 copy-start.2
  42.2 0.0 copy-start.1
  42.3 2.1 %collective-permute-start.4 = (bf16[256,512]{1,0:T(8,128)(2,1)S(1)}, bf16[256,512]{1,0:T(8,128)(2,1)S(1)}, u32[]{:S(2)}, u32[]{:S(2)}) collective-permute-start(bf16[256,512]{1,0:T(8,128)(2,1)S(1)} %shard_map.61.mine_ref), channel_id=1, source_target_pairs={{0,64},{64,0},{128,192},{192,128},{256,320},{320,256},{384,448},{4... | collective-permute-start | bytes 786440 | tf_op jit(solution)/shard_map/ppermute | solution.py:84
  44.3 1.5 %collective-permute-done.4.other_ref = bf16[256,512]{1,0:T(8,128)(2,1)S(1)} collective-permute-done((bf16[256,512]{1,0:T(8,128)(2,1)S(1)}, bf16[256,512]{1,0:T(8,128)(2,1)S(1)}, u32[]{:S(2)}, u32[]{:S(2)}) %collective-permute-start.4) | collective-permute-done | bytes 262176 | tf_op jit(solution)/shard_map/ppermute | solution.py:84
  45.8 0.0 copy-done
  45.8 2.0 %shard_map.62 = (f32[512,512]{1,0:T(8,128)}, bf16[512,512]{1,0:T(8,128)(2,1)}) custom-call(s32[1]{0:T(128)} %bitcast.place_ref.dp_ref, bf16[256,512]{1,0:T(8,128)(2,1)S(1)} %shard_map.61.mine_ref, bf16[256,512]{1,0:T(8,128)(2,1)S(1)} %collective-permute-done.4.other_ref, f32[512,512]{1,0:T(8,128)S(1)} %bitcast.13, ...), custom_call_target="tpu_custom_call" | custom-call | flops 536870912 | bytes 4194304 | tf_op jit(solution)/shard_map/pallas_call | solution.py:142
  47.8 10.3 %all-to-all-start.1 = ((bf16[64,8,512]{2,1,0:T(8,128)(2,1)}), bf16[64,8,512]{2,1,0:T(8,128)(2,1)S(1)}, u32[]{:S(2)}, u32[]{:S(2)}) async-start(bf16[64,8,512]{2,1,0:T(8,128)(2,1)} %bitcast.7), calls=%async_computation.1 | async-start | bytes 1048576 | tf_op jit(solution)/shard_map/all_to_all | solution.py:151
  58.1 0.0 copy-done.2
  58.2 19.7 %all-to-all-done.1 = bf16[64,8,512]{2,1,0:T(8,128)(2,1)S(1)} async-done(((bf16[64,8,512]{2,1,0:T(8,128)(2,1)}), bf16[64,8,512]{2,1,0:T(8,128)(2,1)S(1)}, u32[]{:S(2)}, u32[]{:S(2)}) %all-to-all-start.1) | async-done | bytes 524320 | tf_op jit(solution)/shard_map/all_to_all | solution.py:151
  77.9 0.0 copy-done.1
  77.9 0.9 %select_bitcast_fusion = bf16[64,1,8,512]{3,2,1,0:T(8,128)(2,1)} fusion(bf16[64,8,512]{2,1,0:T(8,128)(2,1)S(1)} %all-to-all-done.1, pred[64]{0:T(512)(128)(4,1)S(1)} %compare_bitcast_fusion, bf16[64,1,8,512]{3,2,1,0:T(8,128)(2,1)S(1)} %copy-done.1), kind=kLoop, calls=%fused_computation | loop fusion | flops 262144 | bytes 1572928 | tf_op jit(solution)/shard_map/reshape | solution.py:153
  (2 shorter events, 0.0 us)
Async XLA Ops:
  0.6 18.5 %collective-permute-start = (bf16[4,512,512]{2,1,0:T(8,128)(2,1)}, bf16[4,512,512]{2,1,0:T(8,128)(2,1)S(1)}, u32[]{:S(2)}, u32[]{:S(2)}) collective-permute-start(bf16[4,512,512]{2,1,0:T(8,128)(2,1)} %bitcast.15), channel_id=1, source_target_pairs={{0,64},{64,0},{128,192},{192,128},{256,320},{320,256},{384,448},{4... | collective-permute-start | bytes 6291464 | tf_op jit(solution)/shard_map/ppermute | solution.py:84
  2.6 36.6 %all-to-all-start = ((bf16[64,8,512]{2,1,0:T(8,128)(2,1)}), bf16[64,8,512]{2,1,0:T(8,128)(2,1)S(1)}, u32[]{:S(2)}, u32[]{:S(2)}) async-start(bf16[64,8,512]{2,1,0:T(8,128)(2,1)} %bitcast.20), calls=%async_computation | async-start | bytes 1048576 | tf_op jit(solution)/shard_map/all_to_all | solution.py:92
  21.1 20.9 %collective-permute-start.1 = (bf16[256,512]{1,0:T(8,128)(2,1)}, bf16[256,512]{1,0:T(8,128)(2,1)S(1)}, u32[]{:S(2)}, u32[]{:S(2)}) collective-permute-start(bf16[256,512]{1,0:T(8,128)(2,1)} %get-tuple-element.18), channel_id=1, source_target_pairs={{0,128},{64,448},{128,256},{192,64},{256,384},{320,192},{384,0},{4... | collective-permute-start | bytes 786440 | tf_op jit(solution)/shard_map/ppermute | solution.py:88
  24.5 17.5 %collective-permute-start.2 = (bf16[256,512]{1,0:T(8,128)(2,1)S(1)}, bf16[256,512]{1,0:T(8,128)(2,1)S(1)}, u32[]{:S(2)}, u32[]{:S(2)}) collective-permute-start(bf16[256,512]{1,0:T(8,128)(2,1)S(1)} %get-tuple-element.19), channel_id=1, source_target_pairs={{0,256},{64,320},{128,384},{192,448},{256,0},{320,64},{384,128},{4... | collective-permute-start | bytes 786440 | tf_op jit(solution)/shard_map/ppermute | solution.py:88
  29.2 12.9 %collective-permute-start.3 = (bf16[256,512]{1,0:T(8,128)(2,1)S(1)}, bf16[256,512]{1,0:T(8,128)(2,1)S(1)}, u32[]{:S(2)}, u32[]{:S(2)}) collective-permute-start(bf16[256,512]{1,0:T(8,128)(2,1)S(1)} %get-tuple-element.20), channel_id=1, source_target_pairs={{0,384},{64,192},{128,0},{192,320},{256,128},{320,448},{384,256},{... | collective-permute-start | bytes 786440 | tf_op jit(solution)/shard_map/ppermute | solution.py:88
  39.1 6.7 %copy-start = (f32[1,1,512,512]{3,2,1,0:T(8,128)S(1)}, f32[1,1,512,512]{3,2,1,0:T(8,128)}, u32[]{:S(2)}) copy-start(f32[1,1,512,512]{3,2,1,0:T(8,128)} %param.5) | copy-start | bytes 3145732
  42.2 15.9 %copy-start.2 = (s32[1,64]{1,0:T(1,128)S(1)}, s32[1,64]{1,0:T(1,128)}, u32[]{:S(2)}) copy-start(s32[1,64]{1,0:T(1,128)} %param.7) | copy-start | bytes 772
  42.2 35.7 %copy-start.1 = (bf16[64,1,8,512]{3,2,1,0:T(8,128)(2,1)S(1)}, bf16[64,1,8,512]{3,2,1,0:T(8,128)(2,1)}, u32[]{:S(2)}) copy-start(bf16[64,1,8,512]{3,2,1,0:T(8,128)(2,1)} %param.6) | copy-start | bytes 1572868
  42.3 3.6 %collective-permute-start.4 = (bf16[256,512]{1,0:T(8,128)(2,1)S(1)}, bf16[256,512]{1,0:T(8,128)(2,1)S(1)}, u32[]{:S(2)}, u32[]{:S(2)}) collective-permute-start(bf16[256,512]{1,0:T(8,128)(2,1)S(1)} %shard_map.61.mine_ref), channel_id=1, source_target_pairs={{0,64},{64,0},{128,192},{192,128},{256,320},{320,256},{384,448},{4... | collective-permute-start | bytes 786440 | tf_op jit(solution)/shard_map/ppermute | solution.py:84
  47.8 30.1 %all-to-all-start.1 = ((bf16[64,8,512]{2,1,0:T(8,128)(2,1)}), bf16[64,8,512]{2,1,0:T(8,128)(2,1)S(1)}, u32[]{:S(2)}, u32[]{:S(2)}) async-start(bf16[64,8,512]{2,1,0:T(8,128)(2,1)} %bitcast.7), calls=%async_computation.1 | async-start | bytes 1048576 | tf_op jit(solution)/shard_map/all_to_all | solution.py:151

commit v8 on v7

--- a/solution.py
+++ b/solution.py
@@ -49,12 +49,12 @@
     refs[-1][...] = add(*[ref[...] for ref in refs[:-1]])
 
 
-def refresh_kernel(dp_ref, mine_ref, other_ref, factor_ref, fifth_ref, base_ref, fresh_ref, refined_ref):
+def refine_kernel(dp_ref, mine_ref, other_ref, fifth_ref, base_ref, gram_ref, refined_ref):
     summed = jnp.concatenate([mine_ref[...], other_ref[...]], axis=0)
 
     def update(contract):
         gram = lax.dot_general(summed, summed, (((contract,), (contract,)), ((), ())), preferred_element_type=jnp.float32)
-        fresh_ref[...] = keep_rate * factor_ref[...] + (1.0 - keep_rate) * gram
+        gram_ref[...] = gram
         coupled = dot(fifth_ref[...], gram.astype(jnp.bfloat16))
         refined_ref[...] = (base_ref[...] - 0.25 * (1.0 - keep_rate) * coupled).astype(jnp.bfloat16)
 
@@ -65,6 +65,10 @@
     @pl.when(lax.rem(dp_ref[0], 2) != 0)
     def _():
         update(0)
+
+
+def factor_kernel(factor_ref, gram_ref, fresh_ref):
+    fresh_ref[...] = keep_rate * factor_ref[...] + (1.0 - keep_rate) * gram_ref[...]
 
 
 def cost(flops, moved):
@@ -139,16 +143,23 @@
     )(sums[0], *received)
     other = swapped(mine)
 
-    fresh, refined = pl.pallas_call(
-        refresh_kernel,
+    gram, refined = pl.pallas_call(
+        refine_kernel,
         out_shape=(whole, matrix),
-        in_specs=[SMEM] + [VMEM] * 5,
+        in_specs=[SMEM] + [VMEM] * 4,
         out_specs=(VMEM, VMEM),
         compiler_params=PARAMS,
         cost_estimate=cost(2 * flops, 16 * size**2),
-    )(dp.reshape(1), mine, other, factors[0, 0], fifth, base)
-
+    )(dp.reshape(1), mine, other, fifth, base)
     fresh_roots = lax.all_to_all(refined.reshape(old_pieces.shape), "mp", split_axis=0, concat_axis=0, tiled=True)
+    fresh = pl.pallas_call(
+        factor_kernel,
+        out_shape=whole,
+        in_specs=[VMEM, VMEM],
+        out_specs=VMEM,
+        compiler_params=PARAMS,
+        cost_estimate=cost(0, 12 * size**2),
+    )(factors[0, 0], gram)
     refresh = plan[0] < workers
     new_roots = jnp.where(refresh[:, None, None], fresh_roots, old_pieces).reshape(root_prev.shape)
     return fresh[None, None], new_roots

time: 79.3 us -> 79 us (level)
  waiting for transfers between devices: 27.8 us -> 26.7 us
    all_to_all x1, waiting for transfers between devices: 19.7 us -> 18.6 us  [local(): lax.all_to_all(refined.reshape(old_pieces.shape), 'mp', split_axis=0, con...]
    pallas_call x1 -> x2, Pallas kernels: 2.02 us -> 2.76 us  [the longest x1 1.63 us: local(): pl.pallas_call(refine_kernel, out_shape=(whole, matrix), in_specs=[SMEM]...]
  transfers between devices with their start and end apart: 7 -> 7, of which waited for: 3 -> 3; matrix products, arithmetic and copies ran while one was open for 0% -> 0% of each run, Pallas kernels for 6% -> 8%
where the time goes in v8:
time: 79 us; the launch traced here: 78.6 us
  starting transfers between devices  42.4 us (54%)
  waiting for transfers between devices  26.7 us (34%)
  Pallas kernels  7.79 us (10%)
  other arithmetic  0.94 us (1%)
    all_to_all x1, waiting for transfers between devices, local(): lax.all_to_all(refined.reshape(old_pieces.shape), 'mp', split_axis=0, con...  18.6 us
    all_to_all x1, starting transfers between devices, local(): lax.all_to_all(old_pieces, 'mp', split_axis=0, concat_axis=0, tiled=True)  16.6 us
    ppermute x3, starting transfers between devices, around(): return lax.ppermute(value, 'dp', pairs)  11.4 us
    all_to_all x1, starting transfers between devices, local(): lax.all_to_all(refined.reshape(old_pieces.shape), 'mp', split_axis=0, con...  10.4 us
    all_to_all x1, waiting for transfers between devices, local(): lax.all_to_all(old_pieces, 'mp', split_axis=0, concat_axis=0, tiled=True)  6.59 us
    ppermute x2, starting transfers between devices, swapped(): return lax.ppermute(value, 'dp', [(i, i ^ 1) for i in range(replicas)])  3.97 us
    pallas_call x1, Pallas kernels, local(): pl.pallas_call(base_kernel, out_shape=(matrix, whole), in_specs=[VMEM, HB...  2.93 us
    pallas_call x1, Pallas kernels, local(): pl.pallas_call(chip_kernel, out_shape=(part,) * ring, grid_spec=pltpu.Pre...  1.97 us
  transfers between devices with their start and end apart: 7, of which 3 were waited for; matrix products, arithmetic and copies ran while one was open for 0% of the time, Pallas kernels for 8%

profile of v8, /device:TPU:8, one launch (start us, length us, event | category | flops | bytes accessed | tf_op | source)
XLA Modules:
  0.0 78.6 jit_solution(14724340856919166123)
XLA Ops:
  0.6 1.9 %collective-permute-start = (bf16[4,512,512]{2,1,0:T(8,128)(2,1)}, bf16[4,512,512]{2,1,0:T(8,128)(2,1)S(1)}, u32[]{:S(2)}, u32[]{:S(2)}) collective-permute-start(bf16[4,512,512]{2,1,0:T(8,128)(2,1)} %bitcast.15), channel_id=1, source_target_pairs={{0,64},{64,0},{128,192},{192,128},{256,320},{320,256},{384,448},{4... | collective-permute-start | bytes 6291464 | tf_op jit(solution)/shard_map/ppermute | solution.py:88
  2.6 16.6 %all-to-all-start = ((bf16[64,8,512]{2,1,0:T(8,128)(2,1)}), bf16[64,8,512]{2,1,0:T(8,128)(2,1)S(1)}, u32[]{:S(2)}, u32[]{:S(2)}) async-start(bf16[64,8,512]{2,1,0:T(8,128)(2,1)} %bitcast.20), calls=%async_computation | async-start | bytes 1048576 | tf_op jit(solution)/shard_map/all_to_all | solution.py:96
  19.2 0.0 collective-permute-done.refs_4_.refs_5_.refs_6_.refs_7_
  19.2 2.0 %shard_map.59 = (bf16[256,512]{1,0:T(8,128)(2,1)S(1)}, bf16[256,512]{1,0:T(8,128)(2,1)}, bf16[256,512]{1,0:T(8,128)(2,1)S(1)}, bf16[256,512]{1,0:T(8,128)(2,1)S(1)}) custom-call(s32[1]{0:T(128)} %bitcast.1.place_ref.dp_ref, bf16[4,512,512]{2,1,0:T(8,128)(2,1)} %bitcast.16, bf16[4,512,512]{2,1,0:T(8,128)(2,1)} %bitcast.17, bf16[4,512,512]{2,1,0:T(8,128)(2,1)} %bitcast.18, ...), custom_call_target="tpu_custom_call" | custom-call | bytes 1 | tf_op jit(solution)/shard_map/pallas_call | solution.py:110
  21.1 3.4 %collective-permute-start.1 = (bf16[256,512]{1,0:T(8,128)(2,1)}, bf16[256,512]{1,0:T(8,128)(2,1)S(1)}, u32[]{:S(2)}, u32[]{:S(2)}) collective-permute-start(bf16[256,512]{1,0:T(8,128)(2,1)} %get-tuple-element.18), channel_id=1, source_target_pairs={{0,128},{64,448},{128,256},{192,64},{256,384},{320,192},{384,0},{4... | collective-permute-start | bytes 786440 | tf_op jit(solution)/shard_map/ppermute | solution.py:92
  24.5 4.6 %collective-permute-start.2 = (bf16[256,512]{1,0:T(8,128)(2,1)S(1)}, bf16[256,512]{1,0:T(8,128)(2,1)S(1)}, u32[]{:S(2)}, u32[]{:S(2)}) collective-permute-start(bf16[256,512]{1,0:T(8,128)(2,1)S(1)} %get-tuple-element.19), channel_id=1, source_target_pairs={{0,256},{64,320},{128,384},{192,448},{256,0},{320,64},{384,128},{4... | collective-permute-start | bytes 786440 | tf_op jit(solution)/shard_map/ppermute | solution.py:92
  29.2 3.3 %collective-permute-start.3 = (bf16[256,512]{1,0:T(8,128)(2,1)S(1)}, bf16[256,512]{1,0:T(8,128)(2,1)S(1)}, u32[]{:S(2)}, u32[]{:S(2)}) collective-permute-start(bf16[256,512]{1,0:T(8,128)(2,1)S(1)} %get-tuple-element.20), channel_id=1, source_target_pairs={{0,384},{64,192},{128,0},{192,320},{256,128},{320,448},{384,256},{... | collective-permute-start | bytes 786440 | tf_op jit(solution)/shard_map/ppermute | solution.py:92
  32.5 6.6 %all-to-all-done = bf16[64,8,512]{2,1,0:T(8,128)(2,1)S(1)} async-done(((bf16[64,8,512]{2,1,0:T(8,128)(2,1)}), bf16[64,8,512]{2,1,0:T(8,128)(2,1)S(1)}, u32[]{:S(2)}, u32[]{:S(2)}) %all-to-all-start) | async-done | bytes 524320 | tf_op jit(solution)/shard_map/all_to_all | solution.py:96
  39.1 2.9 %shard_map.60 = (bf16[512,512]{1,0:T(8,128)(2,1)S(1)}, f32[512,512]{1,0:T(8,128)S(1)}) custom-call(bf16[512,512]{1,0:T(8,128)(2,1)S(1)} %bitcast.14, f32[512,512]{1,0:T(8,128)} %bitcast.12), custom_call_target="tpu_custom_call" | custom-call | flops 2415919104 | bytes 3145728 | tf_op jit(solution)/shard_map/pallas_call | solution.py:126
  42.1 0.0 collective-permute-done.1.refs_1_
  42.1 0.0 collective-permute-done.2.refs_2_
  42.1 0.0 collective-permute-done.3.refs_3_
  42.1 0.0 copy-start.2
  42.1 0.0 copy-start
  42.1 0.1 shard_map.61.mine_ref
  42.3 2.1 %collective-permute-start.4 = (bf16[256,512]{1,0:T(8,128)(2,1)S(1)}, bf16[256,512]{1,0:T(8,128)(2,1)S(1)}, u32[]{:S(2)}, u32[]{:S(2)}) collective-permute-start(bf16[256,512]{1,0:T(8,128)(2,1)S(1)} %shard_map.61.mine_ref), channel_id=1, source_target_pairs={{0,64},{64,0},{128,192},{192,128},{256,320},{320,256},{384,448},{4... | collective-permute-start | bytes 786440 | tf_op jit(solution)/shard_map/ppermute | solution.py:88
  44.3 1.5 %collective-permute-done.4.other_ref = bf16[256,512]{1,0:T(8,128)(2,1)S(1)} collective-permute-done((bf16[256,512]{1,0:T(8,128)(2,1)S(1)}, bf16[256,512]{1,0:T(8,128)(2,1)S(1)}, u32[]{:S(2)}, u32[]{:S(2)}) %collective-permute-start.4) | collective-permute-done | bytes 262176 | tf_op jit(solution)/shard_map/ppermute | solution.py:88
  45.8 1.6 %shard_map.62 = (f32[512,512]{1,0:T(8,128)S(1)}, bf16[512,512]{1,0:T(8,128)(2,1)}) custom-call(s32[1]{0:T(128)} %bitcast.1.place_ref.dp_ref, bf16[256,512]{1,0:T(8,128)(2,1)S(1)} %shard_map.61.mine_ref, bf16[256,512]{1,0:T(8,128)(2,1)S(1)} %collective-permute-done.4.other_ref, bf16[512,512]{1,0:T(8,128)(2,1)S(1)} %get-tuple-element.24.fifth_ref, ...), custom_call_target="tpu_custom_call" | custom-call | flops 536870912 | bytes 4194304 | tf_op jit(solution)/shard_map/pallas_call | solution.py:146
  47.4 10.4 %all-to-all-start.1 = ((bf16[64,8,512]{2,1,0:T(8,128)(2,1)}), bf16[64,8,512]{2,1,0:T(8,128)(2,1)S(1)}, u32[]{:S(2)}, u32[]{:S(2)}) async-start(bf16[64,8,512]{2,1,0:T(8,128)(2,1)} %bitcast.7), calls=%async_computation.1 | async-start | bytes 1048576 | tf_op jit(solution)/shard_map/all_to_all | solution.py:154
  57.9 0.0 copy-done.2
  57.9 0.0 copy-done
  57.9 1.1 %shard_map.63 = f32[512,512]{1,0:T(8,128)} custom-call(f32[512,512]{1,0:T(8,128)S(1)} %bitcast.13, f32[512,512]{1,0:T(8,128)S(1)} %get-tuple-element.26.gram_ref), custom_call_target="tpu_custom_call" | custom-call | bytes 3145728 | tf_op jit(solution)/shard_map/pallas_call | solution.py:155
  59.0 18.6 %all-to-all-done.1 = bf16[64,8,512]{2,1,0:T(8,128)(2,1)S(1)} async-done(((bf16[64,8,512]{2,1,0:T(8,128)(2,1)}), bf16[64,8,512]{2,1,0:T(8,128)(2,1)S(1)}, u32[]{:S(2)}, u32[]{:S(2)}) %all-to-all-start.1) | async-done | bytes 524320 | tf_op jit(solution)/shard_map/all_to_all | solution.py:154
  77.6 0.9 %select_bitcast_fusion = bf16[64,1,8,512]{3,2,1,0:T(8,128)(2,1)} fusion(bf16[64,8,512]{2,1,0:T(8,128)(2,1)S(1)} %all-to-all-done.1, pred[64]{0:T(512)(128)(4,1)S(1)} %compare_bitcast_fusion, bf16[64,1,8,512]{3,2,1,0:T(8,128)(2,1)S(1)} %copy-done.1), kind=kLoop, calls=%fused_computation | loop fusion | flops 262144 | bytes 1572928 | tf_op jit(solution)/shard_map/reshape | solution.py:164
  (3 shorter events, 0.0 us)
Async XLA Ops:
  0.6 18.5 %collective-permute-start = (bf16[4,512,512]{2,1,0:T(8,128)(2,1)}, bf16[4,512,512]{2,1,0:T(8,128)(2,1)S(1)}, u32[]{:S(2)}, u32[]{:S(2)}) collective-permute-start(bf16[4,512,512]{2,1,0:T(8,128)(2,1)} %bitcast.15), channel_id=1, source_target_pairs={{0,64},{64,0},{128,192},{192,128},{256,320},{320,256},{384,448},{4... | collective-permute-start | bytes 6291464 | tf_op jit(solution)/shard_map/ppermute | solution.py:88
  2.6 36.6 %all-to-all-start = ((bf16[64,8,512]{2,1,0:T(8,128)(2,1)}), bf16[64,8,512]{2,1,0:T(8,128)(2,1)S(1)}, u32[]{:S(2)}, u32[]{:S(2)}) async-start(bf16[64,8,512]{2,1,0:T(8,128)(2,1)} %bitcast.20), calls=%async_computation | async-start | bytes 1048576 | tf_op jit(solution)/shard_map/all_to_all | solution.py:96
  21.1 20.9 %collective-permute-start.1 = (bf16[256,512]{1,0:T(8,128)(2,1)}, bf16[256,512]{1,0:T(8,128)(2,1)S(1)}, u32[]{:S(2)}, u32[]{:S(2)}) collective-permute-start(bf16[256,512]{1,0:T(8,128)(2,1)} %get-tuple-element.18), channel_id=1, source_target_pairs={{0,128},{64,448},{128,256},{192,64},{256,384},{320,192},{384,0},{4... | collective-permute-start | bytes 786440 | tf_op jit(solution)/shard_map/ppermute | solution.py:92
  24.5 17.5 %collective-permute-start.2 = (bf16[256,512]{1,0:T(8,128)(2,1)S(1)}, bf16[256,512]{1,0:T(8,128)(2,1)S(1)}, u32[]{:S(2)}, u32[]{:S(2)}) collective-permute-start(bf16[256,512]{1,0:T(8,128)(2,1)S(1)} %get-tuple-element.19), channel_id=1, source_target_pairs={{0,256},{64,320},{128,384},{192,448},{256,0},{320,64},{384,128},{4... | collective-permute-start | bytes 786440 | tf_op jit(solution)/shard_map/ppermute | solution.py:92
  29.2 12.9 %collective-permute-start.3 = (bf16[256,512]{1,0:T(8,128)(2,1)S(1)}, bf16[256,512]{1,0:T(8,128)(2,1)S(1)}, u32[]{:S(2)}, u32[]{:S(2)}) collective-permute-start(bf16[256,512]{1,0:T(8,128)(2,1)S(1)} %get-tuple-element.20), channel_id=1, source_target_pairs={{0,384},{64,192},{128,0},{192,320},{256,128},{320,448},{384,256},{... | collective-permute-start | bytes 786440 | tf_op jit(solution)/shard_map/ppermute | solution.py:92
  42.1 15.8 %copy-start.2 = (s32[1,64]{1,0:T(1,128)S(1)}, s32[1,64]{1,0:T(1,128)}, u32[]{:S(2)}) copy-start(s32[1,64]{1,0:T(1,128)} %param.7) | copy-start | bytes 772
  42.1 15.8 %copy-start = (f32[1,1,512,512]{3,2,1,0:T(8,128)S(1)}, f32[1,1,512,512]{3,2,1,0:T(8,128)}, u32[]{:S(2)}) copy-start(f32[1,1,512,512]{3,2,1,0:T(8,128)} %param.5) | copy-start | bytes 3145732
  42.3 3.6 %collective-permute-start.4 = (bf16[256,512]{1,0:T(8,128)(2,1)S(1)}, bf16[256,512]{1,0:T(8,128)(2,1)S(1)}, u32[]{:S(2)}, u32[]{:S(2)}) collective-permute-start(bf16[256,512]{1,0:T(8,128)(2,1)S(1)} %shard_map.61.mine_ref), channel_id=1, source_target_pairs={{0,64},{64,0},{128,192},{192,128},{256,320},{320,256},{384,448},{4... | collective-permute-start | bytes 786440 | tf_op jit(solution)/shard_map/ppermute | solution.py:88
  47.4 30.2 %copy-start.1 = (bf16[64,1,8,512]{3,2,1,0:T(8,128)(2,1)S(1)}, bf16[64,1,8,512]{3,2,1,0:T(8,128)(2,1)}, u32[]{:S(2)}) copy-start(bf16[64,1,8,512]{3,2,1,0:T(8,128)(2,1)} %param.6) | copy-start | bytes 1572868
  47.4 30.2 %all-to-all-start.1 = ((bf16[64,8,512]{2,1,0:T(8,128)(2,1)}), bf16[64,8,512]{2,1,0:T(8,128)(2,1)S(1)}, u32[]{:S(2)}, u32[]{:S(2)}) async-start(bf16[64,8,512]{2,1,0:T(8,128)(2,1)} %bitcast.7), calls=%async_computation.1 | async-start | bytes 1048576 | tf_op jit(solution)/shard_map/all_to_all | solution.py:154

commit v9 on v8

--- a/solution.py
+++ b/solution.py
@@ -21,9 +21,11 @@
     return high, (value - high.astype(jnp.float32)).astype(jnp.bfloat16)
 
 
-def base_kernel(root_ref, factor_ref, fifth_ref, base_ref, old, sem):
-    load = pltpu.make_async_copy(factor_ref, old, sem)
+def base_kernel(dp_ref, root_ref, factor_ref, blocks_ref, fifth_ref, base_ref, own_ref, old, sems):
+    load = pltpu.make_async_copy(factor_ref, old, sems.at[0])
+    load_own = pltpu.make_async_copy(blocks_ref.at[lax.div(dp_ref[0], 2)], own_ref, sems.at[1])
     load.start()
+    load_own.start()
     root = root_ref[...]
     high, low = split(dot(root, root))
     high, low = split(dot(high, high) + (dot(high, low) + dot(low, high)))
@@ -33,24 +35,28 @@
     factor, rest = split(old[...])
     coupled = dot(high, factor) + (dot(high, rest) + dot(low, factor))
     base_ref[...] = 1.25 * root.astype(jnp.float32) - 0.25 * keep_rate * coupled
+    load_own.wait()
 
 
 def add(*values):
     return sum(value.astype(jnp.float32) for value in values).astype(jnp.bfloat16)
 
 
-def chip_kernel(place_ref, *refs):
-    ring = len(refs) // 3
-    for k in range(ring):
-        refs[2 * ring + k][...] = add(refs[k][0], refs[ring + k][0])
+def chip_kernel(dp_ref, next_ref, next_other_ref, far_ref, far_other_ref, next_out_ref, far_out_ref):
+    far_out_ref[...] = add(far_ref[0], far_other_ref[0])
+    next_out_ref[...] = add(next_ref[0], next_other_ref[0])
 
 
-def finish_kernel(*refs):
-    refs[-1][...] = add(*[ref[...] for ref in refs[:-1]])
+def finish_kernel(dp_ref, own_ref, next_ref, far_ref, mine_ref):
+    half = far_ref.shape[0]
+    core = lax.rem(dp_ref[0], 2)
+    for i, extra in ((1 - core, ()), (core, (far_ref[...],))):
+        rows = pl.ds(pl.multiple_of(half * i, half), half)
+        mine_ref[rows] = add(own_ref[rows], next_ref[rows], *extra)
 
 
 def refine_kernel(dp_ref, mine_ref, other_ref, fifth_ref, base_ref, gram_ref, refined_ref):
-    summed = jnp.concatenate([mine_ref[...], other_ref[...]], axis=0)
+    summed = add(mine_ref[...], other_ref[...])
 
     def update(contract):
         gram = lax.dot_general(summed, summed, (((contract,), (contract,)), ((), ())), preferred_element_type=jnp.float32)
@@ -97,50 +103,47 @@
 
     matrix = jax.ShapeDtypeStruct((size, size), jnp.bfloat16)
     part = jax.ShapeDtypeStruct((half, size), jnp.bfloat16)
+    held = pltpu.with_memory_space_constraint(blocks, pltpu.HBM)
+    place = dp.reshape(1)
+    full = pl.BlockSpec((size, size), lambda i, place: (0, 0))
+    one = pl.BlockSpec((half, size), lambda i, place: (0, 0))
 
-    def my_half(step):
-        def index(i, place):
-            core = lax.rem(place[0], 2)
-            return lax.rem(lax.div(place[0], 2) + (1 - 2 * core) * step + ring, ring), core, 0
+    def next_chip(i, place):
+        return lax.rem(lax.div(place[0], 2) + 1 + (ring - 2) * lax.rem(place[0], 2), ring), 0, 0
 
-        return pl.BlockSpec((1, half, size), index)
+    ahead = pl.BlockSpec((1, size, size), next_chip)
+    far = pl.BlockSpec(
+        (1, half, size), lambda i, place: (lax.rem(lax.div(place[0], 2) + 2, ring), lax.rem(place[0], 2), 0)
+    )
 
-    held = pltpu.with_memory_space_constraint(blocks, pltpu.HBM)
-    specs = [my_half(step) for step in range(ring)]
-    sums = pl.pallas_call(
-        chip_kernel,
-        out_shape=(part,) * ring,
-        grid_spec=pltpu.PrefetchScalarGridSpec(
-            num_scalar_prefetch=1,
-            grid=(1,),
-            in_specs=specs * 2,
-            out_specs=(pl.BlockSpec((half, size), lambda i, place: (0, 0)),) * ring,
-        ),
-        compiler_params=PARAMS,
-        cost_estimate=cost(0, 1),
-    )(dp.reshape(1), *[held] * ring, *[theirs] * ring)
-    received = [around(sums[step], step) for step in range(1, ring)]
+    def call(kernel, out_shape, in_specs, out_specs, *operands):
+        return pl.pallas_call(
+            kernel,
+            out_shape=out_shape,
+            grid_spec=pltpu.PrefetchScalarGridSpec(
+                num_scalar_prefetch=1, grid=(1,), in_specs=in_specs, out_specs=out_specs
+            ),
+            compiler_params=PARAMS,
+            cost_estimate=cost(0, 1),
+        )(place, *operands)
+
+    specs = [ahead, ahead, far, far]
+    to_next, to_far = call(chip_kernel, (matrix, part), specs, (full, one), held, theirs, held, theirs)
+    received = [around(to_far, 2), around(to_next, 1)]
     flops = 2 * size**3
     old_factor = pltpu.with_memory_space_constraint(factors[0, 0], pltpu.HBM)
     whole = jax.ShapeDtypeStruct((size, size), jnp.float32)
-    fifth, base = pl.pallas_call(
+    fifth, base, own = pl.pallas_call(
         base_kernel,
-        out_shape=(matrix, whole),
-        in_specs=[VMEM, HBM],
-        out_specs=(VMEM, VMEM),
-        scratch_shapes=[pltpu.VMEM((size, size), jnp.float32), pltpu.SemaphoreType.DMA],
+        out_shape=(matrix, whole, matrix),
+        in_specs=[SMEM, VMEM, HBM, HBM],
+        out_specs=(VMEM, VMEM, VMEM),
+        scratch_shapes=[pltpu.VMEM((size, size), jnp.float32), pltpu.SemaphoreType.DMA((2,))],
         compiler_params=PARAMS,
         cost_estimate=cost(9 * flops, 12 * size**2),
-    )(initial, old_factor)
-    fifth, base, *received = lax.optimization_barrier((fifth, base, *received))
-    mine = pl.pallas_call(
-        finish_kernel,
-        out_shape=part,
-        in_specs=[VMEM] * ring,
-        out_specs=VMEM,
-        compiler_params=PARAMS,
-        cost_estimate=cost(0, 1),
-    )(sums[0], *received)
+    )(place, initial, old_factor, held)
+    fifth, base, own, *received = lax.optimization_barrier((fifth, base, own, *received))
+    mine = call(finish_kernel, matrix, [full, full, one], full, own, received[1], received[0])
     other = swapped(mine)
 
     gram, refined = pl.pallas_call(
@@ -150,7 +153,7 @@
         out_specs=(VMEM, VMEM),
         compiler_params=PARAMS,
         cost_estimate=cost(2 * flops, 16 * size**2),
-    )(dp.reshape(1), mine, other, fifth, base)
+    )(place, mine, other, fifth, base)
     fresh_roots = lax.all_to_all(refined.reshape(old_pieces.shape), "mp", split_axis=0, concat_axis=0, tiled=True)
     fresh = pl.pallas_call(
         factor_kernel,

time: 79 us -> 79 us (level)
  waiting for transfers between devices: 26.7 us -> 30.8 us
  starting transfers between devices: 42.4 us -> 38.7 us
    all_to_all x1, waiting for transfers between devices: 6.59 us -> 10.6 us  [local(): lax.all_to_all(old_pieces, 'mp', split_axis=0, concat_axis=0, tiled=True)]
    ppermute x3 -> x2, starting transfers between devices: 11.4 us -> 8.04 us  [around(): return lax.ppermute(value, 'dp', pairs)]
  transfers between devices with their start and end apart: 7 -> 6, of which waited for: 3 -> 3; matrix products, arithmetic and copies ran while one was open for 0% -> 0% of each run, Pallas kernels for 8% -> 7%
where the time goes in v9:
time: 79 us; the launch traced here: 78.6 us
  starting transfers between devices  38.7 us (49%)
  waiting for transfers between devices  30.8 us (39%)
  Pallas kernels  7.37 us (9%)
  other arithmetic  0.94 us (1%)
    all_to_all x1, waiting for transfers between devices, local(): lax.all_to_all(refined.reshape(old_pieces.shape), 'mp', split_axis=0, con...  18.3 us
    all_to_all x1, starting transfers between devices, local(): lax.all_to_all(old_pieces, 'mp', split_axis=0, concat_axis=0, tiled=True)  16.6 us
    all_to_all x1, waiting for transfers between devices, local(): lax.all_to_all(old_pieces, 'mp', split_axis=0, concat_axis=0, tiled=True)  10.6 us
    all_to_all x1, starting transfers between devices, local(): lax.all_to_all(refined.reshape(old_pieces.shape), 'mp', split_axis=0, con...  10.1 us
    ppermute x2, starting transfers between devices, around(): return lax.ppermute(value, 'dp', pairs)  8.04 us
    ppermute x2, starting transfers between devices, swapped(): return lax.ppermute(value, 'dp', [(i, i ^ 1) for i in range(replicas)])  3.97 us
    pallas_call x1, Pallas kernels, local(): pl.pallas_call(base_kernel, out_shape=(matrix, whole, matrix), in_specs=[...  2.94 us
    ppermute x2, waiting for transfers between devices, swapped(): return lax.ppermute(value, 'dp', [(i, i ^ 1) for i in range(replicas)])  1.88 us
  transfers between devices with their start and end apart: 6, of which 3 were waited for; matrix products, arithmetic and copies ran while one was open for 0% of the time, Pallas kernels for 7%

profile of v9, /device:TPU:8, one launch (start us, length us, event | category | flops | bytes accessed | tf_op | source)
XLA Modules:
  0.0 78.6 jit_solution(12691980637877441785)
XLA Ops:
  0.6 1.9 %collective-permute-start = (bf16[4,512,512]{2,1,0:T(8,128)(2,1)}, bf16[4,512,512]{2,1,0:T(8,128)(2,1)S(1)}, u32[]{:S(2)}, u32[]{:S(2)}) collective-permute-start(bf16[4,512,512]{2,1,0:T(8,128)(2,1)} %bitcast.15), channel_id=1, source_target_pairs={{0,64},{64,0},{128,192},{192,128},{256,320},{320,256},{384,448},{4... | collective-permute-start | bytes 6291464 | tf_op jit(solution)/shard_map/ppermute | solution.py:94
  2.6 16.6 %all-to-all-start = ((bf16[64,8,512]{2,1,0:T(8,128)(2,1)}), bf16[64,8,512]{2,1,0:T(8,128)(2,1)S(1)}, u32[]{:S(2)}, u32[]{:S(2)}) async-start(bf16[64,8,512]{2,1,0:T(8,128)(2,1)} %bitcast.19), calls=%async_computation | async-start | bytes 1048576 | tf_op jit(solution)/shard_map/all_to_all | solution.py:102
  19.2 0.0 collective-permute-done.next_other_ref.far_other_ref
  19.2 1.3 %shard_map.60 = (bf16[512,512]{1,0:T(8,128)(2,1)S(1)}, bf16[256,512]{1,0:T(8,128)(2,1)S(1)}) custom-call(s32[1]{0:T(128)} %bitcast.1.dp_ref, bf16[4,512,512]{2,1,0:T(8,128)(2,1)} %bitcast.16, bf16[4,512,512]{2,1,0:T(8,128)(2,1)S(1)} %collective-permute-done.next_other_ref.far_other_ref, bf16[4,512,512]{2,1,0:T(8,128)(2,1)} %bitcast.17, ...), custom_call_target="tpu_custom_call" | custom-call | bytes 1 | tf_op jit(solution)/shard_map/pallas_call | solution.py:120
  20.5 3.4 %collective-permute-start.2 = (bf16[512,512]{1,0:T(8,128)(2,1)S(1)}, bf16[512,512]{1,0:T(8,128)(2,1)S(1)}, u32[]{:S(2)}, u32[]{:S(2)}) collective-permute-start(bf16[512,512]{1,0:T(8,128)(2,1)S(1)} %get-tuple-element.18), channel_id=1, source_target_pairs={{0,128},{64,448},{128,256},{192,64},{256,384},{320,192},{384,0},{4... | collective-permute-start | bytes 1572872 | tf_op jit(solution)/shard_map/ppermute | solution.py:98
  23.9 4.6 %collective-permute-start.1 = (bf16[256,512]{1,0:T(8,128)(2,1)S(1)}, bf16[256,512]{1,0:T(8,128)(2,1)S(1)}, u32[]{:S(2)}, u32[]{:S(2)}) collective-permute-start(bf16[256,512]{1,0:T(8,128)(2,1)S(1)} %get-tuple-element.17), channel_id=1, source_target_pairs={{0,256},{64,320},{128,384},{192,448},{256,0},{320,64},{384,128},{4... | collective-permute-start | bytes 786440 | tf_op jit(solution)/shard_map/ppermute | solution.py:98
  28.5 10.6 %all-to-all-done = bf16[64,8,512]{2,1,0:T(8,128)(2,1)S(1)} async-done(((bf16[64,8,512]{2,1,0:T(8,128)(2,1)}), bf16[64,8,512]{2,1,0:T(8,128)(2,1)S(1)}, u32[]{:S(2)}, u32[]{:S(2)}) %all-to-all-start) | async-done | bytes 524320 | tf_op jit(solution)/shard_map/all_to_all | solution.py:102
  39.1 2.9 %shard_map.59 = (bf16[512,512]{1,0:T(8,128)(2,1)S(1)}, f32[512,512]{1,0:T(8,128)S(1)}, bf16[512,512]{1,0:T(8,128)(2,1)S(1)}) custom-call(s32[1]{0:T(128)} %bitcast.1.dp_ref, bf16[512,512]{1,0:T(8,128)(2,1)S(1)} %bitcast.14, f32[512,512]{1,0:T(8,128)} %bitcast.12, bf16[4,512,512]{2,1,0:T(8,128)(2,1)} %bitcast.18), custom_call_target="tpu_custom_call" | custom-call | flops 2415919104 | bytes 3145728 | tf_op jit(solution)/shard_map/pallas_call | solution.py:136
  42.1 0.0 collective-permute-done.1.far_ref
  42.1 0.0 collective-permute-done.2.next_ref
  42.1 0.2 shard_map.61.mine_ref
  42.3 0.0 copy-start.2
  42.3 0.0 copy-start
  42.3 2.1 %collective-permute-start.3 = (bf16[512,512]{1,0:T(8,128)(2,1)S(1)}, bf16[512,512]{1,0:T(8,128)(2,1)S(1)}, u32[]{:S(2)}, u32[]{:S(2)}) collective-permute-start(bf16[512,512]{1,0:T(8,128)(2,1)S(1)} %shard_map.61.mine_ref), channel_id=1, source_target_pairs={{0,64},{64,0},{128,192},{192,128},{256,320},{320,256},{384,448},{4... | collective-permute-start | bytes 1572872 | tf_op jit(solution)/shard_map/ppermute | solution.py:94
  44.4 1.9 %collective-permute-done.3.other_ref = bf16[512,512]{1,0:T(8,128)(2,1)S(1)} collective-permute-done((bf16[512,512]{1,0:T(8,128)(2,1)S(1)}, bf16[512,512]{1,0:T(8,128)(2,1)S(1)}, u32[]{:S(2)}, u32[]{:S(2)}) %collective-permute-start.3) | collective-permute-done | bytes 524320 | tf_op jit(solution)/shard_map/ppermute | solution.py:94
  46.2 1.8 %shard_map.62 = (f32[512,512]{1,0:T(8,128)S(1)}, bf16[512,512]{1,0:T(8,128)(2,1)}) custom-call(s32[1]{0:T(128)} %bitcast.1.dp_ref, bf16[512,512]{1,0:T(8,128)(2,1)S(1)} %shard_map.61.mine_ref, bf16[512,512]{1,0:T(8,128)(2,1)S(1)} %collective-permute-done.3.other_ref, bf16[512,512]{1,0:T(8,128)(2,1)S(1)} %get-tuple-element.22.fifth_ref, ...), custom_call_target="tpu_custom_call" | custom-call | flops 536870912 | bytes 4194304 | tf_op jit(solution)/shard_map/pallas_call | solution.py:149
  48.1 0.0 copy-start.1
  48.1 10.1 %all-to-all-start.1 = ((bf16[64,8,512]{2,1,0:T(8,128)(2,1)}), bf16[64,8,512]{2,1,0:T(8,128)(2,1)S(1)}, u32[]{:S(2)}, u32[]{:S(2)}) async-start(bf16[64,8,512]{2,1,0:T(8,128)(2,1)} %bitcast.7), calls=%async_computation.1 | async-start | bytes 1048576 | tf_op jit(solution)/shard_map/all_to_all | solution.py:157
  58.2 0.0 copy-done.2
  58.2 0.0 copy-done
  58.2 1.1 %shard_map.63 = f32[512,512]{1,0:T(8,128)} custom-call(f32[512,512]{1,0:T(8,128)S(1)} %bitcast.13, f32[512,512]{1,0:T(8,128)S(1)} %get-tuple-element.24.gram_ref), custom_call_target="tpu_custom_call" | custom-call | bytes 3145728 | tf_op jit(solution)/shard_map/pallas_call | solution.py:158
  59.3 18.3 %all-to-all-done.1 = bf16[64,8,512]{2,1,0:T(8,128)(2,1)S(1)} async-done(((bf16[64,8,512]{2,1,0:T(8,128)(2,1)}), bf16[64,8,512]{2,1,0:T(8,128)(2,1)S(1)}, u32[]{:S(2)}, u32[]{:S(2)}) %all-to-all-start.1) | async-done | bytes 524320 | tf_op jit(solution)/shard_map/all_to_all | solution.py:157
  77.7 0.0 copy-done.1
  77.7 0.9 %select_bitcast_fusion = bf16[64,1,8,512]{3,2,1,0:T(8,128)(2,1)} fusion(bf16[64,8,512]{2,1,0:T(8,128)(2,1)S(1)} %all-to-all-done.1, pred[64]{0:T(512)(128)(4,1)S(1)} %compare_bitcast_fusion, bf16[64,1,8,512]{3,2,1,0:T(8,128)(2,1)S(1)} %copy-done.1), kind=kLoop, calls=%fused_computation | loop fusion | flops 262144 | bytes 1572928 | tf_op jit(solution)/shard_map/reshape | solution.py:167
  (1 shorter events, 0.0 us)
Async XLA Ops:
  0.6 18.5 %collective-permute-start = (bf16[4,512,512]{2,1,0:T(8,128)(2,1)}, bf16[4,512,512]{2,1,0:T(8,128)(2,1)S(1)}, u32[]{:S(2)}, u32[]{:S(2)}) collective-permute-start(bf16[4,512,512]{2,1,0:T(8,128)(2,1)} %bitcast.15), channel_id=1, source_target_pairs={{0,64},{64,0},{128,192},{192,128},{256,320},{320,256},{384,448},{4... | collective-permute-start | bytes 6291464 | tf_op jit(solution)/shard_map/ppermute | solution.py:94
  2.6 36.6 %all-to-all-start = ((bf16[64,8,512]{2,1,0:T(8,128)(2,1)}), bf16[64,8,512]{2,1,0:T(8,128)(2,1)S(1)}, u32[]{:S(2)}, u32[]{:S(2)}) async-start(bf16[64,8,512]{2,1,0:T(8,128)(2,1)} %bitcast.19), calls=%async_computation | async-start | bytes 1048576 | tf_op jit(solution)/shard_map/all_to_all | solution.py:102
  20.5 21.6 %collective-permute-start.2 = (bf16[512,512]{1,0:T(8,128)(2,1)S(1)}, bf16[512,512]{1,0:T(8,128)(2,1)S(1)}, u32[]{:S(2)}, u32[]{:S(2)}) collective-permute-start(bf16[512,512]{1,0:T(8,128)(2,1)S(1)} %get-tuple-element.18), channel_id=1, source_target_pairs={{0,128},{64,448},{128,256},{192,64},{256,384},{320,192},{384,0},{4... | collective-permute-start | bytes 1572872 | tf_op jit(solution)/shard_map/ppermute | solution.py:98
  23.9 18.2 %collective-permute-start.1 = (bf16[256,512]{1,0:T(8,128)(2,1)S(1)}, bf16[256,512]{1,0:T(8,128)(2,1)S(1)}, u32[]{:S(2)}, u32[]{:S(2)}) collective-permute-start(bf16[256,512]{1,0:T(8,128)(2,1)S(1)} %get-tuple-element.17), channel_id=1, source_target_pairs={{0,256},{64,320},{128,384},{192,448},{256,0},{320,64},{384,128},{4... | collective-permute-start | bytes 786440 | tf_op jit(solution)/shard_map/ppermute | solution.py:98
  42.3 15.9 %copy-start.2 = (s32[1,64]{1,0:T(1,128)S(1)}, s32[1,64]{1,0:T(1,128)}, u32[]{:S(2)}) copy-start(s32[1,64]{1,0:T(1,128)} %param.7) | copy-start | bytes 772
  42.3 15.9 %copy-start = (f32[1,1,512,512]{3,2,1,0:T(8,128)S(1)}, f32[1,1,512,512]{3,2,1,0:T(8,128)}, u32[]{:S(2)}) copy-start(f32[1,1,512,512]{3,2,1,0:T(8,128)} %param.5) | copy-start | bytes 3145732
  42.3 3.9 %collective-permute-start.3 = (bf16[512,512]{1,0:T(8,128)(2,1)S(1)}, bf16[512,512]{1,0:T(8,128)(2,1)S(1)}, u32[]{:S(2)}, u32[]{:S(2)}) collective-permute-start(bf16[512,512]{1,0:T(8,128)(2,1)S(1)} %shard_map.61.mine_ref), channel_id=1, source_target_pairs={{0,64},{64,0},{128,192},{192,128},{256,320},{320,256},{384,448},{4... | collective-permute-start | bytes 1572872 | tf_op jit(solution)/shard_map/ppermute | solution.py:94
  48.1 29.6 %copy-start.1 = (bf16[64,1,8,512]{3,2,1,0:T(8,128)(2,1)S(1)}, bf16[64,1,8,512]{3,2,1,0:T(8,128)(2,1)}, u32[]{:S(2)}) copy-start(bf16[64,1,8,512]{3,2,1,0:T(8,128)(2,1)} %param.6) | copy-start | bytes 1572868
  48.1 29.6 %all-to-all-start.1 = ((bf16[64,8,512]{2,1,0:T(8,128)(2,1)}), bf16[64,8,512]{2,1,0:T(8,128)(2,1)S(1)}, u32[]{:S(2)}, u32[]{:S(2)}) async-start(bf16[64,8,512]{2,1,0:T(8,128)(2,1)} %bitcast.7), calls=%async_computation.1 | async-start | bytes 1048576 | tf_op jit(solution)/shard_map/all_to_all | solution.py:157

commit v10 on v9

--- a/solution.py
+++ b/solution.py
@@ -21,21 +21,20 @@
     return high, (value - high.astype(jnp.float32)).astype(jnp.bfloat16)
 
 
-def base_kernel(dp_ref, root_ref, factor_ref, blocks_ref, fifth_ref, base_ref, own_ref, old, sems):
-    load = pltpu.make_async_copy(factor_ref, old, sems.at[0])
-    load_own = pltpu.make_async_copy(blocks_ref.at[lax.div(dp_ref[0], 2)], own_ref, sems.at[1])
+def fifth_kernel(dp_ref, root_ref, blocks_ref, high_ref, low_ref, own_ref, sem):
+    load = pltpu.make_async_copy(blocks_ref.at[lax.div(dp_ref[0], 2)], own_ref, sem)
     load.start()
-    load_own.start()
     root = root_ref[...]
     high, low = split(dot(root, root))
     high, low = split(dot(high, high) + (dot(high, low) + dot(low, high)))
-    high, low = split(dot(root, high) + dot(root, low))
-    fifth_ref[...] = high
+    high_ref[...], low_ref[...] = split(dot(root, high) + dot(root, low))
     load.wait()
-    factor, rest = split(old[...])
-    coupled = dot(high, factor) + (dot(high, rest) + dot(low, factor))
-    base_ref[...] = 1.25 * root.astype(jnp.float32) - 0.25 * keep_rate * coupled
-    load_own.wait()
+
+
+def base_kernel(root_ref, factor_ref, high_ref, low_ref, base_ref):
+    factor, rest = split(factor_ref[...])
+    coupled = dot(high_ref[...], factor) + (dot(high_ref[...], rest) + dot(low_ref[...], factor))
+    base_ref[...] = 1.25 * root_ref[...].astype(jnp.float32) - 0.25 * keep_rate * coupled
 
 
 def add(*values):
@@ -131,20 +130,27 @@
     to_next, to_far = call(chip_kernel, (matrix, part), specs, (full, one), held, theirs, held, theirs)
     received = [around(to_far, 2), around(to_next, 1)]
     flops = 2 * size**3
-    old_factor = pltpu.with_memory_space_constraint(factors[0, 0], pltpu.HBM)
     whole = jax.ShapeDtypeStruct((size, size), jnp.float32)
-    fifth, base, own = pl.pallas_call(
-        base_kernel,
-        out_shape=(matrix, whole, matrix),
-        in_specs=[SMEM, VMEM, HBM, HBM],
+    fifth, rest, own = pl.pallas_call(
+        fifth_kernel,
+        out_shape=(matrix, matrix, matrix),
+        in_specs=[SMEM, VMEM, HBM],
         out_specs=(VMEM, VMEM, VMEM),
-        scratch_shapes=[pltpu.VMEM((size, size), jnp.float32), pltpu.SemaphoreType.DMA((2,))],
+        scratch_shapes=[pltpu.SemaphoreType.DMA],
         compiler_params=PARAMS,
-        cost_estimate=cost(9 * flops, 12 * size**2),
-    )(place, initial, old_factor, held)
-    fifth, base, own, *received = lax.optimization_barrier((fifth, base, own, *received))
+        cost_estimate=cost(6 * flops, 8 * size**2),
+    )(place, initial, held)
+    fifth, rest, own, *received = lax.optimization_barrier((fifth, rest, own, *received))
     mine = call(finish_kernel, matrix, [full, full, one], full, own, received[1], received[0])
     other = swapped(mine)
+    base = pl.pallas_call(
+        base_kernel,
+        out_shape=whole,
+        in_specs=[VMEM] * 4,
+        out_specs=VMEM,
+        compiler_params=PARAMS,
+        cost_estimate=cost(3 * flops, 12 * size**2),
+    )(initial, factors[0, 0], fifth, rest)
 
     gram, refined = pl.pallas_call(
         refine_kernel,

time: 79 us -> 78.9 us (level)
  waiting for transfers between devices: 30.8 us -> 29.8 us
  starting transfers between devices: 38.7 us -> 39.5 us
    ppermute x2, waiting for transfers between devices: 1.88 us -> 0.87 us  [swapped(): return lax.ppermute(value, 'dp', [(i, i ^ 1) for i in range(replicas)])]
    all_to_all x1, starting transfers between devices: 10.1 us -> 10.9 us  [local(): lax.all_to_all(refined.reshape(old_pieces.shape), 'mp', split_axis=0, con...]
    pallas_call x1 -> x2, Pallas kernels: 2.94 us -> 2.93 us  [the longest x1 1.95 us: local(): pl.pallas_call(fifth_kernel, out_shape=(matrix, matrix, matrix), in_specs...]
where the time goes in v10:
time: 78.9 us; the launch traced here: 78.5 us
  starting transfers between devices  39.5 us (50%)
  waiting for transfers between devices  29.8 us (38%)
  Pallas kernels  7.36 us (9%)
  other arithmetic  0.94 us (1%)
    all_to_all x1, waiting for transfers between devices, local(): lax.all_to_all(refined.reshape(old_pieces.shape), 'mp', split_axis=0, con...  18.4 us
    all_to_all x1, starting transfers between devices, local(): lax.all_to_all(old_pieces, 'mp', split_axis=0, concat_axis=0, tiled=True)  16.6 us
    all_to_all x1, starting transfers between devices, local(): lax.all_to_all(refined.reshape(old_pieces.shape), 'mp', split_axis=0, con...  10.9 us
    all_to_all x1, waiting for transfers between devices, local(): lax.all_to_all(old_pieces, 'mp', split_axis=0, concat_axis=0, tiled=True)  10.6 us
    ppermute x2, starting transfers between devices, around(): return lax.ppermute(value, 'dp', pairs)  8.04 us
    ppermute x2, starting transfers between devices, swapped(): return lax.ppermute(value, 'dp', [(i, i ^ 1) for i in range(replicas)])  3.97 us
    pallas_call x1, Pallas kernels, local(): pl.pallas_call(fifth_kernel, out_shape=(matrix, matrix, matrix), in_specs...  1.95 us
    pallas_call x1, Pallas kernels, local(): pl.pallas_call(refine_kernel, out_shape=(whole, matrix), in_specs=[SMEM]...  1.83 us
  transfers between devices with their start and end apart: 6, of which 3 were waited for; matrix products, arithmetic and copies ran while one was open for 0% of the time, Pallas kernels for 7%

profile of v10, /device:TPU:8, one launch (start us, length us, event | category | flops | bytes accessed | tf_op | source)
XLA Modules:
  0.0 78.5 jit_solution(9692714383790647686)
XLA Ops:
  0.6 1.9 %collective-permute-start = (bf16[4,512,512]{2,1,0:T(8,128)(2,1)}, bf16[4,512,512]{2,1,0:T(8,128)(2,1)S(1)}, u32[]{:S(2)}, u32[]{:S(2)}) collective-permute-start(bf16[4,512,512]{2,1,0:T(8,128)(2,1)} %bitcast.16), channel_id=1, source_target_pairs={{0,64},{64,0},{128,192},{192,128},{256,320},{320,256},{384,448},{4... | collective-permute-start | bytes 6291464 | tf_op jit(solution)/shard_map/ppermute | solution.py:93
  2.6 16.6 %all-to-all-start = ((bf16[64,8,512]{2,1,0:T(8,128)(2,1)}), bf16[64,8,512]{2,1,0:T(8,128)(2,1)S(1)}, u32[]{:S(2)}, u32[]{:S(2)}) async-start(bf16[64,8,512]{2,1,0:T(8,128)(2,1)} %bitcast.20), calls=%async_computation | async-start | bytes 1048576 | tf_op jit(solution)/shard_map/all_to_all | solution.py:101
  19.2 0.0 collective-permute-done.next_other_ref.far_other_ref
  19.2 1.3 %shard_map.60 = (bf16[512,512]{1,0:T(8,128)(2,1)S(1)}, bf16[256,512]{1,0:T(8,128)(2,1)S(1)}) custom-call(s32[1]{0:T(128)} %bitcast.1.dp_ref, bf16[4,512,512]{2,1,0:T(8,128)(2,1)} %bitcast.17, bf16[4,512,512]{2,1,0:T(8,128)(2,1)S(1)} %collective-permute-done.next_other_ref.far_other_ref, bf16[4,512,512]{2,1,0:T(8,128)(2,1)} %bitcast.18, ...), custom_call_target="tpu_custom_call" | custom-call | bytes 1 | tf_op jit(solution)/shard_map/pallas_call | solution.py:119
  20.5 3.4 %collective-permute-start.2 = (bf16[512,512]{1,0:T(8,128)(2,1)S(1)}, bf16[512,512]{1,0:T(8,128)(2,1)S(1)}, u32[]{:S(2)}, u32[]{:S(2)}) collective-permute-start(bf16[512,512]{1,0:T(8,128)(2,1)S(1)} %get-tuple-element.18), channel_id=1, source_target_pairs={{0,128},{64,448},{128,256},{192,64},{256,384},{320,192},{384,0},{4... | collective-permute-start | bytes 1572872 | tf_op jit(solution)/shard_map/ppermute | solution.py:97
  23.9 4.6 %collective-permute-start.1 = (bf16[256,512]{1,0:T(8,128)(2,1)S(1)}, bf16[256,512]{1,0:T(8,128)(2,1)S(1)}, u32[]{:S(2)}, u32[]{:S(2)}) collective-permute-start(bf16[256,512]{1,0:T(8,128)(2,1)S(1)} %get-tuple-element.17), channel_id=1, source_target_pairs={{0,256},{64,320},{128,384},{192,448},{256,0},{320,64},{384,128},{4... | collective-permute-start | bytes 786440 | tf_op jit(solution)/shard_map/ppermute | solution.py:97
  28.5 10.6 %all-to-all-done = bf16[64,8,512]{2,1,0:T(8,128)(2,1)S(1)} async-done(((bf16[64,8,512]{2,1,0:T(8,128)(2,1)}), bf16[64,8,512]{2,1,0:T(8,128)(2,1)S(1)}, u32[]{:S(2)}, u32[]{:S(2)}) %all-to-all-start) | async-done | bytes 524320 | tf_op jit(solution)/shard_map/all_to_all | solution.py:101
  39.1 2.0 %shard_map.59 = (bf16[512,512]{1,0:T(8,128)(2,1)S(1)}, bf16[512,512]{1,0:T(8,128)(2,1)S(1)}, bf16[512,512]{1,0:T(8,128)(2,1)S(1)}) custom-call(s32[1]{0:T(128)} %bitcast.1.dp_ref, bf16[512,512]{1,0:T(8,128)(2,1)S(1)} %bitcast.14, bf16[4,512,512]{2,1,0:T(8,128)(2,1)} %bitcast.19), custom_call_target="tpu_custom_call" | custom-call | flops 1610612736 | bytes 2097152 | tf_op jit(solution)/shard_map/pallas_call | solution.py:134
  41.1 0.0 copy-start
  41.1 0.0 collective-permute-done.1.far_ref
  41.1 0.0 collective-permute-done.2.next_ref
  41.1 0.2 shard_map.61.mine_ref
  41.3 2.1 %collective-permute-start.3 = (bf16[512,512]{1,0:T(8,128)(2,1)S(1)}, bf16[512,512]{1,0:T(8,128)(2,1)S(1)}, u32[]{:S(2)}, u32[]{:S(2)}) collective-permute-start(bf16[512,512]{1,0:T(8,128)(2,1)S(1)} %shard_map.61.mine_ref), channel_id=1, source_target_pairs={{0,64},{64,0},{128,192},{192,128},{256,320},{320,256},{384,448},{4... | collective-permute-start | bytes 1572872 | tf_op jit(solution)/shard_map/ppermute | solution.py:93
  43.3 0.0 copy-done
  43.4 1.0 %shard_map.62.base_ref = f32[512,512]{1,0:T(8,128)S(1)} custom-call(bf16[512,512]{1,0:T(8,128)(2,1)S(1)} %bitcast.15, f32[512,512]{1,0:T(8,128)S(1)} %bitcast.12, bf16[512,512]{1,0:T(8,128)(2,1)S(1)} %get-tuple-element.22.high_ref.fifth_ref, bf16[512,512]{1,0:T(8,128)(2,1)S(1)} %get-tuple-element.23.low_ref), custom_call_target="tpu_custom_call" | custom-call | flops 805306368 | bytes 3145728 | tf_op jit(solution)/shard_map/pallas_call | solution.py:146
  44.3 0.0 copy-start.2
  44.4 0.9 %collective-permute-done.3.other_ref = bf16[512,512]{1,0:T(8,128)(2,1)S(1)} collective-permute-done((bf16[512,512]{1,0:T(8,128)(2,1)S(1)}, bf16[512,512]{1,0:T(8,128)(2,1)S(1)}, u32[]{:S(2)}, u32[]{:S(2)}) %collective-permute-start.3) | collective-permute-done | bytes 524320 | tf_op jit(solution)/shard_map/ppermute | solution.py:93
  45.2 1.8 %shard_map.63 = (f32[512,512]{1,0:T(8,128)S(1)}, bf16[512,512]{1,0:T(8,128)(2,1)}) custom-call(s32[1]{0:T(128)} %bitcast.1.dp_ref, bf16[512,512]{1,0:T(8,128)(2,1)S(1)} %shard_map.61.mine_ref, bf16[512,512]{1,0:T(8,128)(2,1)S(1)} %collective-permute-done.3.other_ref, bf16[512,512]{1,0:T(8,128)(2,1)S(1)} %get-tuple-element.22.high_ref.fifth_ref, ...), custom_call_target="tpu_custom_call" | custom-call | flops 536870912 | bytes 4194304 | tf_op jit(solution)/shard_map/pallas_call | solution.py:155
  47.1 10.9 %all-to-all-start.1 = ((bf16[64,8,512]{2,1,0:T(8,128)(2,1)}), bf16[64,8,512]{2,1,0:T(8,128)(2,1)S(1)}, u32[]{:S(2)}, u32[]{:S(2)}) async-start(bf16[64,8,512]{2,1,0:T(8,128)(2,1)} %bitcast.7), calls=%async_computation.1 | async-start | bytes 1048576 | tf_op jit(solution)/shard_map/all_to_all | solution.py:163
  58.0 0.0 copy-done.2
  58.0 1.1 %shard_map.64 = f32[512,512]{1,0:T(8,128)} custom-call(f32[512,512]{1,0:T(8,128)S(1)} %bitcast.13, f32[512,512]{1,0:T(8,128)S(1)} %get-tuple-element.24.gram_ref), custom_call_target="tpu_custom_call" | custom-call | bytes 3145728 | tf_op jit(solution)/shard_map/pallas_call | solution.py:164
  59.2 18.4 %all-to-all-done.1 = bf16[64,8,512]{2,1,0:T(8,128)(2,1)S(1)} async-done(((bf16[64,8,512]{2,1,0:T(8,128)(2,1)}), bf16[64,8,512]{2,1,0:T(8,128)(2,1)S(1)}, u32[]{:S(2)}, u32[]{:S(2)}) %all-to-all-start.1) | async-done | bytes 524320 | tf_op jit(solution)/shard_map/all_to_all | solution.py:163
  77.5 0.0 copy-done.1
  77.5 0.9 %select_bitcast_fusion = bf16[64,1,8,512]{3,2,1,0:T(8,128)(2,1)} fusion(bf16[64,8,512]{2,1,0:T(8,128)(2,1)S(1)} %all-to-all-done.1, pred[64]{0:T(512)(128)(4,1)S(1)} %compare_bitcast_fusion, bf16[64,1,8,512]{3,2,1,0:T(8,128)(2,1)S(1)} %copy-done.1), kind=kLoop, calls=%fused_computation | loop fusion | flops 262144 | bytes 1572928 | tf_op jit(solution)/shard_map/reshape | solution.py:173
  (2 shorter events, 0.0 us)
Async XLA Ops:
  0.6 18.5 %collective-permute-start = (bf16[4,512,512]{2,1,0:T(8,128)(2,1)}, bf16[4,512,512]{2,1,0:T(8,128)(2,1)S(1)}, u32[]{:S(2)}, u32[]{:S(2)}) collective-permute-start(bf16[4,512,512]{2,1,0:T(8,128)(2,1)} %bitcast.16), channel_id=1, source_target_pairs={{0,64},{64,0},{128,192},{192,128},{256,320},{320,256},{384,448},{4... | collective-permute-start | bytes 6291464 | tf_op jit(solution)/shard_map/ppermute | solution.py:93
  2.6 36.6 %all-to-all-start = ((bf16[64,8,512]{2,1,0:T(8,128)(2,1)}), bf16[64,8,512]{2,1,0:T(8,128)(2,1)S(1)}, u32[]{:S(2)}, u32[]{:S(2)}) async-start(bf16[64,8,512]{2,1,0:T(8,128)(2,1)} %bitcast.20), calls=%async_computation | async-start | bytes 1048576 | tf_op jit(solution)/shard_map/all_to_all | solution.py:101
  20.5 20.6 %collective-permute-start.2 = (bf16[512,512]{1,0:T(8,128)(2,1)S(1)}, bf16[512,512]{1,0:T(8,128)(2,1)S(1)}, u32[]{:S(2)}, u32[]{:S(2)}) collective-permute-start(bf16[512,512]{1,0:T(8,128)(2,1)S(1)} %get-tuple-element.18), channel_id=1, source_target_pairs={{0,128},{64,448},{128,256},{192,64},{256,384},{320,192},{384,0},{4... | collective-permute-start | bytes 1572872 | tf_op jit(solution)/shard_map/ppermute | solution.py:97
  23.9 17.2 %collective-permute-start.1 = (bf16[256,512]{1,0:T(8,128)(2,1)S(1)}, bf16[256,512]{1,0:T(8,128)(2,1)S(1)}, u32[]{:S(2)}, u32[]{:S(2)}) collective-permute-start(bf16[256,512]{1,0:T(8,128)(2,1)S(1)} %get-tuple-element.17), channel_id=1, source_target_pairs={{0,256},{64,320},{128,384},{192,448},{256,0},{320,64},{384,128},{4... | collective-permute-start | bytes 786440 | tf_op jit(solution)/shard_map/ppermute | solution.py:97
  41.1 2.3 %copy-start = (f32[1,1,512,512]{3,2,1,0:T(8,128)S(1)}, f32[1,1,512,512]{3,2,1,0:T(8,128)}, u32[]{:S(2)}) copy-start(f32[1,1,512,512]{3,2,1,0:T(8,128)} %param.5) | copy-start | bytes 3145732
  41.3 3.9 %collective-permute-start.3 = (bf16[512,512]{1,0:T(8,128)(2,1)S(1)}, bf16[512,512]{1,0:T(8,128)(2,1)S(1)}, u32[]{:S(2)}, u32[]{:S(2)}) collective-permute-start(bf16[512,512]{1,0:T(8,128)(2,1)S(1)} %shard_map.61.mine_ref), channel_id=1, source_target_pairs={{0,64},{64,0},{128,192},{192,128},{256,320},{320,256},{384,448},{4... | collective-permute-start | bytes 1572872 | tf_op jit(solution)/shard_map/ppermute | solution.py:93
  44.3 13.7 %copy-start.2 = (s32[1,64]{1,0:T(1,128)S(1)}, s32[1,64]{1,0:T(1,128)}, u32[]{:S(2)}) copy-start(s32[1,64]{1,0:T(1,128)} %param.7) | copy-start | bytes 772
  47.1 30.5 %copy-start.1 = (bf16[64,1,8,512]{3,2,1,0:T(8,128)(2,1)S(1)}, bf16[64,1,8,512]{3,2,1,0:T(8,128)(2,1)}, u32[]{:S(2)}) copy-start(bf16[64,1,8,512]{3,2,1,0:T(8,128)(2,1)} %param.6) | copy-start | bytes 1572868
  47.1 30.5 %all-to-all-start.1 = ((bf16[64,8,512]{2,1,0:T(8,128)(2,1)}), bf16[64,8,512]{2,1,0:T(8,128)(2,1)S(1)}, u32[]{:S(2)}, u32[]{:S(2)}) async-start(bf16[64,8,512]{2,1,0:T(8,128)(2,1)} %bitcast.7), calls=%async_computation.1 | async-start | bytes 1048576 | tf_op jit(solution)/shard_map/all_to_all | solution.py:163

commit v11 on v10

--- a/solution.py
+++ b/solution.py
@@ -1,3 +1,6 @@
+import functools
+import random
+
 import jax
 import jax.numpy as jnp
 from jax import lax
@@ -10,6 +13,12 @@
 HBM = pl.BlockSpec(memory_space=pltpu.HBM)
 SMEM = pl.BlockSpec(memory_space=pltpu.SMEM)
 PARAMS = pltpu.CompilerParams(vmem_limit_bytes=20 * 1024 * 1024)
+
+
+def sending_order(workers):
+    order = list(range(workers))
+    random.Random(4).shuffle(order)
+    return order
 
 
 def dot(a, b):
@@ -54,14 +63,17 @@
         mine_ref[rows] = add(own_ref[rows], next_ref[rows], *extra)
 
 
-def refine_kernel(dp_ref, mine_ref, other_ref, fifth_ref, base_ref, gram_ref, refined_ref):
+def refine_kernel(order, dp_ref, mine_ref, other_ref, fifth_ref, base_ref, gram_ref, refined_ref):
     summed = add(mine_ref[...], other_ref[...])
 
     def update(contract):
         gram = lax.dot_general(summed, summed, (((contract,), (contract,)), ((), ())), preferred_element_type=jnp.float32)
         gram_ref[...] = gram
         coupled = dot(fifth_ref[...], gram.astype(jnp.bfloat16))
-        refined_ref[...] = (base_ref[...] - 0.25 * (1.0 - keep_rate) * coupled).astype(jnp.bfloat16)
+        refined = base_ref[...] - 0.25 * (1.0 - keep_rate) * coupled
+        rows = refined_ref.shape[1]
+        for at, worker in enumerate(order):
+            refined_ref[at] = refined[worker * rows : (worker + 1) * rows].astype(jnp.bfloat16)
 
     @pl.when(lax.rem(dp_ref[0], 2) == 0)
     def _():
@@ -74,6 +86,12 @@
 
 def factor_kernel(factor_ref, gram_ref, fresh_ref):
     fresh_ref[...] = keep_rate * factor_ref[...] + (1.0 - keep_rate) * gram_ref[...]
+
+
+def select_kernel(order, plan_ref, fresh_ref, old_ref, out_ref):
+    for at, worker in enumerate(order):
+        refresh = plan_ref[worker] < len(order)
+        out_ref[worker] = jnp.where(refresh, fresh_ref[at], old_ref[worker])
 
 
 def cost(flops, moved):
@@ -152,15 +170,18 @@
         cost_estimate=cost(3 * flops, 12 * size**2),
     )(initial, factors[0, 0], fifth, rest)
 
+    order = sending_order(workers)
     gram, refined = pl.pallas_call(
-        refine_kernel,
-        out_shape=(whole, matrix),
+        functools.partial(refine_kernel, order),
+        out_shape=(whole, jax.ShapeDtypeStruct(old_pieces.shape, jnp.bfloat16)),
         in_specs=[SMEM] + [VMEM] * 4,
         out_specs=(VMEM, VMEM),
         compiler_params=PARAMS,
         cost_estimate=cost(2 * flops, 16 * size**2),
     )(place, mine, other, fifth, base)
-    fresh_roots = lax.all_to_all(refined.reshape(old_pieces.shape), "mp", split_axis=0, concat_axis=0, tiled=True)
+    fresh_roots = lax.all_to_all(
+        refined, "mp", split_axis=0, concat_axis=0, tiled=True, axis_index_groups=[order]
+    )
     fresh = pl.pallas_call(
         factor_kernel,
         out_shape=whole,
@@ -169,9 +190,15 @@
         compiler_params=PARAMS,
         cost_estimate=cost(0, 12 * size**2),
     )(factors[0, 0], gram)
-    refresh = plan[0] < workers
-    new_roots = jnp.where(refresh[:, None, None], fresh_roots, old_pieces).reshape(root_prev.shape)
-    return fresh[None, None], new_roots
+    new_roots = pl.pallas_call(
+        functools.partial(select_kernel, order),
+        out_shape=jax.ShapeDtypeStruct(old_pieces.shape, jnp.bfloat16),
+        in_specs=[SMEM, VMEM, VMEM],
+        out_specs=VMEM,
+        compiler_params=PARAMS,
+        cost_estimate=cost(0, 6 * size**2),
+    )(plan[0], fresh_roots, old_pieces)
+    return fresh[None, None], new_roots.reshape(root_prev.shape)
 
 
 def solution(mesh):

time: 78.9 us -> 75.8 us (0.961)
  the two profiles are of different devices: /device:TPU:8 before, /device:TPU:4 now
where the time goes in v11:
time: 75.8 us; the launch traced here: 75.4 us
  starting transfers between devices  39.5 us (52%)
  waiting for transfers between devices  26.3 us (35%)
  Pallas kernels  7.98 us (11%)
  local copies, waits for them, and re-layouts  0.8 us (1%)
  between operations  0.77 us (1%)
    all_to_all x1, starting transfers between devices, local(): lax.all_to_all(old_pieces, 'mp', split_axis=0, concat_axis=0, tiled=True)  16.6 us
    all_to_all x1, waiting for transfers between devices, local(): lax.all_to_all(refined, 'mp', split_axis=0, concat_axis=0, tiled=True, ax...  13.4 us
    all_to_all x1, starting transfers between devices, local(): lax.all_to_all(refined, 'mp', split_axis=0, concat_axis=0, tiled=True, ax...  13.2 us
    all_to_all x1, waiting for transfers between devices, local(): lax.all_to_all(old_pieces, 'mp', split_axis=0, concat_axis=0, tiled=True)  12 us
    ppermute x2, starting transfers between devices, around(): return lax.ppermute(value, 'dp', pairs)  5.81 us
    ppermute x2, starting transfers between devices, swapped(): return lax.ppermute(value, 'dp', [(i, i ^ 1) for i in range(replicas)])  3.97 us
    pallas_call x1, Pallas kernels, local(): pl.pallas_call(fifth_kernel, out_shape=(matrix, matrix, matrix), in_specs...  1.96 us
  transfers between devices with their start and end apart: 6, of which 3 were waited for; matrix products, arithmetic and copies ran while one was open for 0% of the time, Pallas kernels for 7%

profile of v11, /device:TPU:4, one launch (start us, length us, event | category | flops | bytes accessed | tf_op | source)
XLA Modules:
  0.0 75.4 jit_solution(16242626741409309315)
XLA Ops:
  0.6 1.9 %collective-permute-start = (bf16[4,512,512]{2,1,0:T(8,128)(2,1)}, bf16[4,512,512]{2,1,0:T(8,128)(2,1)S(1)}, u32[]{:S(2)}, u32[]{:S(2)}) collective-permute-start(bf16[4,512,512]{2,1,0:T(8,128)(2,1)} %bitcast.17), channel_id=1, source_target_pairs={{0,64},{64,0},{128,192},{192,128},{256,320},{320,256},{384,448},{4... | collective-permute-start | bytes 6291464 | tf_op jit(solution)/shard_map/ppermute | solution.py:111
  2.6 16.6 %all-to-all-start = ((bf16[64,8,512]{2,1,0:T(8,128)(2,1)}), bf16[64,8,512]{2,1,0:T(8,128)(2,1)S(1)}, u32[]{:S(2)}, u32[]{:S(2)}) async-start(bf16[64,8,512]{2,1,0:T(8,128)(2,1)} %bitcast.14), calls=%async_computation | async-start | bytes 1048576 | tf_op jit(solution)/shard_map/all_to_all | solution.py:119
  19.2 0.0 collective-permute-done.next_other_ref.far_other_ref
  19.2 1.3 %shard_map.60 = (bf16[512,512]{1,0:T(8,128)(2,1)S(1)}, bf16[256,512]{1,0:T(8,128)(2,1)S(1)}) custom-call(s32[1]{0:T(128)} %bitcast.1.dp_ref, bf16[4,512,512]{2,1,0:T(8,128)(2,1)} %bitcast.18, bf16[4,512,512]{2,1,0:T(8,128)(2,1)S(1)} %collective-permute-done.next_other_ref.far_other_ref, bf16[4,512,512]{2,1,0:T(8,128)(2,1)} %bitcast.19, ...), custom_call_target="tpu_custom_call" | custom-call | bytes 1 | tf_op jit(solution)/shard_map/pallas_call | solution.py:137
  20.5 3.1 %collective-permute-start.2 = (bf16[512,512]{1,0:T(8,128)(2,1)S(1)}, bf16[512,512]{1,0:T(8,128)(2,1)S(1)}, u32[]{:S(2)}, u32[]{:S(2)}) collective-permute-start(bf16[512,512]{1,0:T(8,128)(2,1)S(1)} %get-tuple-element.18), channel_id=1, source_target_pairs={{0,128},{64,448},{128,256},{192,64},{256,384},{320,192},{384,0},{4... | collective-permute-start | bytes 1572872 | tf_op jit(solution)/shard_map/ppermute | solution.py:115
  23.6 2.7 %collective-permute-start.1 = (bf16[256,512]{1,0:T(8,128)(2,1)S(1)}, bf16[256,512]{1,0:T(8,128)(2,1)S(1)}, u32[]{:S(2)}, u32[]{:S(2)}) collective-permute-start(bf16[256,512]{1,0:T(8,128)(2,1)S(1)} %get-tuple-element.17), channel_id=1, source_target_pairs={{0,256},{64,320},{128,384},{192,448},{256,0},{320,64},{384,128},{4... | collective-permute-start | bytes 786440 | tf_op jit(solution)/shard_map/ppermute | solution.py:115
  26.3 12.0 %all-to-all-done = bf16[64,8,512]{2,1,0:T(8,128)(2,1)S(1)} async-done(((bf16[64,8,512]{2,1,0:T(8,128)(2,1)}), bf16[64,8,512]{2,1,0:T(8,128)(2,1)S(1)}, u32[]{:S(2)}, u32[]{:S(2)}) %all-to-all-start) | async-done | bytes 524320 | tf_op jit(solution)/shard_map/all_to_all | solution.py:119
  38.3 2.0 %shard_map.59 = (bf16[512,512]{1,0:T(8,128)(2,1)S(1)}, bf16[512,512]{1,0:T(8,128)(2,1)S(1)}, bf16[512,512]{1,0:T(8,128)(2,1)S(1)}) custom-call(s32[1]{0:T(128)} %bitcast.1.dp_ref, bf16[512,512]{1,0:T(8,128)(2,1)S(1)} %bitcast.12, bf16[4,512,512]{2,1,0:T(8,128)(2,1)} %bitcast.20), custom_call_target="tpu_custom_call" | custom-call | flops 1610612736 | bytes 2097152 | tf_op jit(solution)/shard_map/pallas_call | solution.py:152
  40.3 0.0 copy-start
  40.3 0.0 collective-permute-done.1.far_ref
  40.3 0.0 collective-permute-done.2.next_ref
  40.3 0.2 shard_map.61.mine_ref
  40.5 2.1 %collective-permute-start.3 = (bf16[512,512]{1,0:T(8,128)(2,1)S(1)}, bf16[512,512]{1,0:T(8,128)(2,1)S(1)}, u32[]{:S(2)}, u32[]{:S(2)}) collective-permute-start(bf16[512,512]{1,0:T(8,128)(2,1)S(1)} %shard_map.61.mine_ref), channel_id=1, source_target_pairs={{0,64},{64,0},{128,192},{192,128},{256,320},{320,256},{384,448},{4... | collective-permute-start | bytes 1572872 | tf_op jit(solution)/shard_map/ppermute | solution.py:111
  42.6 0.0 copy-done
  42.6 1.0 %shard_map.62.base_ref = f32[512,512]{1,0:T(8,128)S(1)} custom-call(bf16[512,512]{1,0:T(8,128)(2,1)S(1)} %bitcast.13, f32[512,512]{1,0:T(8,128)S(1)} %bitcast.10, bf16[512,512]{1,0:T(8,128)(2,1)S(1)} %get-tuple-element.22.high_ref.fifth_ref, bf16[512,512]{1,0:T(8,128)(2,1)S(1)} %get-tuple-element.23.low_ref), custom_call_target="tpu_custom_call" | custom-call | flops 805306368 | bytes 3145728 | tf_op jit(solution)/shard_map/pallas_call | solution.py:164
  43.6 0.9 %collective-permute-done.3.other_ref = bf16[512,512]{1,0:T(8,128)(2,1)S(1)} collective-permute-done((bf16[512,512]{1,0:T(8,128)(2,1)S(1)}, bf16[512,512]{1,0:T(8,128)(2,1)S(1)}, u32[]{:S(2)}, u32[]{:S(2)}) %collective-permute-start.3) | collective-permute-done | bytes 524320 | tf_op jit(solution)/shard_map/ppermute | solution.py:111
  44.4 1.0 %shard_map.63 = (f32[512,512]{1,0:T(8,128)S(1)}, bf16[64,8,512]{2,1,0:T(8,128)(2,1)S(1)}) custom-call(s32[1]{0:T(128)} %bitcast.1.dp_ref, bf16[512,512]{1,0:T(8,128)(2,1)S(1)} %shard_map.61.mine_ref, bf16[512,512]{1,0:T(8,128)(2,1)S(1)} %collective-permute-done.3.other_ref, bf16[512,512]{1,0:T(8,128)(2,1)S(1)} %get-tuple-element.22.high_ref.fifth_ref, ...), custom_call_target="tpu_custom_call" | custom-call | flops 536870912 | bytes 4194304 | tf_op jit(solution)/shard_map/pallas_call | solution.py:174
  45.5 0.0 copy-start.2
  45.5 0.8 %copy-done.2 = bf16[64,8,512]{2,1,0:T(8,128)(2,1)} copy-done((bf16[64,8,512]{2,1,0:T(8,128)(2,1)}, bf16[64,8,512]{2,1,0:T(8,128)(2,1)S(1)}, u32[]{:S(2)}) %copy-start.2) | copy-done | bytes 524312
  46.3 13.2 %all-to-all-start.1 = ((bf16[64,8,512]{2,1,0:T(8,128)(2,1)}), bf16[64,8,512]{2,1,0:T(8,128)(2,1)S(1)}, u32[]{:S(2)}, u32[]{:S(2)}) async-start(bf16[64,8,512]{2,1,0:T(8,128)(2,1)} %copy-done.2), calls=%async_computation.1 | async-start | bytes 1048576 | tf_op jit(solution)/shard_map/all_to_all | solution.py:182
  59.5 1.1 %shard_map.64 = f32[512,512]{1,0:T(8,128)} custom-call(f32[512,512]{1,0:T(8,128)S(1)} %bitcast.11, f32[512,512]{1,0:T(8,128)S(1)} %get-tuple-element.24.gram_ref), custom_call_target="tpu_custom_call" | custom-call | bytes 3145728 | tf_op jit(solution)/shard_map/pallas_call | solution.py:185
  60.6 13.4 %all-to-all-done.1.fresh_ref = bf16[64,8,512]{2,1,0:T(8,128)(2,1)S(1)} async-done(((bf16[64,8,512]{2,1,0:T(8,128)(2,1)}), bf16[64,8,512]{2,1,0:T(8,128)(2,1)S(1)}, u32[]{:S(2)}, u32[]{:S(2)}) %all-to-all-start.1) | async-done | bytes 524320 | tf_op jit(solution)/shard_map/all_to_all | solution.py:182
  74.0 0.0 copy-done.3
  74.0 1.4 %shard_map.65 = bf16[64,8,512]{2,1,0:T(8,128)(2,1)} custom-call(s32[64]{0:T(128)S(1)} %bitcast.16, bf16[64,8,512]{2,1,0:T(8,128)(2,1)S(1)} %all-to-all-done.1.fresh_ref, bf16[64,8,512]{2,1,0:T(8,128)(2,1)S(1)} %bitcast.15), custom_call_target="tpu_custom_call" | custom-call | bytes 1572864 | tf_op jit(solution)/shard_map/pallas_call | solution.py:193
  (3 shorter events, 0.0 us)
Async XLA Ops:
  0.6 18.5 %collective-permute-start = (bf16[4,512,512]{2,1,0:T(8,128)(2,1)}, bf16[4,512,512]{2,1,0:T(8,128)(2,1)S(1)}, u32[]{:S(2)}, u32[]{:S(2)}) collective-permute-start(bf16[4,512,512]{2,1,0:T(8,128)(2,1)} %bitcast.17), channel_id=1, source_target_pairs={{0,64},{64,0},{128,192},{192,128},{256,320},{320,256},{384,448},{4... | collective-permute-start | bytes 6291464 | tf_op jit(solution)/shard_map/ppermute | solution.py:111
  2.6 35.8 %all-to-all-start = ((bf16[64,8,512]{2,1,0:T(8,128)(2,1)}), bf16[64,8,512]{2,1,0:T(8,128)(2,1)S(1)}, u32[]{:S(2)}, u32[]{:S(2)}) async-start(bf16[64,8,512]{2,1,0:T(8,128)(2,1)} %bitcast.14), calls=%async_computation | async-start | bytes 1048576 | tf_op jit(solution)/shard_map/all_to_all | solution.py:119
  20.5 19.8 %collective-permute-start.2 = (bf16[512,512]{1,0:T(8,128)(2,1)S(1)}, bf16[512,512]{1,0:T(8,128)(2,1)S(1)}, u32[]{:S(2)}, u32[]{:S(2)}) collective-permute-start(bf16[512,512]{1,0:T(8,128)(2,1)S(1)} %get-tuple-element.18), channel_id=1, source_target_pairs={{0,128},{64,448},{128,256},{192,64},{256,384},{320,192},{384,0},{4... | collective-permute-start | bytes 1572872 | tf_op jit(solution)/shard_map/ppermute | solution.py:115
  23.6 16.7 %collective-permute-start.1 = (bf16[256,512]{1,0:T(8,128)(2,1)S(1)}, bf16[256,512]{1,0:T(8,128)(2,1)S(1)}, u32[]{:S(2)}, u32[]{:S(2)}) collective-permute-start(bf16[256,512]{1,0:T(8,128)(2,1)S(1)} %get-tuple-element.17), channel_id=1, source_target_pairs={{0,256},{64,320},{128,384},{192,448},{256,0},{320,64},{384,128},{4... | collective-permute-start | bytes 786440 | tf_op jit(solution)/shard_map/ppermute | solution.py:115
  40.3 2.3 %copy-start = (f32[1,1,512,512]{3,2,1,0:T(8,128)S(1)}, f32[1,1,512,512]{3,2,1,0:T(8,128)}, u32[]{:S(2)}) copy-start(f32[1,1,512,512]{3,2,1,0:T(8,128)} %param.5) | copy-start | bytes 3145732
  40.5 3.9 %collective-permute-start.3 = (bf16[512,512]{1,0:T(8,128)(2,1)S(1)}, bf16[512,512]{1,0:T(8,128)(2,1)S(1)}, u32[]{:S(2)}, u32[]{:S(2)}) collective-permute-start(bf16[512,512]{1,0:T(8,128)(2,1)S(1)} %shard_map.61.mine_ref), channel_id=1, source_target_pairs={{0,64},{64,0},{128,192},{192,128},{256,320},{320,256},{384,448},{4... | collective-permute-start | bytes 1572872 | tf_op jit(solution)/shard_map/ppermute | solution.py:111
  45.5 0.8 %copy-start.2 = (bf16[64,8,512]{2,1,0:T(8,128)(2,1)}, bf16[64,8,512]{2,1,0:T(8,128)(2,1)S(1)}, u32[]{:S(2)}) copy-start(bf16[64,8,512]{2,1,0:T(8,128)(2,1)S(1)} %get-tuple-element.25) | copy-start | bytes 1572868
  46.3 27.7 %copy-start.1 = (bf16[64,1,8,512]{3,2,1,0:T(8,128)(2,1)S(1)}, bf16[64,1,8,512]{3,2,1,0:T(8,128)(2,1)}, u32[]{:S(2)}) copy-start(bf16[64,1,8,512]{3,2,1,0:T(8,128)(2,1)} %param.6) | copy-start | bytes 1572868
  46.3 27.7 %copy-start.3 = (s32[1,64]{1,0:T(1,128)S(1)}, s32[1,64]{1,0:T(1,128)}, u32[]{:S(2)}) copy-start(s32[1,64]{1,0:T(1,128)} %param.7) | copy-start | bytes 772
  46.3 27.7 %all-to-all-start.1 = ((bf16[64,8,512]{2,1,0:T(8,128)(2,1)}), bf16[64,8,512]{2,1,0:T(8,128)(2,1)S(1)}, u32[]{:S(2)}, u32[]{:S(2)}) async-start(bf16[64,8,512]{2,1,0:T(8,128)(2,1)} %copy-done.2), calls=%async_computation.1 | async-start | bytes 1048576 | tf_op jit(solution)/shard_map/all_to_all | solution.py:182

commit v12 on v11

--- a/solution.py
+++ b/solution.py
@@ -63,7 +63,7 @@
         mine_ref[rows] = add(own_ref[rows], next_ref[rows], *extra)
 
 
-def refine_kernel(order, dp_ref, mine_ref, other_ref, fifth_ref, base_ref, gram_ref, refined_ref):
+def refine_kernel(order, dp_ref, mine_ref, other_ref, fifth_ref, base_ref, gram_ref, out_ref, refined_ref, sem):
     summed = add(mine_ref[...], other_ref[...])
 
     def update(contract):
@@ -74,6 +74,9 @@
         rows = refined_ref.shape[1]
         for at, worker in enumerate(order):
             refined_ref[at] = refined[worker * rows : (worker + 1) * rows].astype(jnp.bfloat16)
+        copy = pltpu.make_async_copy(refined_ref, out_ref, sem)
+        copy.start()
+        copy.wait()
 
     @pl.when(lax.rem(dp_ref[0], 2) == 0)
     def _():
@@ -175,7 +178,8 @@
         functools.partial(refine_kernel, order),
         out_shape=(whole, jax.ShapeDtypeStruct(old_pieces.shape, jnp.bfloat16)),
         in_specs=[SMEM] + [VMEM] * 4,
-        out_specs=(VMEM, VMEM),
+        out_specs=(VMEM, HBM),
+        scratch_shapes=[pltpu.VMEM(old_pieces.shape, jnp.bfloat16), pltpu.SemaphoreType.DMA],
         compiler_params=PARAMS,
         cost_estimate=cost(2 * flops, 16 * size**2),
     )(place, mine, other, fifth, base)

time: 75.8 us -> 75.9 us (level)
  no operation moved by 1% of the time
where the time goes in v12:
time: 75.9 us; the launch traced here: 75.4 us
  starting transfers between devices  39.5 us (52%)
  waiting for transfers between devices  26.3 us (35%)
  Pallas kernels  8.03 us (11%)
  local copies, waits for them, and re-layouts  0.8 us (1%)
  between operations  0.77 us (1%)
    all_to_all x1, starting transfers between devices, local(): lax.all_to_all(old_pieces, 'mp', split_axis=0, concat_axis=0, tiled=True)  16.6 us
    all_to_all x1, waiting for transfers between devices, local(): lax.all_to_all(refined, 'mp', split_axis=0, concat_axis=0, tiled=True, ax...  13.4 us
    all_to_all x1, starting transfers between devices, local(): lax.all_to_all(refined, 'mp', split_axis=0, concat_axis=0, tiled=True, ax...  13.2 us
    all_to_all x1, waiting for transfers between devices, local(): lax.all_to_all(old_pieces, 'mp', split_axis=0, concat_axis=0, tiled=True)  12 us
    ppermute x2, starting transfers between devices, around(): return lax.ppermute(value, 'dp', pairs)  5.81 us
    ppermute x2, starting transfers between devices, swapped(): return lax.ppermute(value, 'dp', [(i, i ^ 1) for i in range(replicas)])  3.97 us
    pallas_call x1, Pallas kernels, local(): pl.pallas_call(fifth_kernel, out_shape=(matrix, matrix, matrix), in_specs...  1.96 us
  transfers between devices with their start and end apart: 6, of which 3 were waited for; matrix products, arithmetic and copies ran while one was open for 0% of the time, Pallas kernels for 7%

profile of v12, /device:TPU:4, one launch (start us, length us, event | category | flops | bytes accessed | tf_op | source)
XLA Modules:
  0.0 75.4 jit_solution(16502497339549718036)
XLA Ops:
  0.6 1.9 %collective-permute-start = (bf16[4,512,512]{2,1,0:T(8,128)(2,1)}, bf16[4,512,512]{2,1,0:T(8,128)(2,1)S(1)}, u32[]{:S(2)}, u32[]{:S(2)}) collective-permute-start(bf16[4,512,512]{2,1,0:T(8,128)(2,1)} %bitcast.17), channel_id=1, source_target_pairs={{0,64},{64,0},{128,192},{192,128},{256,320},{320,256},{384,448},{4... | collective-permute-start | bytes 6291464 | tf_op jit(solution)/shard_map/ppermute | solution.py:114
  2.6 16.6 %all-to-all-start = ((bf16[64,8,512]{2,1,0:T(8,128)(2,1)}), bf16[64,8,512]{2,1,0:T(8,128)(2,1)S(1)}, u32[]{:S(2)}, u32[]{:S(2)}) async-start(bf16[64,8,512]{2,1,0:T(8,128)(2,1)} %bitcast.14), calls=%async_computation | async-start | bytes 1048576 | tf_op jit(solution)/shard_map/all_to_all | solution.py:122
  19.2 0.0 collective-permute-done.next_other_ref.far_other_ref
  19.2 1.3 %shard_map.60 = (bf16[512,512]{1,0:T(8,128)(2,1)S(1)}, bf16[256,512]{1,0:T(8,128)(2,1)S(1)}) custom-call(s32[1]{0:T(128)} %bitcast.1.dp_ref, bf16[4,512,512]{2,1,0:T(8,128)(2,1)} %bitcast.18, bf16[4,512,512]{2,1,0:T(8,128)(2,1)S(1)} %collective-permute-done.next_other_ref.far_other_ref, bf16[4,512,512]{2,1,0:T(8,128)(2,1)} %bitcast.19, ...), custom_call_target="tpu_custom_call" | custom-call | bytes 1 | tf_op jit(solution)/shard_map/pallas_call | solution.py:140
  20.5 3.1 %collective-permute-start.2 = (bf16[512,512]{1,0:T(8,128)(2,1)S(1)}, bf16[512,512]{1,0:T(8,128)(2,1)S(1)}, u32[]{:S(2)}, u32[]{:S(2)}) collective-permute-start(bf16[512,512]{1,0:T(8,128)(2,1)S(1)} %get-tuple-element.18), channel_id=1, source_target_pairs={{0,128},{64,448},{128,256},{192,64},{256,384},{320,192},{384,0},{4... | collective-permute-start | bytes 1572872 | tf_op jit(solution)/shard_map/ppermute | solution.py:118
  23.6 2.7 %collective-permute-start.1 = (bf16[256,512]{1,0:T(8,128)(2,1)S(1)}, bf16[256,512]{1,0:T(8,128)(2,1)S(1)}, u32[]{:S(2)}, u32[]{:S(2)}) collective-permute-start(bf16[256,512]{1,0:T(8,128)(2,1)S(1)} %get-tuple-element.17), channel_id=1, source_target_pairs={{0,256},{64,320},{128,384},{192,448},{256,0},{320,64},{384,128},{4... | collective-permute-start | bytes 786440 | tf_op jit(solution)/shard_map/ppermute | solution.py:118
  26.3 12.0 %all-to-all-done = bf16[64,8,512]{2,1,0:T(8,128)(2,1)S(1)} async-done(((bf16[64,8,512]{2,1,0:T(8,128)(2,1)}), bf16[64,8,512]{2,1,0:T(8,128)(2,1)S(1)}, u32[]{:S(2)}, u32[]{:S(2)}) %all-to-all-start) | async-done | bytes 524320 | tf_op jit(solution)/shard_map/all_to_all | solution.py:122
  38.3 2.0 %shard_map.59 = (bf16[512,512]{1,0:T(8,128)(2,1)S(1)}, bf16[512,512]{1,0:T(8,128)(2,1)S(1)}, bf16[512,512]{1,0:T(8,128)(2,1)S(1)}) custom-call(s32[1]{0:T(128)} %bitcast.1.dp_ref, bf16[512,512]{1,0:T(8,128)(2,1)S(1)} %bitcast.12, bf16[4,512,512]{2,1,0:T(8,128)(2,1)} %bitcast.20), custom_call_target="tpu_custom_call" | custom-call | flops 1610612736 | bytes 2097152 | tf_op jit(solution)/shard_map/pallas_call | solution.py:155
  40.3 0.0 copy-start
  40.3 0.0 collective-permute-done.1.far_ref
  40.3 0.0 collective-permute-done.2.next_ref
  40.3 0.2 shard_map.61.mine_ref
  40.5 2.1 %collective-permute-start.3 = (bf16[512,512]{1,0:T(8,128)(2,1)S(1)}, bf16[512,512]{1,0:T(8,128)(2,1)S(1)}, u32[]{:S(2)}, u32[]{:S(2)}) collective-permute-start(bf16[512,512]{1,0:T(8,128)(2,1)S(1)} %shard_map.61.mine_ref), channel_id=1, source_target_pairs={{0,64},{64,0},{128,192},{192,128},{256,320},{320,256},{384,448},{4... | collective-permute-start | bytes 1572872 | tf_op jit(solution)/shard_map/ppermute | solution.py:114
  42.6 0.0 copy-done
  42.6 1.0 %shard_map.62.base_ref = f32[512,512]{1,0:T(8,128)S(1)} custom-call(bf16[512,512]{1,0:T(8,128)(2,1)S(1)} %bitcast.13, f32[512,512]{1,0:T(8,128)S(1)} %bitcast.10, bf16[512,512]{1,0:T(8,128)(2,1)S(1)} %get-tuple-element.22.high_ref.fifth_ref, bf16[512,512]{1,0:T(8,128)(2,1)S(1)} %get-tuple-element.23.low_ref), custom_call_target="tpu_custom_call" | custom-call | flops 805306368 | bytes 3145728 | tf_op jit(solution)/shard_map/pallas_call | solution.py:167
  43.6 0.9 %collective-permute-done.3.other_ref = bf16[512,512]{1,0:T(8,128)(2,1)S(1)} collective-permute-done((bf16[512,512]{1,0:T(8,128)(2,1)S(1)}, bf16[512,512]{1,0:T(8,128)(2,1)S(1)}, u32[]{:S(2)}, u32[]{:S(2)}) %collective-permute-start.3) | collective-permute-done | bytes 524320 | tf_op jit(solution)/shard_map/ppermute | solution.py:114
  44.4 1.1 %shard_map.63 = (f32[512,512]{1,0:T(8,128)S(1)}, bf16[64,8,512]{2,1,0:T(8,128)(2,1)S(1)}) custom-call(s32[1]{0:T(128)} %bitcast.1.dp_ref, bf16[512,512]{1,0:T(8,128)(2,1)S(1)} %shard_map.61.mine_ref, bf16[512,512]{1,0:T(8,128)(2,1)S(1)} %collective-permute-done.3.other_ref, bf16[512,512]{1,0:T(8,128)(2,1)S(1)} %get-tuple-element.22.high_ref.fifth_ref, ...), custom_call_target="tpu_custom_call" | custom-call | flops 536870912 | bytes 4194304 | tf_op jit(solution)/shard_map/pallas_call | solution.py:177
  45.5 0.0 copy-start.2
  45.6 0.8 %copy-done.2 = bf16[64,8,512]{2,1,0:T(8,128)(2,1)} copy-done((bf16[64,8,512]{2,1,0:T(8,128)(2,1)}, bf16[64,8,512]{2,1,0:T(8,128)(2,1)S(1)}, u32[]{:S(2)}) %copy-start.2) | copy-done | bytes 524312
  46.3 13.2 %all-to-all-start.1 = ((bf16[64,8,512]{2,1,0:T(8,128)(2,1)}), bf16[64,8,512]{2,1,0:T(8,128)(2,1)S(1)}, u32[]{:S(2)}, u32[]{:S(2)}) async-start(bf16[64,8,512]{2,1,0:T(8,128)(2,1)} %copy-done.2), calls=%async_computation.1 | async-start | bytes 1048576 | tf_op jit(solution)/shard_map/all_to_all | solution.py:186
  59.5 1.1 %shard_map.64 = f32[512,512]{1,0:T(8,128)} custom-call(f32[512,512]{1,0:T(8,128)S(1)} %bitcast.11, f32[512,512]{1,0:T(8,128)S(1)} %get-tuple-element.24.gram_ref), custom_call_target="tpu_custom_call" | custom-call | bytes 3145728 | tf_op jit(solution)/shard_map/pallas_call | solution.py:189
  60.6 13.4 %all-to-all-done.1.fresh_ref = bf16[64,8,512]{2,1,0:T(8,128)(2,1)S(1)} async-done(((bf16[64,8,512]{2,1,0:T(8,128)(2,1)}), bf16[64,8,512]{2,1,0:T(8,128)(2,1)S(1)}, u32[]{:S(2)}, u32[]{:S(2)}) %all-to-all-start.1) | async-done | bytes 524320 | tf_op jit(solution)/shard_map/all_to_all | solution.py:186
  74.0 0.0 copy-done.1
  74.0 1.4 %shard_map.65 = bf16[64,8,512]{2,1,0:T(8,128)(2,1)} custom-call(s32[64]{0:T(128)S(1)} %bitcast.16, bf16[64,8,512]{2,1,0:T(8,128)(2,1)S(1)} %all-to-all-done.1.fresh_ref, bf16[64,8,512]{2,1,0:T(8,128)(2,1)S(1)} %bitcast.15), custom_call_target="tpu_custom_call" | custom-call | bytes 1572864 | tf_op jit(solution)/shard_map/pallas_call | solution.py:197
  (3 shorter events, 0.0 us)
Async XLA Ops:
  0.6 18.5 %collective-permute-start = (bf16[4,512,512]{2,1,0:T(8,128)(2,1)}, bf16[4,512,512]{2,1,0:T(8,128)(2,1)S(1)}, u32[]{:S(2)}, u32[]{:S(2)}) collective-permute-start(bf16[4,512,512]{2,1,0:T(8,128)(2,1)} %bitcast.17), channel_id=1, source_target_pairs={{0,64},{64,0},{128,192},{192,128},{256,320},{320,256},{384,448},{4... | collective-permute-start | bytes 6291464 | tf_op jit(solution)/shard_map/ppermute | solution.py:114
  2.6 35.8 %all-to-all-start = ((bf16[64,8,512]{2,1,0:T(8,128)(2,1)}), bf16[64,8,512]{2,1,0:T(8,128)(2,1)S(1)}, u32[]{:S(2)}, u32[]{:S(2)}) async-start(bf16[64,8,512]{2,1,0:T(8,128)(2,1)} %bitcast.14), calls=%async_computation | async-start | bytes 1048576 | tf_op jit(solution)/shard_map/all_to_all | solution.py:122
  20.5 19.8 %collective-permute-start.2 = (bf16[512,512]{1,0:T(8,128)(2,1)S(1)}, bf16[512,512]{1,0:T(8,128)(2,1)S(1)}, u32[]{:S(2)}, u32[]{:S(2)}) collective-permute-start(bf16[512,512]{1,0:T(8,128)(2,1)S(1)} %get-tuple-element.18), channel_id=1, source_target_pairs={{0,128},{64,448},{128,256},{192,64},{256,384},{320,192},{384,0},{4... | collective-permute-start | bytes 1572872 | tf_op jit(solution)/shard_map/ppermute | solution.py:118
  23.6 16.7 %collective-permute-start.1 = (bf16[256,512]{1,0:T(8,128)(2,1)S(1)}, bf16[256,512]{1,0:T(8,128)(2,1)S(1)}, u32[]{:S(2)}, u32[]{:S(2)}) collective-permute-start(bf16[256,512]{1,0:T(8,128)(2,1)S(1)} %get-tuple-element.17), channel_id=1, source_target_pairs={{0,256},{64,320},{128,384},{192,448},{256,0},{320,64},{384,128},{4... | collective-permute-start | bytes 786440 | tf_op jit(solution)/shard_map/ppermute | solution.py:118
  40.3 2.3 %copy-start = (f32[1,1,512,512]{3,2,1,0:T(8,128)S(1)}, f32[1,1,512,512]{3,2,1,0:T(8,128)}, u32[]{:S(2)}) copy-start(f32[1,1,512,512]{3,2,1,0:T(8,128)} %param.5) | copy-start | bytes 3145732
  40.5 3.9 %collective-permute-start.3 = (bf16[512,512]{1,0:T(8,128)(2,1)S(1)}, bf16[512,512]{1,0:T(8,128)(2,1)S(1)}, u32[]{:S(2)}, u32[]{:S(2)}) collective-permute-start(bf16[512,512]{1,0:T(8,128)(2,1)S(1)} %shard_map.61.mine_ref), channel_id=1, source_target_pairs={{0,64},{64,0},{128,192},{192,128},{256,320},{320,256},{384,448},{4... | collective-permute-start | bytes 1572872 | tf_op jit(solution)/shard_map/ppermute | solution.py:114
  45.5 0.8 %copy-start.2 = (bf16[64,8,512]{2,1,0:T(8,128)(2,1)}, bf16[64,8,512]{2,1,0:T(8,128)(2,1)S(1)}, u32[]{:S(2)}) copy-start(bf16[64,8,512]{2,1,0:T(8,128)(2,1)S(1)} %get-tuple-element.25) | copy-start | bytes 1572868
  46.3 27.7 %copy-start.1 = (bf16[64,1,8,512]{3,2,1,0:T(8,128)(2,1)S(1)}, bf16[64,1,8,512]{3,2,1,0:T(8,128)(2,1)}, u32[]{:S(2)}) copy-start(bf16[64,1,8,512]{3,2,1,0:T(8,128)(2,1)} %param.6) | copy-start | bytes 1572868
  46.3 27.7 %copy-start.3 = (s32[1,64]{1,0:T(1,128)S(1)}, s32[1,64]{1,0:T(1,128)}, u32[]{:S(2)}) copy-start(s32[1,64]{1,0:T(1,128)} %param.7) | copy-start | bytes 772
  46.3 27.7 %all-to-all-start.1 = ((bf16[64,8,512]{2,1,0:T(8,128)(2,1)}), bf16[64,8,512]{2,1,0:T(8,128)(2,1)S(1)}, u32[]{:S(2)}, u32[]{:S(2)}) async-start(bf16[64,8,512]{2,1,0:T(8,128)(2,1)} %copy-done.2), calls=%async_computation.1 | async-start | bytes 1048576 | tf_op jit(solution)/shard_map/all_to_all | solution.py:186
